TPU v7x, 32 devices: a whole 2x2x4 slice. The times are simulated.
32 devices in a mesh: seq: 8 (over z, y), batch: 4 (over x, core).
Axes of the slice: x: 2, y: 2, z: 4, core: 2. Of those that a mesh axis runs over, the one named last changes fastest.
Arguments:
- tokens: bfloat16 [4, 3072, 1152], P('batch', 'seq'), may hold values from -6 to 6
- skip_tokens: bfloat16 [4, 3072, 1152], P('batch', 'seq'), may hold values from -6 to 6
- segment_ids: int32 [4, 3072], P('batch'), may hold values from 0 to 11, as said below
- upstream: bfloat16 [4, 3072, 1152], P('batch', 'seq'), may hold values from -6 to 6
- skip_weight: bfloat16 [2304, 1152], replicated, may hold values from -0.125 to 0.125
- skip_bias: bfloat16 [1152], replicated, may hold values from -1.5 to 1.5
- first_gain: bfloat16 [1152], replicated, may hold values from 0.25 to 1.75
- first_shift: bfloat16 [1152], replicated, may hold values from -1.5 to 1.5
- attn_weight: bfloat16 [1152, 3456], replicated, may hold values from -0.1875 to 0.1875
- attn_bias: bfloat16 [2304], replicated, may hold values from -1.5 to 1.5
- proj_weight: bfloat16 [1152, 1152], replicated, may hold values from -1.5 to 1.5
- proj_bias: bfloat16 [1152], replicated, may hold values from -1.5 to 1.5
- second_gain: bfloat16 [1152], replicated, may hold values from 0.25 to 1.75
- second_shift: bfloat16 [1152], replicated, may hold values from -1.5 to 1.5
- expand_weight: bfloat16 [1152, 4608], replicated, may hold values from -0.1875 to 0.1875
- expand_bias: bfloat16 [4608], replicated, may hold values from -1.5 to 1.5
- shrink_weight: bfloat16 [4608, 1152], replicated, may hold values from -0.09375 to 0.09375
- shrink_bias: bfloat16 [1152], replicated, may hold values from -1.5 to 1.5
Outputs:
- result: bfloat16 [4, 3072, 1152], P('batch', 'seq')
- tokens_grad: bfloat16 [4, 3072, 1152], P('batch', 'seq')
- skip_grad: bfloat16 [4, 3072, 1152], P('batch', 'seq')
- skip_weight_grad: float32 [2304, 1152], P('seq', 'batch')
- skip_bias_grad: float32 [1152], P(('seq', 'batch'))
- first_gain_grad: float32 [1152], P(('seq', 'batch'))
- first_shift_grad: float32 [1152], P(('seq', 'batch'))
- attn_weight_grad: float32 [1152, 3456], P('seq', 'batch')
- attn_bias_grad: float32 [2304], P(('seq', 'batch'))
- proj_weight_grad: float32 [1152, 1152], P('seq', 'batch')
- proj_bias_grad: float32 [1152], P(('seq', 'batch'))
- second_gain_grad: float32 [1152], P(('seq', 'batch'))
- second_shift_grad: float32 [1152], P(('seq', 'batch'))
- expand_weight_grad: float32 [1152, 4608], P('seq', 'batch')
- expand_bias_grad: float32 [4608], P(('seq', 'batch'))
- shrink_weight_grad: float32 [4608, 1152], P('seq', 'batch')
- shrink_bias_grad: float32 [1152], P(('seq', 'batch'))
Inputs may be any that keep to these rules, and one draw needn't show every extreme that they name: `segment_ids`: along each group the ids start at 0 and rise by one from item to item, and every group holds the same number of items. Every item holds 194 to 322 rows, except a group's last, which may hold fewer; each group's first item holds exactly 322.
All inputs are finite; a program needn't handle non-finite values.
Results may differ from a plain program's by a relative error of at most 0.017.
Values may be sent and summed in bfloat16 or wider, within the bound.
A program may use at most 256 MiB of HBM per device.

v0:
```python
from functools import partial

import jax
import jax.numpy as jnp
from jax import lax
from jax.experimental import pallas as pl
from jax.experimental.pallas import tpu as pltpu
from jax.sharding import PartitionSpec as P

HEADS = 16
ITEM_MOST = 322
LANES = 128
MESH = pl.DeviceIdType.MESH


def padded(value, sides, width):
    for axis, dim in sides:
        size, length = (lax.axis_size(axis), value.shape[dim])
        up = [(i, (i + 1) % size) for i in range(size - 1)]
        down = [(j, i) for i, j in up]
        last = lax.slice_in_dim(value, length - width, length, axis=dim)
        first = lax.slice_in_dim(value, 0, width, axis=dim)
        before = lax.ppermute(last, axis, up)
        after = lax.ppermute(first, axis, down)
        value = jnp.concatenate([before, value, after], axis=dim)
    return value


def shortened(value):
    return jax.tree.map(lambda a: a.astype(jnp.bfloat16) if a.dtype == jnp.float32 else a, value)


def normalize(inputs, gain_vec, shift_vec):
    centred = inputs - jnp.mean(inputs, axis=-1, keepdims=True)
    variance = jnp.mean(centred * centred, axis=-1, keepdims=True)
    return centred * lax.rsqrt(variance + 1e-05) * gain_vec + shift_vec


def matmul(operand, other_op):
    return jnp.dot(operand, other_op, preferred_element_type=jnp.float32)


def outer_sum(left, right):
    return lax.dot_general(
        left, right, (((0,), (0,)), ((), ())), preferred_element_type=jnp.float32
    )


def to_items(tensor, blocks):
    group_count, length, features = tensor.shape
    reshaped = tensor.reshape(group_count, length, blocks, features // blocks)
    return jnp.transpose(reshaped, (0, 2, 1, 3)).reshape(
        group_count * blocks, length, features // blocks
    )


def from_items(tensor, blocks):
    item_count, length, features = tensor.shape
    reshaped = tensor.reshape(item_count // blocks, blocks, length, features)
    return jnp.transpose(reshaped, (0, 2, 1, 3)).reshape(
        item_count // blocks, length, blocks * features
    )


def masked_scores(query_part, key_part, query_ids, key_ids, head_dim):
    query_heads = query_part.reshape(query_part.shape[0], -1, head_dim)
    key_heads = key_part.reshape(key_part.shape[0], -1, head_dim)
    products = jnp.einsum(
        "qhd,khd->hqk", query_heads, key_heads, preferred_element_type=jnp.float32
    )
    matching = query_ids[:, None] == key_ids[None, :]
    return jnp.where(matching[None], products * head_dim ** (-0.5), -1e30)


def forward_block(pieces, head_dim):
    query_part, key_part, value_part, query_ids, key_ids = pieces
    scores = masked_scores(query_part, key_part, query_ids, key_ids, head_dim)
    highest = jnp.max(scores, axis=-1, keepdims=True)
    raised = jnp.exp(scores - highest)
    denominator = jnp.sum(raised, axis=-1, keepdims=True)
    attention = raised / denominator
    value_heads = value_part.reshape(value_part.shape[0], -1, head_dim)
    mixed_heads = jnp.einsum(
        "hqk,khd->qhd",
        attention.astype(jnp.bfloat16),
        value_heads,
        preferred_element_type=jnp.float32,
    )
    return (mixed_heads.reshape(query_part.shape[0], -1), (highest + jnp.log(denominator))[..., 0])


def backward_block(pieces, head_dim):
    query_part, key_part, value_part, query_ids, key_ids, grad_part, lse_part = pieces
    length = query_part.shape[0]
    key_span = key_part.shape[0]
    scores = masked_scores(query_part, key_part, query_ids, key_ids, head_dim)
    attention = jnp.exp(scores - lse_part[..., None])
    query_heads = query_part.reshape(length, -1, head_dim)
    key_heads = key_part.reshape(key_span, -1, head_dim)
    value_heads = value_part.reshape(key_span, -1, head_dim)
    grad_heads = grad_part.reshape(length, -1, head_dim)
    prob_grad = jnp.einsum(
        "qhd,khd->hqk", grad_heads, value_heads, preferred_element_type=jnp.float32
    )
    row_dot = jnp.sum(attention * prob_grad, axis=-1, keepdims=True)
    score_grad = (head_dim ** (-0.5) * attention * (prob_grad - row_dot)).astype(jnp.bfloat16)
    query_grad = jnp.einsum(
        "hqk,khd->qhd", score_grad, key_heads, preferred_element_type=jnp.float32
    )
    key_grad = jnp.einsum(
        "hqk,qhd->khd", score_grad, query_heads, preferred_element_type=jnp.float32
    )
    value_grad = jnp.einsum(
        "hqk,qhd->khd",
        attention.astype(jnp.bfloat16),
        grad_heads,
        preferred_element_type=jnp.float32,
    )
    return (
        query_grad.reshape(length, -1),
        key_grad.reshape(key_span, -1),
        value_grad.reshape(key_span, -1),
    )


class Unit:
    def __init__(self, left, left_at, right, right_at, tiles, rows, blocks, out, out_at):
        self.left, self.left_at = left, left_at
        self.right, self.right_at = right, right_at
        self.tiles = tiles
        self.rows = rows
        self.blocks = blocks
        self.places = 1 + max(block[3] for block in blocks)
        self.out, self.out_at = out, out_at

    def shape(self, *lead):
        if self.tiles:
            return (*lead, self.rows, LANES)
        return (*lead, self.rows * 7 // 3, LANES)

    @property
    def x_size(self):
        return 2 * (self.tiles or 1)

    @property
    def part_shape(self):
        return self.shape(2, self.x_size, 2, self.places)

    @property
    def first_shapes(self):
        half = self.x_size // 2
        if self.tiles:
            return (self.shape(half, 2, self.places), self.shape(2 * half, self.places))
        return (self.shape(2, self.places), self.shape(2, self.places))

    @property
    def second_shape(self):
        if self.tiles:
            return self.shape(self.tiles, self.places)
        return self.shape(self.places)

    @property
    def chain_shape(self):
        return self.shape(self.tiles) if self.tiles else self.shape()

    def view(self, ref, order, x, y, place=None):
        if x is None:
            x_at = slice(None)
        elif self.tiles:
            x_at = pl.ds(x * self.tiles, self.tiles)
        else:
            x_at = x
        y_at = slice(None) if y is None else y
        if place is None:
            return ref.at[order, x_at, y_at]
        return ref.at[order, x_at, y_at, place]

    def chains(self):
        return sorted({(order, place, z) for _, order, _, place, z in self.blocks})


def make_units():
    order_of = (0, 1, 1, 0)
    place_of = (0, 0, 1, 1)
    quarter = [
        ((2 * z + y) * 144, order_of[z], y, place_of[z], z) for z in range(4) for y in range(2)
    ]
    units = []
    for z in (0, 3, 1, 2):
        blocks = [(y * 576 + h * 288, h, y, 0, z) for y in range(2) for h in range(2)]
        units.append(Unit("active", z * 1152, "upstream", 0, 0, 288, blocks, "shrink", z))
    for j in range(3):
        units.append(Unit("second", 0, "hidden", j, 3, 144, quarter, "expand", j * 3))
    units.append(Unit("mixed", 0, "branch", 0, 0, 144, quarter, "proj", 0))
    units.append(Unit("normed", 0, "triple_a", 0, 4, 144, quarter, "attn", 0))
    units.append(Unit("normed", 0, "triple_b", 0, 3, 144, quarter, "attn", 4))
    for k in range(2):
        blocks = [(h * 576 + y * 288, h, y, 0, 2 * k + h) for h in range(2) for y in range(2)]
        units.append(Unit("joined", k * 1152, "stream", 0, 0, 288, blocks, "skip", k))
    return units


LEFTS = ("active", "second", "mixed", "normed", "joined")
RIGHTS = ("upstream", "hidden", "branch", "triple_a", "triple_b", "stream")
GRADS = ("shrink", "expand", "proj", "attn", "skip")
GRAD_SHAPES = ((576, 288), (144, 1152), (144, 288), (144, 896), (288, 288))


def add_into(target, other):
    target[...] = (target[...].astype(jnp.float32) + other[...].astype(jnp.float32)).astype(
        target.dtype
    )


class Links:
    def __init__(self):
        self.ids = {}

    def id(self, key):
        return self.ids.setdefault(key, len(self.ids))


def sum_kernel(units, names, *refs):
    r = dict(zip(names, refs))
    seq, batch = lax.axis_index("seq"), lax.axis_index("batch")
    z, y = seq // 2, seq % 2
    x, c = batch // 2, batch % 2
    partner = (seq, 2 * x + (1 - c))
    x_side = (seq, 2 * (1 - x) + c)
    y_side = (2 * z + (1 - y), batch)
    above = (2 * jnp.minimum(z + 1, 3) + y, batch)
    below = (2 * jnp.maximum(z - 1, 0) + y, batch)
    links = Links()

    barrier = pltpu.get_barrier_semaphore()
    for device in (partner, x_side, y_side):
        pl.semaphore_signal(barrier, 1, device_id=device, device_id_type=MESH)

    @pl.when(z < 3)
    def _():
        pl.semaphore_signal(barrier, 1, device_id=above, device_id_type=MESH)

    @pl.when(z > 0)
    def _():
        pl.semaphore_signal(barrier, 1, device_id=below, device_id_type=MESH)

    pl.semaphore_wait(barrier, 3 + (z < 3).astype(jnp.int32) + (z > 0).astype(jnp.int32))

    def remote(key, src, dst, device):
        i = links.id(key)
        return pltpu.make_async_remote_copy(
            src_ref=src,
            dst_ref=dst,
            send_sem=r["sent"].at[i],
            recv_sem=r["came"].at[i],
            device_id=device,
            device_id_type=MESH,
        )

    swaps = {}
    for unit in units:
        key = ("left", unit.left, unit.left_at)
        if key not in swaps:
            at = pl.ds(unit.left_at, 1152)
            swaps[key] = remote(
                key, r[unit.left].at[:, at], r["far_" + unit.left].at[:, at], partner
            )
        key = ("right", unit.right, unit.right_at)
        if key not in swaps:
            swaps[key] = remote(
                key,
                r[unit.right].at[1 - c, unit.right_at],
                r["far_" + unit.right].at[unit.right_at],
                partner,
            )
    for copy in swaps.values():
        copy.start()

    slots = {}
    turns = {"left": 0, "right": 0}

    def load(unit):
        started = []
        for side, name, at in (
            ("left", unit.left, unit.left_at),
            ("right", unit.right, unit.right_at),
        ):
            key = (side, name, at)
            if key in slots:
                continue
            slot = turns[side] % 2
            turns[side] += 1
            slots[key] = slot
            swaps[key].wait_recv()
            if side == "left":
                cols = pl.ds(at, 1152)
                near, far = r[name].at[:, cols], r["far_" + name].at[:, cols]
                hold = r["lefts"].at[slot]
            else:
                near, far = r[name].at[c, at], r["far_" + name].at[at]
                hold = r["rights"].at[slot, :, pl.ds(0, near.shape[-1])]
            for half, src in ((0, near), (1, far)):
                copy = pltpu.make_async_copy(
                    src, hold.at[pl.ds(384 * half, 384)], r[side + "_sem"].at[slot, half]
                )
                copy.start()
                started.append(copy)
        return started

    def compute(u):
        unit = units[u]
        part = r["part", u]
        left = r["lefts"].at[slots["left", unit.left, unit.left_at]]
        right = r["rights"].at[slots["right", unit.right, unit.right_at]]

        def product(n):
            cols = pl.ds(pl.multiple_of(n * 256, 256), 256)
            return lax.dot_general(
                left[...],
                right[:, cols],
                (((0,), (0,)), ((), ())),
                preferred_element_type=jnp.float32,
            )

        rows = unit.rows
        if unit.tiles:

            def body(n, carry):
                tile = product(n).astype(jnp.bfloat16)
                for first, order, y_at, place, _ in unit.blocks:
                    for i in range(2):
                        part[order, 2 * n + i, y_at, place] = tile[
                            first : first + rows, i * LANES : (i + 1) * LANES
                        ]
                return carry

            lax.fori_loop(0, unit.tiles, body, 0)
            return

        def body(n, carry):
            tile = product(n).astype(jnp.bfloat16)
            for first, order, y_at, place, _ in unit.blocks:
                for i in range(2):
                    part[order, n, y_at, place, pl.ds(i * rows, rows)] = tile[
                        first : first + rows, i * LANES : (i + 1) * LANES
                    ]
            return carry

        lax.fori_loop(0, 2, body, 0)
        tile = product(2)
        third = rows // 3
        for first, order, y_at, place, _ in unit.blocks:
            for x_at in range(2):
                pieces = [
                    tile[first + s * third : first + (s + 1) * third, x_at * LANES :][:, :32]
                    for s in range(3)
                ]
                packed = jnp.concatenate(pieces + [jnp.zeros_like(pieces[0])], axis=1)
                part[order, x_at, y_at, place, pl.ds(2 * rows, third)] = packed.astype(jnp.bfloat16)

    def first_copies(u):
        unit, part = units[u], r["part", u]
        return (
            remote(("first", u, 0), unit.view(part, 0, 1 - x, None), r["first", u, 0], x_side),
            remote(("first", u, 1), unit.view(part, 1, None, 1 - y), r["first", u, 1], y_side),
        )

    def second_copies(u):
        unit, part = units[u], r["part", u]
        return (
            remote(("second", u, 0), unit.view(part, 0, x, 1 - y), r["second", u].at[0], y_side),
            remote(("second", u, 1), unit.view(part, 1, 1 - x, y), r["second", u].at[1], x_side),
        )

    def first_stage(u):
        compute(u)
        for copy in first_copies(u):
            copy.start()

    def second_stage(u):
        unit, part = units[u], r["part", u]
        keeps = (unit.view(part, 0, x, None), unit.view(part, 1, None, y))
        for order, (copy, send) in enumerate(zip(first_copies(u), second_copies(u))):
            copy.wait_recv()
            add_into(keeps[order], r["first", u, order])
            send.start()

    def third_stage(u):
        unit, part = units[u], r["part", u]
        for order, copy in enumerate(second_copies(u)):
            copy.wait_recv()
            add_into(unit.view(part, order, x, y), r["second", u].at[order])

    def chain_copy(key, src, dsts, up):
        return remote((key, up), src, dsts[up], above if up else below)

    class Chain:
        def __init__(self, key, src, up_ref, down_ref, z_at):
            self.key, self.src, self.z_at = key, src, z_at
            self.refs = {True: up_ref, False: down_ref}

        def copy(self, up):
            return remote((self.key, up), self.src, self.refs[up], above if up else below)

        def hop(self, step):
            for up, me in ((True, step - 1), (False, 4 - step)):
                if (self.z_at > me) if up else (self.z_at < me):

                    @pl.when(z == me)
                    def _():
                        if step > 1:
                            self.copy(up).wait_recv()
                            add_into(self.src, self.refs[up])
                        self.copy(up).start()

        def total(self):
            value = self.src[...].astype(jnp.float32)
            for up, have in ((True, self.z_at > 0), (False, self.z_at < 3)):
                if have:
                    self.copy(up).wait_recv()
                    value = value + self.refs[up][...].astype(jnp.float32)
            return value

        def drain(self):
            for up, some in ((True, self.z_at > 0), (False, self.z_at < 3)):
                if some:

                    @pl.when((z < self.z_at) if up else (z > self.z_at))
                    def _():
                        self.copy(up).wait_send()

    def unit_chains(u):
        unit, part = units[u], r["part", u]
        found = []
        for order, place, z_at in unit.chains():
            src = unit.view(part, order, x, y, place)
            up = r["up", u, order, place] if z_at > 0 else None
            down = r["down", u, order, place] if z_at < 3 else None
            found.append((order, place, Chain(("chain", u, order, place), src, up, down, z_at)))
        return found

    def hop_stage(u, step):
        for _, _, chain in unit_chains(u):
            chain.hop(step)

    def last_stage(u):
        unit = units[u]
        out = r["out_" + unit.out]
        rows = unit.rows
        for order, place, chain in unit_chains(u):

            @pl.when(z == chain.z_at)
            def _():
                value = chain.total()
                if unit.tiles:
                    for t in range(unit.tiles):
                        at = (unit.out_at + t) * LANES
                        out[:, at : at + LANES] = value[t]
                    return
                base = order * rows if rows == 288 and unit.out == "shrink" else 0
                third = rows // 3
                for i in range(2):
                    out[base : base + rows, i * LANES : (i + 1) * LANES] = value[
                        i * rows : (i + 1) * rows
                    ]
                for s in range(3):
                    out[base + s * third : base + (s + 1) * third, 256:288] = value[
                        2 * rows : 2 * rows + third, s * 32 : (s + 1) * 32
                    ]

    vec = r["vec"]

    def vec_copies():
        return (
            remote("vec_core", vec.at[1 - c], r["vec_core"], partner),
            remote("vec_x", vec.at[c, 1 - x], r["vec_x"], x_side),
            remote("vec_y", vec.at[c, x, 1 - y], r["vec_y"], y_side),
        )

    vec_keeps = (vec.at[c], vec.at[c, x], vec.at[c, x, y])
    vec_lands = (r["vec_core"], r["vec_x"], r["vec_y"])
    vec_chains = [
        Chain(("vec", b), vec.at[c, x, y, b], r["vec_up"].at[b], r["vec_down"].at[b], b)
        for b in range(4)
    ]

    def vec_stage(step):
        if step < 3:
            if step > 0:
                vec_copies()[step - 1].wait_recv()
                add_into(vec_keeps[step - 1], vec_lands[step - 1])
            vec_copies()[step].start()
        elif step < 6:
            if step == 3:
                vec_copies()[2].wait_recv()
                add_into(vec_keeps[2], vec_lands[2])
            for chain in vec_chains:
                chain.hop(step - 2)
        elif step == 6:
            for chain in vec_chains:

                @pl.when(z == chain.z_at)
                def _():
                    r["out_vec"][...] = chain.total()

    count = len(units)
    started = load(units[0])
    for tick in range(count + 6):
        if tick < count:
            for copy in started:
                copy.wait()
            if tick + 1 < count:
                started = load(units[tick + 1])
            first_stage(tick)
        vec_stage(tick)
        if 0 <= tick - 1 < count:
            second_stage(tick - 1)
        if 0 <= tick - 2 < count:
            third_stage(tick - 2)
            hop_stage(tick - 2, 1)
        if 0 <= tick - 3 < count:
            hop_stage(tick - 3, 2)
        if 0 <= tick - 4 < count:
            hop_stage(tick - 4, 3)
        if 0 <= tick - 5 < count:
            last_stage(tick - 5)
    for copy in swaps.values():
        copy.wait_send()
    for u in range(count):
        for copy in first_copies(u) + second_copies(u):
            copy.wait_send()
        for _, _, chain in unit_chains(u):
            chain.drain()
    for copy in vec_copies():
        copy.wait_send()
    for chain in vec_chains:
        chain.drain()


def weight_sums(lefts, rights, vec):
    units = make_units()
    low = jnp.bfloat16
    names, in_specs, operands = [], [], []
    for name, value in [*lefts.items(), *rights.items()]:
        names.append(name)
        in_specs.append(pl.BlockSpec(memory_space=pl.ANY))
        operands.append(value)
    names.append("vec_in")
    in_specs.append(pl.BlockSpec(memory_space=pltpu.VMEM))
    operands.append(vec)
    out_shape, out_specs = [], []
    for name, shape in zip(GRADS, GRAD_SHAPES):
        names.append("out_" + name)
        out_shape.append(jax.ShapeDtypeStruct(shape, jnp.float32))
        out_specs.append(pl.BlockSpec(memory_space=pltpu.VMEM))
    names.append("out_vec")
    out_shape.append(jax.ShapeDtypeStruct((4, LANES), jnp.float32))
    out_specs.append(pl.BlockSpec(memory_space=pltpu.VMEM))
    for name in LEFTS:
        names.append("far_" + name)
        out_shape.append(jax.ShapeDtypeStruct(lefts[name].shape, low))
        out_specs.append(pl.BlockSpec(memory_space=pl.ANY))
    for name in RIGHTS:
        names.append("far_" + name)
        out_shape.append(jax.ShapeDtypeStruct(rights[name].shape[1:], low))
        out_specs.append(pl.BlockSpec(memory_space=pl.ANY))
    scratch = []

    def add(name, kind):
        names.append(name)
        scratch.append(kind)

    add("lefts", pltpu.VMEM((2, 768, 1152), low))
    add("rights", pltpu.VMEM((2, 768, 1024), low))
    add("left_sem", pltpu.SemaphoreType.DMA((2, 2)))
    add("right_sem", pltpu.SemaphoreType.DMA((2, 2)))
    for u, unit in enumerate(units):
        add(("part", u), pltpu.VMEM(unit.part_shape, low))
        for order in range(2):
            add(("first", u, order), pltpu.VMEM(unit.first_shapes[order], low))
        add(("second", u), pltpu.VMEM((2, *unit.second_shape), low))
        for order, place, z_at in unit.chains():
            if z_at > 0:
                add(("up", u, order, place), pltpu.VMEM(unit.chain_shape, low))
            if z_at < 3:
                add(("down", u, order, place), pltpu.VMEM(unit.chain_shape, low))
    add("vec", pltpu.VMEM(vec.shape, jnp.float32))
    add("vec_core", pltpu.VMEM(vec.shape[1:], jnp.float32))
    add("vec_x", pltpu.VMEM(vec.shape[2:], jnp.float32))
    add("vec_y", pltpu.VMEM(vec.shape[3:], jnp.float32))
    add("vec_up", pltpu.VMEM(vec.shape[3:], jnp.float32))
    add("vec_down", pltpu.VMEM(vec.shape[3:], jnp.float32))
    add("sent", pltpu.SemaphoreType.DMA((256,)))
    add("came", pltpu.SemaphoreType.DMA((256,)))

    def kernel(*refs):
        r = dict(zip(names, refs))
        r["vec"][...] = r["vec_in"][...]
        sum_kernel(units, names, *refs)

    found = pl.pallas_call(
        kernel,
        out_shape=out_shape,
        in_specs=in_specs,
        out_specs=out_specs,
        scratch_shapes=scratch,
        compiler_params=pltpu.CompilerParams(
            collective_id=0, has_side_effects=True, vmem_limit_bytes=60 * 2**20
        ),
        name="weight_sums",
    )(*operands)
    return dict(zip([*GRADS, "vec"], found[:6]))


def by_core(value):
    rows = value.shape[0]
    cut = value.reshape(rows, 2, 2, 288).transpose(2, 0, 1, 3)
    main = cut[..., :256].reshape(2, rows, 512)
    rest = jnp.pad(cut[..., 256:], ((0, 0), (0, 0), (0, 0), (0, 96))).reshape(2, rows, 256)
    return jnp.concatenate([main, rest], axis=-1)[:, None]


def by_core_wide(value, cuts):
    rows, total = value.shape
    cut = value.reshape(rows, 2, 2, total // 4).transpose(2, 0, 1, 3)
    found = []
    for first, width, pieces in cuts:
        part = cut[..., first : first + width * pieces]
        short = width * pieces - part.shape[-1]
        if short:
            part = jnp.pad(part, ((0, 0), (0, 0), (0, 0), (0, short)))
        part = part.reshape(2, rows, 2, pieces, width).transpose(0, 3, 1, 2, 4)
        found.append(part.reshape(2, pieces, rows, 2 * width))
    return found


PAIRS = (
    ("joined", "stream"),
    ("normed", "triple"),
    ("mixed", "branch"),
    ("second", "hidden"),
    ("active", "upstream"),
)


def summed(lefts, rights, vector_list):
    local_parts = []
    for left, right in PAIRS:
        rows = lax.all_gather(lefts[left], "batch", axis=0, tiled=True)
        columns = lax.all_to_all(rights[right], "batch", split_axis=1, concat_axis=0, tiled=True)
        local_parts.append(outer_sum(rows, columns))
    weight_parts = jax.tree.map(
        lambda part: part.astype(jnp.float32),
        lax.psum_scatter(shortened(tuple(local_parts)), "seq", scatter_dimension=0, tiled=True),
    )
    vectors = tuple(
        lax.psum_scatter(vector, ("seq", "batch"), scatter_dimension=0, tiled=True)
        for vector in vector_list
    )
    return weight_parts, vectors


def summed_by_kernel(lefts, rights, vector_list):
    triple_a, triple_b = by_core_wide(rights["triple"], ((0, 512, 1), (512, 384, 1)))
    pieces = dict(
        upstream=by_core(rights["upstream"]),
        hidden=by_core_wide(rights["hidden"], ((0, 384, 3),))[0],
        branch=by_core(rights["branch"]),
        triple_a=triple_a,
        triple_b=triple_b,
        stream=by_core(rights["stream"]),
    )
    vec = jnp.concatenate([vector.reshape(32, -1) for vector in vector_list], axis=1)
    vec = jnp.pad(vec, ((0, 0), (0, 512 - vec.shape[1]))).reshape(4, 2, 2, 2, 4, LANES)
    vec = vec.transpose(3, 2, 1, 0, 4, 5)
    found = weight_sums(lefts, pieces, vec)
    flat = found["vec"].reshape(-1)
    vectors, at = [], 0
    for vector in vector_list:
        width = vector.shape[0] // 32
        vectors.append(flat[at : at + width])
        at += width
    weight_parts = (
        found["skip"],
        found["attn"][:, :864],
        found["proj"],
        found["expand"],
        found["shrink"],
    )
    return weight_parts, tuple(vectors)


def on_device(
    tokens,
    skip_tokens,
    segment_ids,
    upstream,
    skip_weight,
    skip_bias,
    first_gain,
    first_shift,
    attn_weight,
    attn_bias,
    proj_weight,
    proj_bias,
    second_gain,
    second_shift,
    expand_weight,
    expand_bias,
    shrink_weight,
    shrink_bias,
):
    groups, shard_rows, features = tokens.shape
    head_dim = features // HEADS
    blocks = 4
    row_count = groups * shard_rows
    flat_tokens = tokens.reshape(row_count, features)
    flat_skip = skip_tokens.reshape(row_count, features)
    flat_upstream = upstream.reshape(row_count, features)
    joined = jnp.concatenate([flat_tokens, flat_skip], axis=1)
    stream = matmul(joined, skip_weight) + skip_bias.astype(jnp.float32)
    normed_full, first_back = jax.vjp(
        normalize, stream, first_gain.astype(jnp.float32), first_shift.astype(jnp.float32)
    )
    normed = normed_full.astype(jnp.bfloat16)
    triple = matmul(normed, attn_weight)
    bias_full = attn_bias.astype(jnp.float32)
    query_low = (triple[:, :features] + bias_full[:features]).astype(jnp.bfloat16)
    key_low = triple[:, features : 2 * features].astype(jnp.bfloat16)
    value_low = (triple[:, 2 * features :] + bias_full[features:]).astype(jnp.bfloat16)
    rim_rows = min(shard_rows, (ITEM_MOST + 6) // 8 * 8)
    stacked = jnp.stack([key_low, value_low]).reshape(2, groups, shard_rows, features)
    widened = padded(stacked, (("seq", 2),), rim_rows)
    position = lax.axis_index("seq")
    padded_ids = jnp.pad(segment_ids, ((0, 0), (rim_rows, rim_rows)), constant_values=-1)
    key_ids = lax.dynamic_slice_in_dim(
        padded_ids, position * shard_rows, shard_rows + 2 * rim_rows, 1
    )
    query_ids = lax.dynamic_slice_in_dim(segment_ids, position * shard_rows, shard_rows, 1)
    query_items = to_items(query_low.reshape(groups, shard_rows, features), blocks)
    key_items = to_items(widened[0], blocks)
    value_items = to_items(widened[1], blocks)
    query_id_items = jnp.repeat(query_ids, blocks, axis=0)
    key_id_items = jnp.repeat(key_ids, blocks, axis=0)
    mixed_items, lse_items = lax.map(
        partial(forward_block, head_dim=head_dim),
        (query_items, key_items, value_items, query_id_items, key_id_items),
    )
    mixed = from_items(mixed_items, blocks).reshape(row_count, features).astype(jnp.bfloat16)
    middle = stream + matmul(mixed, proj_weight) + proj_bias.astype(jnp.float32)
    second_full, second_back = jax.vjp(
        normalize, middle, second_gain.astype(jnp.float32), second_shift.astype(jnp.float32)
    )
    second = second_full.astype(jnp.bfloat16)
    hidden = matmul(second, expand_weight) + expand_bias.astype(jnp.float32)
    active_full, gelu_back = jax.vjp(partial(jax.nn.gelu, approximate=False), hidden)
    active = active_full.astype(jnp.bfloat16)
    result = (middle + matmul(active, shrink_weight) + shrink_bias.astype(jnp.float32)).astype(
        jnp.bfloat16
    )
    active_grad = matmul(flat_upstream, shrink_weight.T)
    shrink_bias_grad = jnp.sum(flat_upstream, axis=0, dtype=jnp.float32)
    hidden_grad = gelu_back(active_grad)[0].astype(jnp.bfloat16)
    expand_bias_grad = jnp.sum(hidden_grad, axis=0, dtype=jnp.float32)
    second_grad = matmul(hidden_grad, expand_weight.T)
    middle_norm_grad, second_gain_grad, second_shift_grad = second_back(second_grad)
    middle_grad = flat_upstream.astype(jnp.float32) + middle_norm_grad
    branch_grad = middle_grad.astype(jnp.bfloat16)
    proj_bias_grad = jnp.sum(branch_grad, axis=0, dtype=jnp.float32)
    mixed_grad = matmul(branch_grad, proj_weight.T).astype(jnp.bfloat16)
    grad_items = to_items(mixed_grad.reshape(groups, shard_rows, features), blocks)
    query_grads, key_grads, value_grads = lax.map(
        partial(backward_block, head_dim=head_dim),
        (query_items, key_items, value_items, query_id_items, key_id_items, grad_items, lse_items),
    )
    query_grad = from_items(query_grads, blocks).reshape(row_count, features).astype(jnp.bfloat16)
    window_grad = jnp.stack([from_items(key_grads, blocks), from_items(value_grads, blocks)])
    rim_grads = jnp.concatenate(
        [window_grad[:, :, :rim_rows], window_grad[:, :, shard_rows + rim_rows :]], axis=2
    )
    returned = padded(rim_grads.astype(jnp.bfloat16), (("seq", 2),), rim_rows).astype(
        rim_grads.dtype
    )
    owned = window_grad[:, :, rim_rows : rim_rows + shard_rows]
    owned = owned + jnp.pad(
        returned[:, :, :rim_rows], ((0, 0), (0, 0), (0, shard_rows - rim_rows), (0, 0))
    )
    owned = owned + jnp.pad(
        returned[:, :, 3 * rim_rows :], ((0, 0), (0, 0), (shard_rows - rim_rows, 0), (0, 0))
    )
    key_grad = owned[0].reshape(row_count, features).astype(jnp.bfloat16)
    value_grad = owned[1].reshape(row_count, features).astype(jnp.bfloat16)
    triple_grad = jnp.concatenate([query_grad, key_grad, value_grad], axis=1)
    attn_bias_grad = jnp.concatenate(
        [
            jnp.sum(query_grad, axis=0, dtype=jnp.float32),
            jnp.sum(value_grad, axis=0, dtype=jnp.float32),
        ]
    )
    normed_grad = matmul(triple_grad, attn_weight.T)
    stream_norm_grad, first_gain_grad, first_shift_grad = first_back(normed_grad)
    stream_grad = (middle_grad + stream_norm_grad).astype(jnp.bfloat16)
    skip_bias_grad = jnp.sum(stream_grad, axis=0, dtype=jnp.float32)
    skip_full = matmul(stream_grad, skip_weight.T)
    tokens_grad = skip_full[:, :features].astype(jnp.bfloat16)
    skip_grad = skip_full[:, features:].astype(jnp.bfloat16)
    vector_list = (
        skip_bias_grad,
        first_gain_grad,
        first_shift_grad,
        attn_bias_grad,
        proj_bias_grad,
        second_gain_grad,
        second_shift_grad,
        expand_bias_grad,
        shrink_bias_grad,
    )
    lefts = dict(active=active, second=second, mixed=mixed, normed=normed, joined=joined)
    rights = dict(
        upstream=flat_upstream,
        hidden=hidden_grad,
        branch=branch_grad,
        triple=triple_grad,
        stream=stream_grad,
    )
    if lax.axis_size("seq") == 8 and lax.axis_size("batch") == 4:
        weight_parts, vectors = summed_by_kernel(lefts, rights, vector_list)
    else:
        weight_parts, vectors = summed(lefts, rights, vector_list)
    return (
        result.reshape(groups, shard_rows, features),
        tokens_grad.reshape(groups, shard_rows, features),
        skip_grad.reshape(groups, shard_rows, features),
        weight_parts[0],
        vectors[0],
        vectors[1],
        vectors[2],
        weight_parts[1],
        vectors[3],
        weight_parts[2],
        vectors[4],
        vectors[5],
        vectors[6],
        weight_parts[3],
        vectors[7],
        weight_parts[4],
        vectors[8],
    )


def solution(mesh):
    in_specs = (
        P("batch", "seq", None),
        P("batch", "seq", None),
        P("batch", None),
        P("batch", "seq", None),
        P(),
        P(),
        P(),
        P(),
        P(),
        P(),
        P(),
        P(),
        P(),
        P(),
        P(),
        P(),
        P(),
        P(),
    )
    out_specs = (
        P("batch", "seq", None),
        P("batch", "seq", None),
        P("batch", "seq", None),
        P("seq", "batch"),
        P(("seq", "batch")),
        P(("seq", "batch")),
        P(("seq", "batch")),
        P("seq", "batch"),
        P(("seq", "batch")),
        P("seq", "batch"),
        P(("seq", "batch")),
        P(("seq", "batch")),
        P(("seq", "batch")),
        P("seq", "batch"),
        P(("seq", "batch")),
        P("seq", "batch"),
        P(("seq", "batch")),
    )
    return jax.shard_map(
        on_device, mesh=mesh, in_specs=in_specs, out_specs=out_specs, check_vma=False
    )
```

profile of v0, /device:TPU:0, one launch (start us, length us, event | category | flops | bytes accessed | tf_op | source)
XLA Modules:
  0.0 627.5 jit_solution(6008100060244435691)
XLA Ops:
  2.9 5.7 fusion.45
  10.8 3.7 fusion.50
  20.6 7.1 %collective-permute-start = (bf16[2,1,328,1152]{3,2,0,1:T(8,128)(2,1)}, bf16[2,1,328,1152]{3,2,0,1:T(8,128)(2,1)}, u32[]{:S(2)}, u32[]{:S(2)}) collective-permute-start(bf16[2,1,328,1152]{3,2,0,1:T(8,128)(2,1)} %get-tuple-element.257), channel_id=1, source_target_pairs={{0,4},{4,8},{8,12},{12,16},{16,20},{20,24},{24,28},{1,5},{5,9},{9,... | collective-permute-start | bytes 4534280 | tf_op jit(solution)/shard_map/ppermute | solution.py:23
  44.9 3.0 copy.82
  47.9 3.1 reshape.469
  53.8 2.8 pad_maximum_fusion.3.refs_4_
  57.5 32.5 %collective-permute-done = bf16[2,1,328,1152]{3,2,0,1:T(8,128)(2,1)} collective-permute-done((bf16[2,1,328,1152]{3,2,0,1:T(8,128)(2,1)}, bf16[2,1,328,1152]{3,2,0,1:T(8,128)(2,1)}, u32[]{:S(2)}, u32[]{:S(2)}) %collective-permute-start) | collective-permute-done | bytes 1511456 | tf_op jit(solution)/shard_map/ppermute | solution.py:23
  92.1 2.7 fusion.41
  94.8 5.2 copy.71
  99.9 5.2 copy.73
  108.1 29.2 %while.26 = (s32[]{:T(128)}, bf16[4,384,288]{1,2,0:T(8,128)(2,1)}, f32[4,4,384]{2,1,0:T(4,128)}, bf16[4,1040,288]{1,2,0:T(8,128)(2,1)}, s32[4,384]{1,0:T(4,128)S...) while((s32[]{:T(128)}, bf16[4,384,288]{1,2,0:T(8,128)(2,1)}, ...), condition=%wide.region_5.6_spmd, body=%wide.region_2.5_spmd.sunk | while | flops 473240064 | bytes 24955708 | solution.py:745
  137.3 3.3 fusion.46
  141.4 23.0 %multiply_convert_fusion.1 = (bf16[384,4608]{1,0:T(8,128)(2,1)}, f32[384,4608]{1,0:T(8,128)}, f32[384,4608]{1,0:T(8,128)}) fusion(f32[4608]{0:T(1024)S(1)} %copy-done.47, bf16[384,1152]{1,0:T(8,128)(2,1)S(1)} %add_convert_fusion.2.refs_1_, bf16[1152,4608]{1,0:T(8,128)(2,1)} %param.36), kind=kOutput, calls=%fused_computation.42 | convolution fusion | flops 4193648640 | bytes 29214720 | tf_op jit(solution)/shard_map/dot_general | solution.py:40
  164.4 14.8 %convert_reduce_fusion = (f32[4608]{0:T(1024)}, bf16[384,4608]{1,0:T(8,128)(2,1)S(1)}) fusion(f32[384,4608]{1,0:T(8,128)} %get-tuple-element.240, f32[384,4608]{1,0:T(8,128)} %get-tuple-element.273, bf16[4608,1152]{1,0:T(8,128)(2,1)} %param.38, bf16[1,384,1152]{2,1,0:T(8,128)(2,1)S(1)} %copy-done.15), kind=kOutput, calls=%fused_computation.40 | convolution fusion | flops 4105170432 | bytes 29214720 | tf_op jit(solution)/shard_map/dot_general | solution.py:40
  179.2 10.8 %multiply_reduce_fusion.1 = (f32[1152]{0:T(1024)}, f32[384]{0:T(512)S(1)}, f32[1152]{0:T(1024)}, f32[384,1152]{1,0:T(8,128)S(1)}) fusion(f32[384,1152]{1,0:T(8,128)S(1)} %get-tuple-element.272, f32[384]{0:T(512)S(1)} %fusion.34, f32[384]{0:T(512)S(1)} %broadcast_multiply_fusion, f32[1152]{0:T(1024)S(1)} %copy-done.36, ...), kind=kOutput, calls=%fused_computation.88 | convolution fusion | flops 4080399872 | bytes 17713152 | tf_op jit(solution)/shard_map/dot_general | solution.py:40
  193.7 2.4 convolution_convert_fusion.1
  198.8 64.7 %while.27 = (s32[]{:T(128)}, bf16[4,384,288]{1,2,0:T(8,128)(2,1)}, f32[4,1040,288]{1,2,0:T(8,128)}, f32[4,1040,288]{1,2,0:T(8,128)}, bf16[4,1040,288]{1,2,0:T(8,...) while((s32[]{:T(128)}, bf16[4,384,288]{1,2,0:T(8,128)(2,1)}, ...), condition=%wide.region_12.13_spmd, body=%wide.region_10.12_spmd.sunk | while | flops 1166529024 | bytes 76998608 | solution.py:772
  205.7 2.3 multiply_reduce_fusion.8
  221.7 2.3 multiply_reduce_fusion.8
  237.8 2.3 multiply_reduce_fusion.8
  254.0 2.3 multiply_reduce_fusion.8
  263.5 4.8 fusion.6
  272.6 3.5 fusion.80
  276.1 3.7 fusion.18
  283.8 3.9 reshape.471
  287.6 3.8 copy.76
  291.5 5.5 collective-permute-start.2
  297.0 3.8 copy.77
  302.0 2.3 copy.98
  308.4 3.1 copy.87
  311.5 3.1 reshape.475
  314.6 8.2 %copy.84 = bf16[384,2,2,1152]{0,3,1,2:T(8,128)(2,1)} copy(bf16[384,2,2,1152]{3,2,1,0:T(2,128)(2,1)S(1)} %reshape.471) | data formatting | bytes 7077888 | tf_op jit(solution)/shard_map/reshape | solution.py:625
  322.8 10.5 %copy.85 = bf16[2,3,384,2,384]{4,3,2,1,0:T(2,128)(2,1)S(1)} copy(bf16[2,3,384,2,384]{2,4,1,3,0:T(8,128)(2,1)} %bitcast.227) | data formatting | bytes 7077888 | tf_op jit(solution)/shard_map/transpose | solution.py:632
  333.4 4.0 reshape.473.refs_6_
  337.5 5.2 maximum_bitcast_fusion
  345.9 2.9 maximum_bitcast_fusion.2
  348.8 8.5 %fusion.22 = bf16[1,384,1152]{2,1,0:T(8,128)(2,1)} fusion(f32[384,1152]{1,0:T(8,128)S(1)} %copy-done.5, bf16[384,4608]{1,0:T(8,128)(2,1)S(1)} %copy-done.28, bf16[4608,1152]{1,0:T(8,128)(2,1)} %param.38, f32[1152]{0:T(1024)S(1)} %copy-done.56), kind=kOutput, calls=%fused_computation.78 | convolution fusion | flops 4078190592 | bytes 16814592 | tf_op jit(solution)/shard_map/dot_general | solution.py:40
  357.3 3.7 collective-permute-done.2
  361.0 3.7 copy.78
  364.8 3.7 copy.79
  368.5 11.2 %concatenate.72 = bf16[2,1,1312,1152]{2,3,0,1:T(8,128)(2,1)} concatenate(bf16[2,1,328,1152]{2,3,0,1:T(8,128)(2,1)} %copy.78, bf16[2,1,656,1152]{2,3,0,1:T(8,128)(2,1)S(1)} %copy-done.10, bf16[2,1,328,1152]{2,3,0,1:T(8,128)(2,1)} %copy.79), dimensions={2} | concatenate | bytes 12091392 | tf_op jit(solution)/shard_map/concatenate | solution.py:25
  379.7 3.7 bitcast_convert_fusion
  384.4 4.2 fusion.16
  390.3 7.6 %multiply_reduce_fusion.2 = (f32[1152]{0:T(1024)S(1)}, f32[384]{0:T(512)S(1)}, f32[1152]{0:T(1024)S(1)}, f32[384,1152]{1,0:T(8,128)S(1)}) fusion(f32[384,1152]{1,0:T(8,128)S(1)} %copy-done.3, f32[384]{0:T(512)S(1)} %copy-done.53, f32[384]{0:T(512)S(1)} %copy-done.45, f32[1152]{0:T(1024)S(1)} %copy-done.35, bf16[1152,3456]{1,0:T(8,128)(2,1)} %param.30, ...), kind=kOutput, calls=%fused_computation.92 | convolution fusion | flops 3069146624 | bytes 14174208 | tf_op jit(solution)/shard_map/dot_general | solution.py:40
  402.7 3.8 convolution_convert_fusion
  413.4 2.4 reshape_transpose_reshape.6.refs_8_
  425.1 186.7 %weight_sums.1 = (f32[576,288]{1,0:T(8,128)}, f32[144,1152]{1,0:T(8,128)}, f32[144,288]{1,0:T(8,128)}, f32[144,896]{1,0:T(8,128)}, f32[288,288]{1,0:T(8,128)}, /...) custom-call(bf16[384,4608]{1,0:T(8,128)(2,1)} %get-tuple-element.239, ...), custom_call_target="tpu_custom_call" | custom-call | tf_op jit(solution)/shard_map/weight_sums/pallas_call | solution.py:601
  616.0 2.9 slice_bitcast_fusion
  (356 shorter events, 179.9 us)
Async XLA Ops:
  0.7 136.6 %copy-start = (bf16[1152,1152]{1,0:T(8,128)(2,1)S(1)}, bf16[1152,1152]{1,0:T(8,128)(2,1)}, u32[]{:S(2)}) copy-start(bf16[1152,1152]{1,0:T(8,128)(2,1)} %param.32) | copy-start | bytes 7962628
  2.9 7.0 %copy-start.34 = (f32[1152]{0:T(1024)}, f32[1152]{0:T(1024)S(1)}, u32[]{:S(2)}) copy-start(f32[1152]{0:T(1024)S(1)} %convert_element_type.163) | copy-start | bytes 13828
  2.9 7.9 %slice-start = ((s8[7962624]{0:T(1024)(128)(4,1)}), s8[4194304]{0:T(1024)(128)(4,1)S(1)}, s32[]{:S(2)}) async-start(s8[7962624]{0:T(1024)(128)(4,1)} %bitcast.252), calls=%async_computation | async-start | bytes 8388608
  2.9 7.0 %copy-start.39 = (bf16[2304]{0:T(1024)(128)(2,1)S(1)}, bf16[2304]{0:T(1024)(128)(2,1)}, u32[]{:S(2)}) copy-start(bf16[2304]{0:T(1024)(128)(2,1)} %param.31) | copy-start | bytes 13828
  2.9 7.9 %slice-start.1 = ((s8[7962624]{0:T(1024)(128)(4,1)}), s8[3768320]{0:T(1024)(128)(4,1)S(1)}, s32[]{:S(2)}) async-start(s8[7962624]{0:T(1024)(128)(4,1)} %bitcast.252), calls=%async_computation.1 | async-start | bytes 7536640
  10.8 3.7 copy-start.26
  17.2 10.5 %copy-start.14 = (bf16[1,384,1152]{2,1,0:T(8,128)(2,1)S(1)}, bf16[1,384,1152]{2,1,0:T(8,128)(2,1)}, u32[]{:S(2)}) copy-start(bf16[1,384,1152]{2,1,0:T(8,128)(2,1)} %param.25) | copy-start | bytes 2654212
  17.2 15.5 %copy-start.57 = (bf16[1152]{0:T(1024)(128)(2,1)S(1)}, bf16[1152]{0:T(1024)(128)(2,1)}, u32[]{:S(2)}) copy-start(bf16[1152]{0:T(1024)(128)(2,1)} %param.33) | copy-start | bytes 6916
  19.1 16.6 %copy-start.58 = (bf16[1152]{0:T(1024)(128)(2,1)S(1)}, bf16[1152]{0:T(1024)(128)(2,1)}, u32[]{:S(2)}) copy-start(bf16[1152]{0:T(1024)(128)(2,1)} %param.35) | copy-start | bytes 6916
  19.1 38.4 %collective-permute-start.1 = (bf16[2,1,328,1152]{3,2,0,1:T(8,128)(2,1)}, bf16[2,1,328,1152]{3,2,0,1:T(8,128)(2,1)}, u32[]{:S(2)}, u32[]{:S(2)}) collective-permute-start(bf16[2,1,328,1152]{3,2,0,1:T(8,128)(2,1)} %get-tuple-element.258), channel_id=1, source_target_pairs={{4,0},{8,4},{12,8},{16,12},{20,16},{24,20},{28,24},{5,1},{9,5},{13... | collective-permute-start | bytes 4534280 | tf_op jit(solution)/shard_map/ppermute | solution.py:24
  20.6 69.5 %collective-permute-start = (bf16[2,1,328,1152]{3,2,0,1:T(8,128)(2,1)}, bf16[2,1,328,1152]{3,2,0,1:T(8,128)(2,1)}, u32[]{:S(2)}, u32[]{:S(2)}) collective-permute-start(bf16[2,1,328,1152]{3,2,0,1:T(8,128)(2,1)} %get-tuple-element.257), channel_id=1, source_target_pairs={{0,4},{4,8},{8,12},{12,16},{16,20},{20,24},{24,28},{1,5},{5,9},{9,... | collective-permute-start | bytes 4534280 | tf_op jit(solution)/shard_map/ppermute | solution.py:23
  51.0 39.0 %copy-start.7 = (bf16[2,1,384,1152]{3,2,0,1:T(8,128)(2,1)S(1)}, bf16[2,1,384,1152]{3,2,0,1:T(8,128)(2,1)}, u32[]{:S(2)}) copy-start(bf16[2,1,384,1152]{3,2,0,1:T(8,128)(2,1)} %copy-done.6) | copy-start | bytes 5308420
  140.6 49.4 %copy-start.4 = (f32[384,1152]{1,0:T(8,128)}, f32[384,1152]{1,0:T(8,128)S(1)}, u32[]{:S(2)}) copy-start(f32[384,1152]{1,0:T(8,128)S(1)} %get-tuple-element.272) | copy-start | bytes 5308420
  141.4 23.0 %copy-start.27 = (bf16[384,1152]{1,0:T(8,128)(2,1)}, bf16[384,1152]{1,0:T(8,128)(2,1)S(1)}, u32[]{:S(2)}) copy-start(bf16[384,1152]{1,0:T(8,128)(2,1)S(1)} %add_convert_fusion.2.refs_1_) | copy-start | bytes 2654212
  141.4 23.0 %copy-start.15 = (bf16[1,384,1152]{2,1,0:T(8,128)(2,1)S(1)}, bf16[1,384,1152]{2,1,0:T(8,128)(2,1)}, u32[]{:S(2)}) copy-start(bf16[1,384,1152]{2,1,0:T(8,128)(2,1)} %param.25) | copy-start | bytes 2654212
  179.2 10.8 %copy-start.22 = (bf16[384,4608]{1,0:T(8,128)(2,1)}, bf16[384,4608]{1,0:T(8,128)(2,1)S(1)}, u32[]{:S(2)}) copy-start(bf16[384,4608]{1,0:T(8,128)(2,1)S(1)} %get-tuple-element.277) | copy-start | bytes 10616836
  190.6 5.4 copy-start.48
  199.0 3.9 copy-start.11
  199.0 3.9 copy-start.19
  215.1 3.9 copy-start.11
  215.1 3.9 copy-start.19
  231.2 3.9 copy-start.11
  231.2 3.9 copy-start.19
  247.4 3.9 copy-start.11
  247.4 3.9 copy-start.19
  276.1 3.7 copy-start.13
  276.1 5.2 copy-start.24
  291.5 69.6 %collective-permute-start.2 = (bf16[2,1,328,1152]{3,2,1,0:T(8,128)(2,1)}, bf16[2,1,328,1152]{3,2,1,0:T(8,128)(2,1)}, u32[]{:S(2)}, u32[]{:S(2)}) collective-permute-start(bf16[2,1,328,1152]{3,2,1,0:T(8,128)(2,1)} %copy.76), channel_id=1, source_target_pairs={{0,4},{4,8},{8,12},{12,16},{16,20},{20,24},{24,28},{1,5},{5,9},{9,... | collective-permute-start | bytes 4534280 | tf_op jit(solution)/shard_map/ppermute | solution.py:23
  300.8 64.0 %collective-permute-start.3 = (bf16[2,1,328,1152]{3,2,1,0:T(8,128)(2,1)}, bf16[2,1,328,1152]{3,2,1,0:T(8,128)(2,1)}, u32[]{:S(2)}, u32[]{:S(2)}) collective-permute-start(bf16[2,1,328,1152]{3,2,1,0:T(8,128)(2,1)} %copy.77), channel_id=1, source_target_pairs={{4,0},{8,4},{12,8},{16,12},{20,16},{24,20},{28,24},{5,1},{9,5},{13... | collective-permute-start | bytes 4534280 | tf_op jit(solution)/shard_map/ppermute | solution.py:24
  337.4 5.3 copy-start.17
  337.4 6.3 copy-start.40
  337.4 6.4 %copy-start.55 = (f32[1152]{0:T(1024)S(1)}, f32[1152]{0:T(1024)}, u32[]{:S(2)}) copy-start(f32[1152]{0:T(1024)} %get-tuple-element.187) | copy-start | bytes 13828
  337.4 7.1 %copy-start.54 = (f32[1152]{0:T(1024)S(1)}, f32[1152]{0:T(1024)}, u32[]{:S(2)}) copy-start(f32[1152]{0:T(1024)} %get-tuple-element.191) | copy-start | bytes 13828
  337.4 7.8 %copy-start.46 = (f32[4608]{0:T(1024)S(1)}, f32[4608]{0:T(1024)}, u32[]{:S(2)}) copy-start(f32[4608]{0:T(1024)} %get-tuple-element.276) | copy-start | bytes 55300
  337.4 8.5 %copy-start.29 = (bf16[2,384,512]{2,1,0:T(8,128)(2,1)S(1)}, bf16[2,384,512]{2,1,0:T(8,128)(2,1)}, u32[]{:S(2)}) copy-start(bf16[2,384,512]{2,1,0:T(8,128)(2,1)} %reshape.469) | copy-start | bytes 2359300
  337.4 8.5 %copy-start.30 = (bf16[2,384,512]{2,1,0:T(8,128)(2,1)S(1)}, bf16[2,384,512]{2,1,0:T(8,128)(2,1)}, u32[]{:S(2)}) copy-start(bf16[2,384,512]{2,1,0:T(8,128)(2,1)} %reshape.475) | copy-start | bytes 2359300
  342.7 6.1 copy-start.5
  342.7 6.1 copy-start.56
  357.3 11.2 %copy-start.10 = (bf16[2,1,656,1152]{2,3,0,1:T(8,128)(2,1)S(1)}, bf16[2,1,656,1152]{2,3,0,1:T(8,128)(2,1)}, u32[]{:S(2)}) copy-start(bf16[2,1,656,1152]{2,3,0,1:T(8,128)(2,1)} %maximum_bitcast_fusion) | copy-start | bytes 9068548
  398.3 4.4 slice-start.2
  417.2 3.7 copy-start.31
  418.2 4.8 copy-start.41
  418.2 4.9 copy-start.43
  418.3 4.9 copy-start.33
  418.3 4.9 copy-start.37
  418.3 4.9 copy-start.38
  611.8 7.1 %copy-start.32 = (f32[576,288]{1,0:T(8,128)S(1)}, f32[576,288]{1,0:T(8,128)}, u32[]{:S(2)}) copy-start(f32[576,288]{1,0:T(8,128)} %get-tuple-element.185) | copy-start | bytes 1990660
  616.0 11.4 %copy-start.1 = (bf16[1152,1152]{1,0:T(8,128)(2,1)S(1)}, bf16[1152,1152]{1,0:T(8,128)(2,1)}, u32[]{:S(2)}) copy-start(bf16[1152,1152]{1,0:T(8,128)(2,1)} %param.32) | copy-start | bytes 7962628
  (32 other events, 56.9 us)
where the time goes:
time: 639 us; the launch traced here: 628 us
  local copies, waits for them, and re-layouts  205 us (32%)
  Pallas kernels  187 us (29%)
  matrix products  122 us (19%)
  other arithmetic  59.5 us (9%)
  waiting for transfers between devices  37.1 us (6%)
  starting transfers between devices  15.3 us (2%)
    pallas_call x1, Pallas kernels, weight_sums(): pl.pallas_call(kernel, out_shape=out_shape, in_specs=in_specs, out_specs=...  187 us
    dot_general x10, matrix products, matmul(): return jnp.dot(operand, other_op, preferred_element_type=jnp.float32)  83.7 us
    ppermute x2, waiting for transfers between devices, padded(): before = lax.ppermute(last, axis, up)  36.2 us
    dynamic_slice x40, local copies, waits for them, and re-layouts, on_device(): lax.map(partial(forward_block, head_dim=head_dim), (query_items, key_item...  26.9 us
    unnamed x130, local copies, waits for them, and re-layouts  23.4 us
    dot_general x8, matrix products, masked_scores(): jnp.einsum('qhd,khd->hqk', query_heads, key_heads, preferred_element_type...  14.7 us
  transfers between devices with their start and end apart: 4, of which 3 were waited for; matrix products, arithmetic and copies ran while one was open for 15% of the time, Pallas kernels for 0%

commit v1 on v0

--- a/solution.py
+++ b/solution.py
@@ -1,5 +1,3 @@
-from functools import partial
-
 import jax
 import jax.numpy as jnp
 from jax import lax
@@ -8,119 +6,619 @@
 from jax.sharding import PartitionSpec as P
 
 HEADS = 16
+HEAD_DIM = 72
 ITEM_MOST = 322
 LANES = 128
 MESH = pl.DeviceIdType.MESH
-
-
-def padded(value, sides, width):
-    for axis, dim in sides:
-        size, length = (lax.axis_size(axis), value.shape[dim])
-        up = [(i, (i + 1) % size) for i in range(size - 1)]
-        down = [(j, i) for i, j in up]
-        last = lax.slice_in_dim(value, length - width, length, axis=dim)
-        first = lax.slice_in_dim(value, 0, width, axis=dim)
-        before = lax.ppermute(last, axis, up)
-        after = lax.ppermute(first, axis, down)
-        value = jnp.concatenate([before, value, after], axis=dim)
-    return value
-
-
-def shortened(value):
-    return jax.tree.map(lambda a: a.astype(jnp.bfloat16) if a.dtype == jnp.float32 else a, value)
-
-
-def normalize(inputs, gain_vec, shift_vec):
-    centred = inputs - jnp.mean(inputs, axis=-1, keepdims=True)
-    variance = jnp.mean(centred * centred, axis=-1, keepdims=True)
-    return centred * lax.rsqrt(variance + 1e-05) * gain_vec + shift_vec
-
-
-def matmul(operand, other_op):
-    return jnp.dot(operand, other_op, preferred_element_type=jnp.float32)
-
-
-def outer_sum(left, right):
+SCALE2 = HEAD_DIM**-0.5 * 1.4426950408889634
+
+
+ROOT2 = 2.0**0.5
+
+
+def dot(left, right):
+    return jnp.dot(left, right, preferred_element_type=jnp.float32)
+
+
+def dot_nt(left, right):
+    return lax.dot_general(
+        left, right, (((1,), (1,)), ((), ())), preferred_element_type=jnp.float32
+    )
+
+
+def dot_tn(left, right):
     return lax.dot_general(
         left, right, (((0,), (0,)), ((), ())), preferred_element_type=jnp.float32
     )
 
 
-def to_items(tensor, blocks):
-    group_count, length, features = tensor.shape
-    reshaped = tensor.reshape(group_count, length, blocks, features // blocks)
-    return jnp.transpose(reshaped, (0, 2, 1, 3)).reshape(
-        group_count * blocks, length, features // blocks
-    )
-
-
-def from_items(tensor, blocks):
-    item_count, length, features = tensor.shape
-    reshaped = tensor.reshape(item_count // blocks, blocks, length, features)
-    return jnp.transpose(reshaped, (0, 2, 1, 3)).reshape(
-        item_count // blocks, length, blocks * features
-    )
-
-
-def masked_scores(query_part, key_part, query_ids, key_ids, head_dim):
-    query_heads = query_part.reshape(query_part.shape[0], -1, head_dim)
-    key_heads = key_part.reshape(key_part.shape[0], -1, head_dim)
-    products = jnp.einsum(
-        "qhd,khd->hqk", query_heads, key_heads, preferred_element_type=jnp.float32
-    )
-    matching = query_ids[:, None] == key_ids[None, :]
-    return jnp.where(matching[None], products * head_dim ** (-0.5), -1e30)
-
-
-def forward_block(pieces, head_dim):
-    query_part, key_part, value_part, query_ids, key_ids = pieces
-    scores = masked_scores(query_part, key_part, query_ids, key_ids, head_dim)
-    highest = jnp.max(scores, axis=-1, keepdims=True)
-    raised = jnp.exp(scores - highest)
-    denominator = jnp.sum(raised, axis=-1, keepdims=True)
-    attention = raised / denominator
-    value_heads = value_part.reshape(value_part.shape[0], -1, head_dim)
-    mixed_heads = jnp.einsum(
-        "hqk,khd->qhd",
-        attention.astype(jnp.bfloat16),
-        value_heads,
-        preferred_element_type=jnp.float32,
-    )
-    return (mixed_heads.reshape(query_part.shape[0], -1), (highest + jnp.log(denominator))[..., 0])
-
-
-def backward_block(pieces, head_dim):
-    query_part, key_part, value_part, query_ids, key_ids, grad_part, lse_part = pieces
-    length = query_part.shape[0]
-    key_span = key_part.shape[0]
-    scores = masked_scores(query_part, key_part, query_ids, key_ids, head_dim)
-    attention = jnp.exp(scores - lse_part[..., None])
-    query_heads = query_part.reshape(length, -1, head_dim)
-    key_heads = key_part.reshape(key_span, -1, head_dim)
-    value_heads = value_part.reshape(key_span, -1, head_dim)
-    grad_heads = grad_part.reshape(length, -1, head_dim)
-    prob_grad = jnp.einsum(
-        "qhd,khd->hqk", grad_heads, value_heads, preferred_element_type=jnp.float32
-    )
-    row_dot = jnp.sum(attention * prob_grad, axis=-1, keepdims=True)
-    score_grad = (head_dim ** (-0.5) * attention * (prob_grad - row_dot)).astype(jnp.bfloat16)
-    query_grad = jnp.einsum(
-        "hqk,khd->qhd", score_grad, key_heads, preferred_element_type=jnp.float32
-    )
-    key_grad = jnp.einsum(
-        "hqk,qhd->khd", score_grad, query_heads, preferred_element_type=jnp.float32
-    )
-    value_grad = jnp.einsum(
-        "hqk,qhd->khd",
-        attention.astype(jnp.bfloat16),
-        grad_heads,
-        preferred_element_type=jnp.float32,
-    )
-    return (
-        query_grad.reshape(length, -1),
-        key_grad.reshape(key_span, -1),
-        value_grad.reshape(key_span, -1),
-    )
+def whole():
+    return pl.BlockSpec(memory_space=pltpu.VMEM)
+
+
+def anywhere():
+    return pl.BlockSpec(memory_space=pl.ANY)
+
+
+def params():
+    return pltpu.CompilerParams(vmem_limit_bytes=60 * 2**20)
+
+
+def erf(value):
+    v = jnp.clip(value, -3.832506856900711, 3.832506856900711)
+    s = v * v
+    top = 0.00022905065861350646
+    for a in (0.0034082910107109506, 0.050955695062380861, 0.18520832239976145, 1.128379143519084):
+        top = top * s + a
+    low = -1.1791602954361697e-7
+    for a in (0.000023547966471313185, 0.0010179625278914885, 0.014070470171167667):
+        low = low * s + a
+    low = (low * s + 0.11098505178285362) * s + 0.49746925110067538
+    return v * top / (low * s + 1.0)
+
+
+def row_norm(value):
+    centred = value - jnp.mean(value, axis=-1, keepdims=True)
+    scale = lax.rsqrt(jnp.mean(centred * centred, axis=-1, keepdims=True) + 1e-05)
+    return centred * scale, scale
+
+
+def norm_back(unit, scale, gain, cotangent):
+    inner = cotangent * gain
+    mean = jnp.mean(inner, axis=-1, keepdims=True)
+    along = jnp.mean(inner * unit, axis=-1, keepdims=True)
+    return scale * (inner - mean - unit * along)
+
+
+def column_sum(value):
+    return jnp.sum(value, axis=0, keepdims=True)
+
+
+def stream_kernel(tok, skp, weight, bias, gain, shift, stream, normed, held, sems):
+    copies = [
+        pltpu.make_async_copy(weight.at[:, pl.ds(384 * n, 384)], held.at[n], sems.at[n])
+        for n in range(3)
+    ]
+    for copy in copies:
+        copy.start()
+    features = tok.shape[1]
+    for n, copy in enumerate(copies):
+        copy.wait()
+        at = slice(384 * n, 384 * n + 384)
+        stream[:, at] = (
+            dot(tok[...], held[n, :features])
+            + dot(skp[...], held[n, features:])
+            + bias[:, at].astype(jnp.float32)
+        )
+    unit, _ = row_norm(stream[...])
+    normed[...] = (unit * gain[...].astype(jnp.float32) + shift[...].astype(jnp.float32)).astype(
+        jnp.bfloat16
+    )
+
+
+def stream_norm(tok, skp, weight, bias, gain, shift):
+    rows, features = tok.shape
+    return pl.pallas_call(
+        stream_kernel,
+        out_shape=(
+            jax.ShapeDtypeStruct((rows, features), jnp.float32),
+            jax.ShapeDtypeStruct((rows, features), jnp.bfloat16),
+        ),
+        in_specs=[whole(), whole(), anywhere(), whole(), whole(), whole()],
+        out_specs=(whole(), whole()),
+        scratch_shapes=[
+            pltpu.VMEM((3, 2 * features, 384), jnp.bfloat16),
+            pltpu.SemaphoreType.DMA((3,)),
+        ],
+        compiler_params=params(),
+        cost_estimate=pl.CostEstimate(
+            flops=4 * rows * features * features, bytes_accessed=10**7, transcendentals=0
+        ),
+        name="stream_norm",
+    )(tok, skp, weight, bias[None], gain[None], shift[None])
+
+
+MARKS = (HEAD_DIM, HEAD_DIM + 16, HEAD_DIM + 32)
+
+
+def lanes_of(shape):
+    return lax.broadcasted_iota(jnp.int32, shape, len(shape) - 1)
+
+
+def marked(lane):
+    return (lane == MARKS[0]) | (lane == MARKS[1]) | (lane == MARKS[2])
+
+
+def head_tile(value, h, ones):
+    rows = value.shape[0]
+    lane = lanes_of((rows, LANES - HEAD_DIM)) + HEAD_DIM
+    rest = jnp.where(marked(lane) & ones, 1.0, 0.0).astype(value.dtype)
+    return jnp.concatenate([value[:, HEAD_DIM * h : HEAD_DIM * (h + 1)], rest], axis=1)
+
+
+def project(rows_ref, weight_ref, bias, part, store):
+    features = rows_ref.shape[1]
+    value = dot(rows_ref[...], weight_ref[...])
+    if part != 1:
+        at = 0 if part == 0 else features
+        value = value + bias[:, at : at + features].astype(jnp.float32)
+    value = value.astype(jnp.bfloat16)
+    for h in range(HEADS):
+        store(part, h, head_tile(value, h, part > 0))
+
+
+def project_kernel(normed, weight, bias, out, held, sems):
+    features = normed.shape[1]
+    copies = [
+        pltpu.make_async_copy(weight.at[:, pl.ds(features * p, features)], held.at[p], sems.at[p])
+        for p in range(3)
+    ]
+    for copy in copies:
+        copy.start()
+
+    def store(part, h, value):
+        out[part, h] = value
+
+    for p, copy in enumerate(copies):
+        copy.wait()
+        project(normed, held.at[p], bias, p, store)
+
+
+def own_heads(normed, weight, bias):
+    rows, features = normed.shape
+    return pl.pallas_call(
+        project_kernel,
+        out_shape=jax.ShapeDtypeStruct((3, HEADS, rows, LANES), jnp.bfloat16),
+        in_specs=[whole(), anywhere(), whole()],
+        out_specs=whole(),
+        scratch_shapes=[
+            pltpu.VMEM((3, features, features), jnp.bfloat16),
+            pltpu.SemaphoreType.DMA((3,)),
+        ],
+        compiler_params=params(),
+        cost_estimate=pl.CostEstimate(
+            flops=6 * rows * features * features, bytes_accessed=2 * 10**7, transcendentals=0
+        ),
+        name="own_heads",
+    )(normed, weight, bias[None])
+
+
+HIDE = -1e30
+
+
+def attend_kernel(own, before, after, weight, bias, id_col, id_row, wins, mixed, lse, *scratch):
+    window, halo, held, hide, gathered, sems, out_sems = scratch
+    rim, features = before.shape
+    rows = own.shape[2]
+    span = 3 * rows
+    copies = [
+        pltpu.make_async_copy(weight.at[:, pl.ds(features * p, features)], held.at[p], sems.at[p])
+        for p in range(3)
+    ]
+    copies.append(pltpu.make_async_copy(own, window.at[:, :, pl.ds(rows, rows)], sems.at[3]))
+    for copy in copies:
+        copy.start()
+    pad = rows - rim
+    window[:, :, 0:pad] = jnp.zeros((3, HEADS, pad, LANES), jnp.bfloat16)
+    window[:, :, span - pad : span] = jnp.zeros((3, HEADS, pad, LANES), jnp.bfloat16)
+    halo[0:rim] = before[...]
+    halo[rim:] = after[...]
+
+    def store(part, h, value):
+        window[part, h, pad:rows] = value[:rim]
+        window[part, h, 2 * rows : 2 * rows + rim] = value[rim:]
+
+    for p in (1, 2, 0):
+        copies[p].wait()
+        project(halo, held.at[p], bias, p, store)
+    copies[3].wait()
+    out_copies = [
+        pltpu.make_async_copy(window.at[p], wins.at[p], out_sems.at[p]) for p in range(3)
+    ]
+    for copy in out_copies:
+        copy.start()
+    blocks = rows // LANES
+    reach = span - (blocks - 1) * LANES
+    for i in range(blocks):
+        same = id_col[rows + i * LANES : rows + (i + 1) * LANES] == (
+            id_row[:, i * LANES : i * LANES + reach]
+        )
+        hide[i] = jnp.where(same, 0.0, HIDE)
+    lse[...] = jnp.zeros_like(lse)
+
+    def body(h, carry):
+        for i in range(blocks):
+            keys = pl.ds(i * LANES, reach)
+            scores = dot_nt(
+                window[0, h, rows + i * LANES : rows + (i + 1) * LANES], window[1, h, keys]
+            )
+            scores = scores * SCALE2 + hide[i]
+            highest = jnp.max(scores, axis=-1, keepdims=True)
+            raised = jnp.exp2(scores - highest).astype(jnp.bfloat16)
+            total = dot(raised, window[2, h, keys])
+            denominator = total[:, HEAD_DIM : HEAD_DIM + 1]
+            gathered[h, i * LANES : (i + 1) * LANES] = total / denominator
+            value = highest + jnp.log2(denominator)
+            at = slice(i * LANES, (i + 1) * LANES)
+            lse[at] = jnp.where(lanes_of((LANES, LANES)) == h, value, lse[at])
+        return carry
+
+    lax.fori_loop(0, HEADS, body, 0)
+    for h in range(HEADS):
+        mixed[:, HEAD_DIM * h : HEAD_DIM * (h + 1)] = gathered[h, :, :HEAD_DIM].astype(jnp.bfloat16)
+    for copy in out_copies:
+        copy.wait()
+
+
+def attend(own, before, after, weight, bias, id_col, id_row):
+    rim, features = before.shape
+    rows = own.shape[2]
+    span = 3 * rows
+    return pl.pallas_call(
+        attend_kernel,
+        out_shape=(
+            jax.ShapeDtypeStruct((3, HEADS, span, LANES), jnp.bfloat16),
+            jax.ShapeDtypeStruct((rows, features), jnp.bfloat16),
+            jax.ShapeDtypeStruct((rows, LANES), jnp.float32),
+        ),
+        in_specs=[anywhere(), whole(), whole(), anywhere(), whole(), whole(), whole()],
+        out_specs=(anywhere(), whole(), whole()),
+        scratch_shapes=[
+            pltpu.VMEM((3, HEADS, span, LANES), jnp.bfloat16),
+            pltpu.VMEM((2 * rim, features), jnp.bfloat16),
+            pltpu.VMEM((3, features, features), jnp.bfloat16),
+            pltpu.VMEM((rows // LANES, LANES, span - rows + LANES), jnp.float32),
+            pltpu.VMEM((HEADS, rows, LANES), jnp.float32),
+            pltpu.SemaphoreType.DMA((4,)),
+            pltpu.SemaphoreType.DMA((3,)),
+        ],
+        compiler_params=params(),
+        name="attend",
+    )(own, before, after, weight, bias[None], id_col, id_row)
+
+
+def by_core_store(ref, value):
+    rows = value.shape[0]
+    blank = jnp.zeros((rows, LANES - 32), value.dtype)
+    for b in range(4):
+        x, c = b // 2, b % 2
+        ref[c, 0, :, 256 * x : 256 * x + 256] = value[:, 288 * b : 288 * b + 256]
+        ref[c, 0, :, 512 + LANES * x : 640 + LANES * x] = jnp.concatenate(
+            [value[:, 288 * b + 256 : 288 * b + 288], blank], axis=1
+        )
+
+
+def split3(value):
+    first = value.astype(jnp.bfloat16)
+    rest = value - first.astype(jnp.float32)
+    second = rest.astype(jnp.bfloat16)
+    return first, second, (rest - second.astype(jnp.float32)).astype(jnp.bfloat16)
+
+
+def layer_kernel(
+    stream, mixed, lse, upstream, proj, proj_bias, gain, shift, expand, expand_bias, shrink,
+    shrink_bias, result, active, hidden_by_core, second, branch, branch_by_core, up_by_core,
+    middle_grad, mixed_grad, hidden_sum, sums, middle, total, second_grad,
+):
+    step, steps = pl.program_id(0), pl.num_programs(0)
+    low = jnp.bfloat16
+
+    @pl.when(step == 0)
+    def _():
+        middle[...] = (
+            stream[...] + dot(mixed[...], proj[...]) + proj_bias[...].astype(jnp.float32)
+        )
+        unit, _ = row_norm(middle[...])
+        second[...] = (
+            unit * gain[...].astype(jnp.float32) + shift[...].astype(jnp.float32)
+        ).astype(low)
+        total[...] = middle[...] + shrink_bias[...].astype(jnp.float32)
+        second_grad[...] = jnp.zeros_like(second_grad)
+        by_core_store(up_by_core, upstream[...])
+
+    hidden = dot(second[...], expand[...]) + expand_bias[...].astype(jnp.float32)
+    active_grad = dot_nt(upstream[...], shrink[...])
+    cdf = 0.5 + 0.5 * erf(hidden * (1.0 / ROOT2))
+    density = jnp.exp(-0.5 * hidden * hidden) * 0.3989422804014327
+    raised = (hidden * cdf).astype(low)
+    active[...] = raised
+    hidden_grad = (active_grad * (cdf + hidden * density)).astype(low)
+    for j in range(3):
+        hidden_by_core[0, j] = hidden_grad[:, 384 * j : 384 * (j + 1)]
+    hidden_sum[...] = column_sum(hidden_grad.astype(jnp.float32))
+    total[...] += dot(raised, shrink[...])
+    second_grad[...] += dot_nt(hidden_grad, expand[...])
+
+    @pl.when(step == steps - 1)
+    def _():
+        result[...] = total[...].astype(low)
+        unit, scale = row_norm(middle[...])
+        cotangent = second_grad[...]
+        above = upstream[...].astype(jnp.float32)
+        grad = above + norm_back(unit, scale, gain[...].astype(jnp.float32), cotangent)
+        middle_grad[...] = grad
+        branched = grad.astype(low)
+        branch[...] = branched
+        by_core_store(branch_by_core, branched)
+        sums[0:1] = column_sum(branched.astype(jnp.float32))
+        sums[1:2] = column_sum(cotangent * unit)
+        sums[2:3] = column_sum(cotangent)
+        sums[3:4] = column_sum(above)
+        back = dot_nt(branched, proj[...]).astype(low)
+        features = back.shape[1]
+        mixed_grad[:, :features] = back
+        products = back.astype(jnp.float32) * mixed[...].astype(jnp.float32)
+        shape = (features, LANES)
+        member = lax.broadcasted_iota(jnp.int32, shape, 0) // HEAD_DIM == lanes_of(shape)
+        member = jnp.where(member, 1.0, 0.0).astype(low)
+        high = products.astype(low)
+        inner = dot(high, member) + dot((products - high.astype(jnp.float32)).astype(low), member)
+        pieces = [part[:, :HEADS] for part in split3(lse[...] * (-1.0 / SCALE2)) + split3(-inner)]
+        blank = jnp.zeros((back.shape[0], LANES - 6 * HEADS), low)
+        mixed_grad[:, features:] = jnp.concatenate(pieces + [blank], axis=1)
+
+
+def layer(stream, mixed, lse, upstream, weights):
+    proj, proj_bias, gain, shift, expand, expand_bias, shrink, shrink_bias = weights
+    rows, features = stream.shape
+    hidden = expand.shape[1]
+    wide = hidden // 4
+    low = jnp.bfloat16
+
+    def held(shape):
+        return pl.BlockSpec(shape, lambda t: (0,) * len(shape))
+
+    narrow = (rows, features)
+    vector = (1, features)
+    split = (2, 1, rows, 768)
+    return pl.pallas_call(
+        layer_kernel,
+        grid=(4,),
+        in_specs=[
+            held(narrow), held(narrow), held((rows, LANES)), held(narrow),
+            held((features, features)), held(vector), held(vector), held(vector),
+            pl.BlockSpec((features, wide), lambda t: (0, t)),
+            pl.BlockSpec((1, wide), lambda t: (0, t)),
+            pl.BlockSpec((wide, features), lambda t: (t, 0)),
+            held(vector),
+        ],
+        out_specs=(
+            held(narrow),
+            pl.BlockSpec((rows, wide), lambda t: (0, t)),
+            pl.BlockSpec((1, 3, rows, 384), lambda t: (t % 2, 0, 0, t // 2)),
+            held(narrow), held(narrow), held(split), held(split), held(narrow),
+            held((rows, features + LANES)),
+            pl.BlockSpec((1, wide), lambda t: (0, t)),
+            held((8, features)),
+        ),
+        out_shape=(
+            jax.ShapeDtypeStruct(narrow, low),
+            jax.ShapeDtypeStruct((rows, hidden), low),
+            jax.ShapeDtypeStruct((2, 3, rows, 768), low),
+            jax.ShapeDtypeStruct(narrow, low),
+            jax.ShapeDtypeStruct(narrow, low),
+            jax.ShapeDtypeStruct(split, low),
+            jax.ShapeDtypeStruct(split, low),
+            jax.ShapeDtypeStruct(narrow, jnp.float32),
+            jax.ShapeDtypeStruct((rows, features + LANES), low),
+            jax.ShapeDtypeStruct((1, hidden), jnp.float32),
+            jax.ShapeDtypeStruct((8, features), jnp.float32),
+        ),
+        scratch_shapes=[pltpu.VMEM(narrow, jnp.float32)] * 3,
+        compiler_params=params(),
+        name="layer",
+    )(
+        stream, mixed, lse, upstream, proj, proj_bias[None], gain[None], shift[None], expand,
+        expand_bias[None], shrink, shrink_bias[None],
+    )
+
+
+def back_masks(id_col, id_row, own_hide, rim_hide, rows):
+    blocks = rows // LANES
+    reach = own_hide.shape[2]
+
+    def hidden(first, keys, width):
+        same = id_col[first : first + LANES] == id_row[:, keys : keys + width]
+        return jnp.where(same, 0.0, HIDE)
+
+    for i in range(blocks):
+        own_hide[i] = hidden(rows + i * LANES, i * LANES, reach)
+    for w in range(blocks):
+        rim_hide[w] = hidden(w * LANES, rows, rows)
+        rim_hide[blocks + w] = hidden(2 * rows + w * LANES, rows, rows)
+
+
+def with_stats(value, stats, shift):
+    lane = lanes_of(value.shape)
+    moved = pltpu.roll(stats, shift, 1)
+    return jnp.where(marked(lane), moved, value.astype(jnp.float32)).astype(value.dtype)
+
+
+def back_head(h, queries, keys, values, grads, stats, own_hide, rim_hide, probs, scored, store):
+    span = queries.shape[0]
+    rows = span // 3
+    blocks = rows // LANES
+    reach = span - rows + LANES
+    low = jnp.bfloat16
+    queries[...] = with_stats(queries[...], stats[...], MARKS[0] - h)
+    turn = MARKS[0] - 3 * HEADS - h
+    grads[...] = with_stats(grads[...], stats[...], jnp.where(turn < 0, turn + LANES, turn))
+
+    def pair(q_at, k_at, width, hide):
+        q_rows, k_rows = pl.ds(q_at, LANES), pl.ds(k_at, width)
+        exponent = dot_nt(queries[q_rows], keys[k_rows]) * SCALE2 + hide
+        weight = jnp.exp2(exponent)
+        scored = weight * dot_nt(grads[q_rows], values[k_rows])
+        return weight.astype(low), scored.astype(low)
+
+    query_grad = []
+    for i in range(blocks):
+        at = rows + i * LANES
+        weight, score = pair(at, i * LANES, reach, own_hide[i])
+        query_grad.append(dot(score, keys[i * LANES : i * LANES + reach]))
+        mine = slice(rows - i * LANES, 2 * rows - i * LANES)
+        probs[at : at + LANES] = weight[:, mine]
+        scored[at : at + LANES] = score[:, mine]
+    for w in range(blocks):
+        for at, first, width in (
+            (w * LANES, 0, (w + 1) * LANES),
+            (2 * rows + w * LANES, w * LANES, rows - w * LANES),
+        ):
+            hide = rim_hide[w if at < rows else blocks + w]
+            weight, score = pair(at, rows + first, width, hide[:, first : first + width])
+            probs[at : at + LANES, first : first + width] = weight
+            scored[at : at + LANES, first : first + width] = score
+    factor = HEAD_DIM**-0.5
+    for i in range(blocks):
+        store(0, i * LANES, LANES, query_grad[i] * factor)
+    store(1, 0, rows, dot_tn(scored[...], queries[...]) * factor)
+    store(2, 0, rows, dot_tn(probs[...], grads[...]))
+
+
+def heads_apart(row_ref, out):
+    value = row_ref[...]
+    for h in range(HEADS):
+        out[h] = head_tile(value[:, : HEADS * HEAD_DIM], h, False)
+
+
+def triple_store(apart, triple, triple_a, triple_b):
+    features = HEADS * HEAD_DIM
+    rows = apart.shape[2]
+    for p in range(3):
+        for h in range(HEADS):
+            at = features * p + HEAD_DIM * h
+            triple[:, at : at + HEAD_DIM] = apart[p, h, :, :HEAD_DIM]
+    for b in range(4):
+        x, c = b // 2, b % 2
+        value = triple[:, 864 * b : 864 * (b + 1)]
+        triple_a[c, 0, :, 512 * x : 512 * (x + 1)] = value[:, :512]
+        rest = jnp.concatenate([value[:, 512:], jnp.zeros((rows, 32), value.dtype)], axis=1)
+        triple_b[c, 0, :, 384 * x : 384 * (x + 1)] = rest
+
+
+def attend_back_kernel(
+    wins, grads_in, stats, id_col, id_row, triple, triple_a, triple_b, sums,
+    window, grads, own_hide, rim_hide, probs, scored, apart, sems,
+):
+    span = window.shape[2]
+    rows = span // 3
+    copy = pltpu.make_async_copy(wins, window, sems.at[0])
+    copy.start()
+    back_masks(id_col, id_row, own_hide, rim_hide, rows)
+    probs[...] = jnp.zeros_like(probs)
+    scored[...] = jnp.zeros_like(scored)
+    heads_apart(grads_in, grads)
+    copy.wait()
+
+    def body(h, carry):
+        def store(part, first, count, value):
+            apart[part, h, pl.ds(first, count)] = value.astype(jnp.bfloat16)
+
+        back_head(
+            h, window.at[0, h], window.at[1, h], window.at[2, h], grads.at[h], stats, own_hide,
+            rim_hide, probs, scored, store,
+        )
+        return carry
+
+    lax.fori_loop(0, HEADS, body, 0)
+    triple_store(apart, triple, triple_a, triple_b)
+    sums[...] = column_sum(triple[...].astype(jnp.float32))
+
+
+def attend_back(wins, grads_in, stats, id_col, id_row):
+    span = wins.shape[2]
+    rows = span // 3
+    features = HEADS * HEAD_DIM
+    low = jnp.bfloat16
+    return pl.pallas_call(
+        attend_back_kernel,
+        out_shape=(
+            jax.ShapeDtypeStruct((rows, 3 * features), low),
+            jax.ShapeDtypeStruct((2, 1, rows, 1024), low),
+            jax.ShapeDtypeStruct((2, 1, rows, 768), low),
+            jax.ShapeDtypeStruct((1, 3 * features), jnp.float32),
+        ),
+        in_specs=[anywhere(), whole(), whole(), whole(), whole()],
+        out_specs=(whole(), whole(), whole(), whole()),
+        scratch_shapes=[
+            pltpu.VMEM((3, HEADS, span, LANES), low),
+            pltpu.VMEM((HEADS, span, LANES), low),
+            pltpu.VMEM((rows // LANES, LANES, span - rows + LANES), jnp.float32),
+            pltpu.VMEM((2 * rows // LANES, LANES, rows), jnp.float32),
+            pltpu.VMEM((span, rows), low),
+            pltpu.VMEM((span, rows), low),
+            pltpu.VMEM((3, HEADS, rows, LANES), low),
+            pltpu.SemaphoreType.DMA((1,)),
+        ],
+        compiler_params=params(),
+        name="attend_back",
+    )(wins, grads_in, stats, id_col, id_row)
+
+
+def stream_back_kernel(
+    triple, weight, stream, middle_grad, gain, skip_weight, tok_grad, skip_grad, stream_grad,
+    by_core, sums, held, held_skip, grad, sems,
+):
+    features = stream.shape[1]
+    low = jnp.bfloat16
+    copies = [
+        pltpu.make_async_copy(weight.at[:, pl.ds(features * p, features)], held.at[p], sems.at[p])
+        for p in range(3)
+    ]
+    copies += [
+        pltpu.make_async_copy(
+            skip_weight.at[pl.ds(features * p, features)], held_skip.at[p], sems.at[3 + p]
+        )
+        for p in range(2)
+    ]
+    for copy in copies:
+        copy.start()
+    unit, scale = row_norm(stream[...])
+    for p in range(3):
+        copies[p].wait()
+        part = dot_nt(triple[:, features * p : features * (p + 1)], held[p])
+        if p == 0:
+            grad[...] = part
+        else:
+            grad[...] += part
+    cotangent = grad[...]
+    sums[0:1] = column_sum(cotangent * unit)
+    sums[1:2] = column_sum(cotangent)
+    whole_grad = middle_grad[...] + norm_back(
+        unit, scale, gain[...].astype(jnp.float32), cotangent
+    )
+    rounded = whole_grad.astype(low)
+    stream_grad[...] = rounded
+    by_core_store(by_core, rounded)
+    sums[2:3] = column_sum(rounded.astype(jnp.float32))
+    for p, out in enumerate((tok_grad, skip_grad)):
+        copies[3 + p].wait()
+        out[...] = dot_nt(rounded, held_skip[p]).astype(low)
+
+
+def stream_back(triple, weight, stream, middle_grad, gain, skip_weight):
+    rows, features = stream.shape
+    low = jnp.bfloat16
+    return pl.pallas_call(
+        stream_back_kernel,
+        out_shape=(
+            jax.ShapeDtypeStruct((rows, features), low),
+            jax.ShapeDtypeStruct((rows, features), low),
+            jax.ShapeDtypeStruct((rows, features), low),
+            jax.ShapeDtypeStruct((2, 1, rows, 768), low),
+            jax.ShapeDtypeStruct((8, features), jnp.float32),
+        ),
+        in_specs=[whole(), anywhere(), whole(), whole(), whole(), anywhere()],
+        out_specs=(whole(), whole(), whole(), whole(), whole()),
+        scratch_shapes=[
+            pltpu.VMEM((3, features, features), low),
+            pltpu.VMEM((2, features, features), low),
+            pltpu.VMEM((rows, features), jnp.float32),
+            pltpu.SemaphoreType.DMA((5,)),
+        ],
+        compiler_params=params(),
+        name="stream_back",
+    )(triple, weight, stream, middle_grad, gain[None], skip_weight)
 
 
 class Unit:
@@ -612,68 +1110,53 @@
     return dict(zip([*GRADS, "vec"], found[:6]))
 
 
-def by_core(value):
-    rows = value.shape[0]
-    cut = value.reshape(rows, 2, 2, 288).transpose(2, 0, 1, 3)
-    main = cut[..., :256].reshape(2, rows, 512)
-    rest = jnp.pad(cut[..., 256:], ((0, 0), (0, 0), (0, 0), (0, 96))).reshape(2, rows, 256)
-    return jnp.concatenate([main, rest], axis=-1)[:, None]
-
-
-def by_core_wide(value, cuts):
-    rows, total = value.shape
-    cut = value.reshape(rows, 2, 2, total // 4).transpose(2, 0, 1, 3)
-    found = []
-    for first, width, pieces in cuts:
-        part = cut[..., first : first + width * pieces]
-        short = width * pieces - part.shape[-1]
-        if short:
-            part = jnp.pad(part, ((0, 0), (0, 0), (0, 0), (0, short)))
-        part = part.reshape(2, rows, 2, pieces, width).transpose(0, 3, 1, 2, 4)
-        found.append(part.reshape(2, pieces, rows, 2 * width))
-    return found
-
-
-PAIRS = (
-    ("joined", "stream"),
-    ("normed", "triple"),
-    ("mixed", "branch"),
-    ("second", "hidden"),
-    ("active", "upstream"),
-)
+def unsplit(value):
+    blocks = []
+    for b in range(4):
+        x, c = b // 2, b % 2
+        blocks.append(value[c, 0, :, 256 * x : 256 * x + 256])
+        blocks.append(value[c, 0, :, 512 + LANES * x : 544 + LANES * x])
+    return jnp.concatenate(blocks, axis=1)
+
+
+def outer_sum(left, right):
+    return dot_tn(left, right)
 
 
 def summed(lefts, rights, vector_list):
-    local_parts = []
-    for left, right in PAIRS:
-        rows = lax.all_gather(lefts[left], "batch", axis=0, tiled=True)
-        columns = lax.all_to_all(rights[right], "batch", split_axis=1, concat_axis=0, tiled=True)
-        local_parts.append(outer_sum(rows, columns))
-    weight_parts = jax.tree.map(
-        lambda part: part.astype(jnp.float32),
-        lax.psum_scatter(shortened(tuple(local_parts)), "seq", scatter_dimension=0, tiled=True),
-    )
+    hidden = rights["hidden"]
+    _, pieces, rows, width = hidden.shape
+    hidden = hidden.reshape(2, pieces, rows, 2, width // 2).transpose(2, 3, 0, 1, 4)
+    columns_of = dict(
+        joined=unsplit(rights["stream"]),
+        normed=rights["triple"],
+        mixed=unsplit(rights["branch"]),
+        second=hidden.reshape(rows, -1),
+        active=unsplit(rights["upstream"]),
+    )
+    parts = []
+    for name in ("joined", "normed", "mixed", "second", "active"):
+        gathered = lax.all_gather(lefts[name], "batch", axis=0, tiled=True)
+        columns = lax.all_to_all(
+            columns_of[name], "batch", split_axis=1, concat_axis=0, tiled=True
+        )
+        parts.append(outer_sum(gathered, columns).astype(jnp.bfloat16))
+    parts = lax.psum_scatter(tuple(parts), "seq", scatter_dimension=0, tiled=True)
     vectors = tuple(
         lax.psum_scatter(vector, ("seq", "batch"), scatter_dimension=0, tiled=True)
         for vector in vector_list
     )
-    return weight_parts, vectors
-
-
-def summed_by_kernel(lefts, rights, vector_list):
-    triple_a, triple_b = by_core_wide(rights["triple"], ((0, 512, 1), (512, 384, 1)))
-    pieces = dict(
-        upstream=by_core(rights["upstream"]),
-        hidden=by_core_wide(rights["hidden"], ((0, 384, 3),))[0],
-        branch=by_core(rights["branch"]),
-        triple_a=triple_a,
-        triple_b=triple_b,
-        stream=by_core(rights["stream"]),
-    )
+    return tuple(part.astype(jnp.float32) for part in parts), vectors
+
+
+def pack_vectors(vector_list):
     vec = jnp.concatenate([vector.reshape(32, -1) for vector in vector_list], axis=1)
     vec = jnp.pad(vec, ((0, 0), (0, 512 - vec.shape[1]))).reshape(4, 2, 2, 2, 4, LANES)
-    vec = vec.transpose(3, 2, 1, 0, 4, 5)
-    found = weight_sums(lefts, pieces, vec)
+    return vec.transpose(3, 2, 1, 0, 4, 5)
+
+
+def summed_by_kernel(lefts, rights, vector_list):
+    found = weight_sums(lefts, rights, pack_vectors(vector_list))
     flat = found["vec"].reshape(-1)
     vectors, at = [], 0
     for vector in vector_list:
@@ -688,6 +1171,16 @@
         found["shrink"],
     )
     return weight_parts, tuple(vectors)
+
+
+def rims(value, width):
+    size = lax.axis_size("seq")
+    up = [(i, i + 1) for i in range(size - 1)]
+    down = [(j, i) for i, j in up]
+    return (
+        lax.ppermute(value[-width:], "seq", up),
+        lax.ppermute(value[:width], "seq", down),
+    )
 
 
 def on_device(
@@ -710,127 +1203,65 @@
     shrink_weight,
     shrink_bias,
 ):
-    groups, shard_rows, features = tokens.shape
-    head_dim = features // HEADS
-    blocks = 4
-    row_count = groups * shard_rows
-    flat_tokens = tokens.reshape(row_count, features)
-    flat_skip = skip_tokens.reshape(row_count, features)
-    flat_upstream = upstream.reshape(row_count, features)
-    joined = jnp.concatenate([flat_tokens, flat_skip], axis=1)
-    stream = matmul(joined, skip_weight) + skip_bias.astype(jnp.float32)
-    normed_full, first_back = jax.vjp(
-        normalize, stream, first_gain.astype(jnp.float32), first_shift.astype(jnp.float32)
-    )
-    normed = normed_full.astype(jnp.bfloat16)
-    triple = matmul(normed, attn_weight)
-    bias_full = attn_bias.astype(jnp.float32)
-    query_low = (triple[:, :features] + bias_full[:features]).astype(jnp.bfloat16)
-    key_low = triple[:, features : 2 * features].astype(jnp.bfloat16)
-    value_low = (triple[:, 2 * features :] + bias_full[features:]).astype(jnp.bfloat16)
-    rim_rows = min(shard_rows, (ITEM_MOST + 6) // 8 * 8)
-    stacked = jnp.stack([key_low, value_low]).reshape(2, groups, shard_rows, features)
-    widened = padded(stacked, (("seq", 2),), rim_rows)
+    _, rows, features = tokens.shape
+    rim = (ITEM_MOST - 1 + 15) // 16 * 16
+    tok, skp, above = tokens[0], skip_tokens[0], upstream[0]
     position = lax.axis_index("seq")
-    padded_ids = jnp.pad(segment_ids, ((0, 0), (rim_rows, rim_rows)), constant_values=-1)
-    key_ids = lax.dynamic_slice_in_dim(
-        padded_ids, position * shard_rows, shard_rows + 2 * rim_rows, 1
-    )
-    query_ids = lax.dynamic_slice_in_dim(segment_ids, position * shard_rows, shard_rows, 1)
-    query_items = to_items(query_low.reshape(groups, shard_rows, features), blocks)
-    key_items = to_items(widened[0], blocks)
-    value_items = to_items(widened[1], blocks)
-    query_id_items = jnp.repeat(query_ids, blocks, axis=0)
-    key_id_items = jnp.repeat(key_ids, blocks, axis=0)
-    mixed_items, lse_items = lax.map(
-        partial(forward_block, head_dim=head_dim),
-        (query_items, key_items, value_items, query_id_items, key_id_items),
-    )
-    mixed = from_items(mixed_items, blocks).reshape(row_count, features).astype(jnp.bfloat16)
-    middle = stream + matmul(mixed, proj_weight) + proj_bias.astype(jnp.float32)
-    second_full, second_back = jax.vjp(
-        normalize, middle, second_gain.astype(jnp.float32), second_shift.astype(jnp.float32)
-    )
-    second = second_full.astype(jnp.bfloat16)
-    hidden = matmul(second, expand_weight) + expand_bias.astype(jnp.float32)
-    active_full, gelu_back = jax.vjp(partial(jax.nn.gelu, approximate=False), hidden)
-    active = active_full.astype(jnp.bfloat16)
-    result = (middle + matmul(active, shrink_weight) + shrink_bias.astype(jnp.float32)).astype(
-        jnp.bfloat16
-    )
-    active_grad = matmul(flat_upstream, shrink_weight.T)
-    shrink_bias_grad = jnp.sum(flat_upstream, axis=0, dtype=jnp.float32)
-    hidden_grad = gelu_back(active_grad)[0].astype(jnp.bfloat16)
-    expand_bias_grad = jnp.sum(hidden_grad, axis=0, dtype=jnp.float32)
-    second_grad = matmul(hidden_grad, expand_weight.T)
-    middle_norm_grad, second_gain_grad, second_shift_grad = second_back(second_grad)
-    middle_grad = flat_upstream.astype(jnp.float32) + middle_norm_grad
-    branch_grad = middle_grad.astype(jnp.bfloat16)
-    proj_bias_grad = jnp.sum(branch_grad, axis=0, dtype=jnp.float32)
-    mixed_grad = matmul(branch_grad, proj_weight.T).astype(jnp.bfloat16)
-    grad_items = to_items(mixed_grad.reshape(groups, shard_rows, features), blocks)
-    query_grads, key_grads, value_grads = lax.map(
-        partial(backward_block, head_dim=head_dim),
-        (query_items, key_items, value_items, query_id_items, key_id_items, grad_items, lse_items),
-    )
-    query_grad = from_items(query_grads, blocks).reshape(row_count, features).astype(jnp.bfloat16)
-    window_grad = jnp.stack([from_items(key_grads, blocks), from_items(value_grads, blocks)])
-    rim_grads = jnp.concatenate(
-        [window_grad[:, :, :rim_rows], window_grad[:, :, shard_rows + rim_rows :]], axis=2
-    )
-    returned = padded(rim_grads.astype(jnp.bfloat16), (("seq", 2),), rim_rows).astype(
-        rim_grads.dtype
-    )
-    owned = window_grad[:, :, rim_rows : rim_rows + shard_rows]
-    owned = owned + jnp.pad(
-        returned[:, :, :rim_rows], ((0, 0), (0, 0), (0, shard_rows - rim_rows), (0, 0))
-    )
-    owned = owned + jnp.pad(
-        returned[:, :, 3 * rim_rows :], ((0, 0), (0, 0), (shard_rows - rim_rows, 0), (0, 0))
-    )
-    key_grad = owned[0].reshape(row_count, features).astype(jnp.bfloat16)
-    value_grad = owned[1].reshape(row_count, features).astype(jnp.bfloat16)
-    triple_grad = jnp.concatenate([query_grad, key_grad, value_grad], axis=1)
-    attn_bias_grad = jnp.concatenate(
-        [
-            jnp.sum(query_grad, axis=0, dtype=jnp.float32),
-            jnp.sum(value_grad, axis=0, dtype=jnp.float32),
-        ]
-    )
-    normed_grad = matmul(triple_grad, attn_weight.T)
-    stream_norm_grad, first_gain_grad, first_shift_grad = first_back(normed_grad)
-    stream_grad = (middle_grad + stream_norm_grad).astype(jnp.bfloat16)
-    skip_bias_grad = jnp.sum(stream_grad, axis=0, dtype=jnp.float32)
-    skip_full = matmul(stream_grad, skip_weight.T)
-    tokens_grad = skip_full[:, :features].astype(jnp.bfloat16)
-    skip_grad = skip_full[:, features:].astype(jnp.bfloat16)
+    padded_ids = jnp.pad(segment_ids[0], (rows, rows), constant_values=-1)
+    window_ids = lax.dynamic_slice_in_dim(padded_ids, position * rows, 3 * rows, 0)
+    id_row, id_col = window_ids[None, :], window_ids[:, None]
+
+    stream, normed = stream_norm(tok, skp, skip_weight, skip_bias, first_gain, first_shift)
+    before, after = rims(normed, rim)
+    own = own_heads(normed, attn_weight, attn_bias)
+    wins, mixed, lse = attend(own, before, after, attn_weight, attn_bias, id_col, id_row)
+    (
+        result, active, hidden_by_core, second, branch, branch_by_core, up_by_core, middle_grad,
+        mixed_grad, hidden_sum, sums,
+    ) = layer(
+        stream, mixed, lse, above,
+        (
+            proj_weight, proj_bias, second_gain, second_shift, expand_weight, expand_bias,
+            shrink_weight, shrink_bias,
+        ),
+    )
+    before, after = rims(mixed_grad, rim)
+    blank = jnp.zeros((rows - rim, mixed_grad.shape[1]), mixed_grad.dtype)
+    grad_window = jnp.concatenate([blank, before, mixed_grad, after, blank], axis=0)
+    stats = grad_window[:, features:].astype(jnp.float32)
+    triple, triple_a, triple_b, triple_sum = attend_back(wins, grad_window, stats, id_col, id_row)
+    tok_grad, skip_grad, stream_grad, stream_by_core, stream_sums = stream_back(
+        triple, attn_weight, stream, middle_grad, first_gain, skip_weight
+    )
     vector_list = (
-        skip_bias_grad,
-        first_gain_grad,
-        first_shift_grad,
-        attn_bias_grad,
-        proj_bias_grad,
-        second_gain_grad,
-        second_shift_grad,
-        expand_bias_grad,
-        shrink_bias_grad,
-    )
+        stream_sums[2],
+        stream_sums[0],
+        stream_sums[1],
+        jnp.concatenate([triple_sum[0, :features], triple_sum[0, 2 * features :]]),
+        sums[0],
+        sums[1],
+        sums[2],
+        hidden_sum[0],
+        sums[3],
+    )
+    joined = jnp.concatenate([tok, skp], axis=1)
     lefts = dict(active=active, second=second, mixed=mixed, normed=normed, joined=joined)
     rights = dict(
-        upstream=flat_upstream,
-        hidden=hidden_grad,
-        branch=branch_grad,
-        triple=triple_grad,
-        stream=stream_grad,
+        upstream=up_by_core,
+        hidden=hidden_by_core,
+        branch=branch_by_core,
+        triple_a=triple_a,
+        triple_b=triple_b,
+        stream=stream_by_core,
     )
     if lax.axis_size("seq") == 8 and lax.axis_size("batch") == 4:
         weight_parts, vectors = summed_by_kernel(lefts, rights, vector_list)
     else:
-        weight_parts, vectors = summed(lefts, rights, vector_list)
+        weight_parts, vectors = summed(lefts, dict(rights, triple=triple), vector_list)
     return (
-        result.reshape(groups, shard_rows, features),
-        tokens_grad.reshape(groups, shard_rows, features),
-        skip_grad.reshape(groups, shard_rows, features),
+        result[None],
+        tok_grad[None],
+        skip_grad[None],
         weight_parts[0],
         vectors[0],
         vectors[1],

time: 639 us -> 443 us (0.69)
  local copies, waits for them, and re-layouts: 205 us -> 34.7 us
  Pallas kernels: 187 us -> 337 us
  matrix products: 122 us -> 0 us
  other arithmetic: 59.5 us -> 3.2 us
  waiting for transfers between devices: 37.1 us -> 48 us
    pallas_call x0 -> x6, Pallas kernels: none -> 149 us  [the longest x1 44.5 us: attend_back(): pl.pallas_call(attend_back_kernel, out_shape=(jax.ShapeDtypeStruct((rows,...]
    dot_general x38 -> x0, matrix products: 122 us -> none  [the longest x10 83.7 us: matmul(): return jnp.dot(operand, other_op, preferred_element_type=jnp.float32)]
    reshape x22 -> x2, local copies, waits for them, and re-layouts: 35.2 us -> 0.67 us  [pack_vectors(): jnp.pad(vec, ((0, 0), (0, 512 - vec.shape[1])))]
    slice x20 -> x5, local copies, waits for them, and re-layouts: 40.2 us -> 6.06 us  [the longest x2 4.35 us: rims(): value[:width]]
    dynamic_slice x42 -> x1, local copies, waits for them, and re-layouts: 29.7 us -> 0.08 us  [on_device(): lax.dynamic_slice_in_dim(padded_ids, position * rows, 3 * rows, 0)]
    convert_element_type x16 -> x1, other arithmetic: 16.4 us -> 1.81 us  [on_device(): stats = grad_window[:, features:].astype(jnp.float32)]
    concatenate x5 -> x4, local copies, waits for them, and re-layouts: 14.2 us -> 0.93 us  [the longest x1 0.66 us: on_device(): jnp.concatenate([blank, before, mixed_grad, after, blank], axis=0)]
    dynamic_update_slice x12 -> x0, local copies, waits for them, and re-layouts: 13.2 us -> none  [the longest x4 7.47 us: on_device(): lax.map(partial(backward_block, head_dim=head_dim), (query_items, key_ite...]
  transfers between devices with their start and end apart: 4 -> 4, of which waited for: 3 -> 2; matrix products, arithmetic and copies ran while one was open for 15% -> 2% of each run, Pallas kernels for 0% -> 2%
where the time goes in v1:
time: 443 us; the launch traced here: 437 us
  Pallas kernels  337 us (76%)
  waiting for transfers between devices  48 us (11%)
  local copies, waits for them, and re-layouts  34.7 us (8%)
  starting transfers between devices  12.7 us (3%)
    pallas_call x1, Pallas kernels, weight_sums(): pl.pallas_call(kernel, out_shape=out_shape, in_specs=in_specs, out_specs=...  188 us
    ppermute x2, waiting for transfers between devices, rims(): lax.ppermute(value[-width:], 'seq', up)  48 us
    pallas_call x1, Pallas kernels, attend_back(): pl.pallas_call(attend_back_kernel, out_shape=(jax.ShapeDtypeStruct((rows,...  44.5 us
    pallas_call x1, Pallas kernels, layer(): pl.pallas_call(layer_kernel, grid=(4,), in_specs=[held(narrow), held(narr...  37.9 us
    pallas_call x1, Pallas kernels, attend(): pl.pallas_call(attend_kernel, out_shape=(jax.ShapeDtypeStruct((3, HEADS,...  34.3 us
    pallas_call x1, Pallas kernels, stream_back(): pl.pallas_call(stream_back_kernel, out_shape=(jax.ShapeDtypeStruct((rows,...  14.5 us
    unnamed x41, local copies, waits for them, and re-layouts  13 us
    pallas_call x1, Pallas kernels, own_heads(): pl.pallas_call(project_kernel, out_shape=jax.ShapeDtypeStruct((3, HEADS,...  9.96 us
  transfers between devices with their start and end apart: 4, of which 2 were waited for; matrix products, arithmetic and copies ran while one was open for 2% of the time, Pallas kernels for 2%

profile of v1, /device:TPU:0, one launch (start us, length us, event | category | flops | bytes accessed | tf_op | source)
XLA Modules:
  0.0 437.2 jit_solution(1096901738903909962)
XLA Ops:
  0.7 1.3 broadcast_in_dim.48.gain
  1.9 1.3 broadcast_in_dim.47.bias
  3.2 1.3 broadcast_in_dim.49.shift
  4.5 8.0 %stream_norm.1 = (f32[384,1152]{1,0:T(8,128)}, bf16[384,1152]{1,0:T(8,128)(2,1)}) custom-call(bf16[384,1152]{1,0:T(8,128)(2,1)} %bitcast.12, bf16[384,1152]{1,0:T(8,128)(2,1)} %bitcast.14, bf16[2304,1152]{1,0:T(8,128)(2,1)} %skip_weight.1, bf16[1,1152]{1,0:T(2,128)(2,1)} %broadcast_in_dim.47.bias, bf16[1,1152]{1,0:T(2,128)(2,1)} %broadcast_in_dim.48.gain, ...), custom_call_target="tpu_custom_call" | custom-call | flops 2038431744 | bytes 10000000 | tf_op jit(solution)/shard_map/stream_norm/pallas_call | solution.py:101
  12.6 1.5 fusion.1
  14.1 4.9 %collective-permute-start = (bf16[336,1152]{1,0:T(8,128)(2,1)S(1)}, bf16[336,1152]{1,0:T(8,128)(2,1)S(1)}, u32[]{:S(2)}, u32[]{:S(2)}) collective-permute-start(bf16[336,1152]{1,0:T(8,128)(2,1)S(1)} %get-tuple-element.121), channel_id=1, source_target_pairs={{0,4},{4,8},{8,12},{12,16},{16,20},{20,24},{24,28},{1,5},{5,9},{9,... | collective-permute-start | bytes 2322440 | tf_op jit(solution)/shard_map/ppermute | solution.py:1181
  19.0 1.8 collective-permute-start.1
  20.9 1.0 broadcast_in_dim.62.id_col
  21.9 0.6 broadcast_in_dim.52.id_row
  22.5 0.6 broadcast_in_dim.50.bias
  23.1 0.6 broadcast_in_dim.56.expand_bias
  23.7 0.6 broadcast_in_dim.53.proj_bias
  24.3 0.6 broadcast_in_dim.54.gain
  24.9 0.6 broadcast_in_dim.55.shift
  25.5 0.6 broadcast_in_dim.57.shrink_bias
  26.1 10.0 %own_heads.1.own = bf16[3,16,384,128]{3,2,1,0:T(8,128)(2,1)} custom-call(bf16[384,1152]{1,0:T(8,128)(2,1)} %get-tuple-element.47.normed.refs_3_, bf16[1152,3456]{1,0:T(8,128)(2,1)} %weight.7, bf16[1,2304]{1,0:T(2,128)(2,1)} %broadcast_in_dim.50.bias), custom_call_target="tpu_custom_call" | custom-call | flops 3057647616 | bytes 20000000 | tf_op jit(solution)/shard_map/own_heads/pallas_call | solution.py:169
  36.1 16.0 %collective-permute-done.before = bf16[336,1152]{1,0:T(8,128)(2,1)S(1)} collective-permute-done((bf16[336,1152]{1,0:T(8,128)(2,1)S(1)}, bf16[336,1152]{1,0:T(8,128)(2,1)S(1)}, u32[]{:S(2)}, u32[]{:S(2)}) %collective-permute-start) | collective-permute-done | bytes 774176 | tf_op jit(solution)/shard_map/ppermute | solution.py:1181
  52.1 0.9 copy-done.3
  52.9 0.9 copy-done.4
  53.8 34.3 %attend.1 = (bf16[3,16,1152,128]{3,2,1,0:T(8,128)(2,1)}, bf16[384,1152]{1,0:T(8,128)(2,1)}, f32[384,128]{1,0:T(8,128)}) custom-call(bf16[3,16,384,128]{3,2,1,0:T(8,128)(2,1)} %own_heads.1.own, bf16[336,1152]{1,0:T(8,128)(2,1)} %copy-done.3, bf16[336,1152]{1,0:T(8,128)(2,1)} %copy-done.4, bf16[1152,3456]{1,0:T(8,128)(2,1)} %weight.7, ...), custom_call_target="tpu_custom_call" | custom-call | tf_op jit(solution)/shard_map/attend/pallas_call | solution.py:257
  88.1 37.9 %layer.1 = (bf16[384,1152]{1,0:T(8,128)(2,1)}, bf16[384,4608]{1,0:T(8,128)(2,1)}, bf16[2,3,384,768]{3,2,1,0:T(8,128)(2,1)}, bf16[384,1152]{1,0:T(8,128)(2,1)}, b...) custom-call(f32[384,1152]{1,0:T(8,128)} %get-tuple-element.46.stream, ...), custom_call_target="tpu_custom_call" | custom-call | tf_op jit(solution)/shard_map/layer/pallas_call | solution.py:374
  126.1 2.8 fusion
  128.9 4.6 %collective-permute-start.2 = (bf16[336,1280]{1,0:T(8,128)(2,1)}, bf16[336,1280]{1,0:T(8,128)(2,1)S(1)}, u32[]{:S(2)}, u32[]{:S(2)}) collective-permute-start(bf16[336,1280]{1,0:T(8,128)(2,1)} %get-tuple-element.119), channel_id=1, source_target_pairs={{0,4},{4,8},{8,12},{12,16},{16,20},{20,24},{24,28},{1,5},{5,9},{9,... | collective-permute-start | bytes 2580488 | tf_op jit(solution)/shard_map/ppermute | solution.py:1181
  133.5 1.3 pad_maximum_fusion.refs_4_
  134.9 1.5 collective-permute-start.3
  136.4 0.7 broadcast_dynamic-update-slice_fusion
  137.1 0.1 reshape_squeeze.27
  137.6 32.1 %collective-permute-done.2 = bf16[336,1280]{1,0:T(8,128)(2,1)S(1)} collective-permute-done((bf16[336,1280]{1,0:T(8,128)(2,1)}, bf16[336,1280]{1,0:T(8,128)(2,1)S(1)}, u32[]{:S(2)}, u32[]{:S(2)}) %collective-permute-start.2) | collective-permute-done | bytes 860192 | tf_op jit(solution)/shard_map/ppermute | solution.py:1181
  169.7 1.0 constant_dynamic-update-slice_fusion.2
  170.7 1.0 constant_dynamic-update-slice_fusion.1
  171.7 1.0 constant_dynamic-update-slice_fusion
  172.7 0.7 broadcast_dynamic-update-slice_fusion.1.grads_in
  173.4 1.8 slice_convert_fusion.stats
  175.2 44.5 %attend_back.1 = (bf16[384,3456]{1,0:T(8,128)(2,1)}, bf16[2,1,384,1024]{3,2,1,0:T(8,128)(2,1)}, bf16[2,1,384,768]{3,2,1,0:T(8,128)(2,1)}, f32[1,3456]{1,0:T(1,128)}) custom-call(bf16[3,16,1152,128]{3,2,1,0:T(8,128)(2,1)} %get-tuple-element.51.wins, bf16[1152,1280]{1,0:T(8,128)(2,1)} %broadcast_dynamic-update-slice_fusion.1.grads_in, ...), custom_call_target="tpu_custom_call" | custom-call | tf_op jit(solution)/shard_map/attend_back/pallas_call | solution.py:533
  219.7 0.7 slice_reduce_fusion.5
  220.6 14.5 %stream_back.1 = (bf16[384,1152]{1,0:T(8,128)(2,1)}, bf16[384,1152]{1,0:T(8,128)(2,1)}, bf16[384,1152]{1,0:T(8,128)(2,1)}, bf16[2,1,384,768]{3,2,1,0:T(8,128)(2,1)}, f32[8,1152]{1,0:T(8,128)}) custom-call(bf16[384,3456]{1,0:T(8,128)(2,1)} %get-tuple-element.53.triple, bf16[1152,3456]{1,0:T(8,128)(2,1)} %weight.7, f32[384,1152]{1,0:T(8,128)} %get-tuple-element.46.stream, ...), custom_call_target="tpu_custom_call" | custom-call | tf_op jit(solution)/shard_map/stream_back/pallas_call | solution.py:602
  235.2 0.9 slice_reduce_fusion.6
  236.4 0.1 concatenate.22
  236.6 0.6 copy.41
  237.2 188.1 %weight_sums.1 = (f32[576,288]{1,0:T(8,128)}, f32[144,1152]{1,0:T(8,128)}, f32[144,288]{1,0:T(8,128)}, f32[144,896]{1,0:T(8,128)}, f32[288,288]{1,0:T(8,128)}, /...) custom-call(bf16[384,4608]{1,0:T(8,128)(2,1)} %get-tuple-element.57., ...), custom_call_target="tpu_custom_call" | custom-call | tf_op jit(solution)/shard_map/weight_sums/pallas_call | solution.py:1099
  425.4 1.5 fusion.2
  426.9 1.3 slice.94
  428.2 1.3 slice.90
  429.5 2.3 copy.39
  431.8 1.8 copy.50
  433.6 1.9 copy.51
  435.5 0.7 copy.52
  436.2 0.8 copy.53
  (47 shorter events, 1.1 us)
Async XLA Ops:
  12.5 8.3 %copy-start.8 = (s32[1,3072]{1,0:T(1,128)S(1)}, s32[1,3072]{1,0:T(1,128)}, u32[]{:S(2)}) copy-start(s32[1,3072]{1,0:T(1,128)} %param.20) | copy-start | bytes 36868
  12.5 10.0 %copy-start.11 = (bf16[2304]{0:T(1024)(128)(2,1)S(1)}, bf16[2304]{0:T(1024)(128)(2,1)}, u32[]{:S(2)}) copy-start(bf16[2304]{0:T(1024)(128)(2,1)} %param.27) | copy-start | bytes 13828
  12.5 10.6 %copy-start.9 = (bf16[4608]{0:T(1024)(128)(2,1)S(1)}, bf16[4608]{0:T(1024)(128)(2,1)}, u32[]{:S(2)}) copy-start(bf16[4608]{0:T(1024)(128)(2,1)} %param.33) | copy-start | bytes 27652
  12.5 11.2 %copy-start.12 = (bf16[1152]{0:T(1024)(128)(2,1)S(1)}, bf16[1152]{0:T(1024)(128)(2,1)}, u32[]{:S(2)}) copy-start(bf16[1152]{0:T(1024)(128)(2,1)} %param.29) | copy-start | bytes 6916
  12.5 11.8 %copy-start.13 = (bf16[1152]{0:T(1024)(128)(2,1)S(1)}, bf16[1152]{0:T(1024)(128)(2,1)}, u32[]{:S(2)}) copy-start(bf16[1152]{0:T(1024)(128)(2,1)} %param.30) | copy-start | bytes 6916
  12.5 12.4 %copy-start.14 = (bf16[1152]{0:T(1024)(128)(2,1)S(1)}, bf16[1152]{0:T(1024)(128)(2,1)}, u32[]{:S(2)}) copy-start(bf16[1152]{0:T(1024)(128)(2,1)} %param.31) | copy-start | bytes 6916
  12.5 13.0 %copy-start.15 = (bf16[1152]{0:T(1024)(128)(2,1)S(1)}, bf16[1152]{0:T(1024)(128)(2,1)}, u32[]{:S(2)}) copy-start(bf16[1152]{0:T(1024)(128)(2,1)} %param.35) | copy-start | bytes 6916
  14.1 38.0 %collective-permute-start = (bf16[336,1152]{1,0:T(8,128)(2,1)S(1)}, bf16[336,1152]{1,0:T(8,128)(2,1)S(1)}, u32[]{:S(2)}, u32[]{:S(2)}) collective-permute-start(bf16[336,1152]{1,0:T(8,128)(2,1)S(1)} %get-tuple-element.121), channel_id=1, source_target_pairs={{0,4},{4,8},{8,12},{12,16},{16,20},{20,24},{24,28},{1,5},{5,9},{9,... | collective-permute-start | bytes 2322440 | tf_op jit(solution)/shard_map/ppermute | solution.py:1181
  19.0 33.1 %collective-permute-start.1 = (bf16[336,1152]{1,0:T(8,128)(2,1)S(1)}, bf16[336,1152]{1,0:T(8,128)(2,1)S(1)}, u32[]{:S(2)}, u32[]{:S(2)}) collective-permute-start(bf16[336,1152]{1,0:T(8,128)(2,1)S(1)} %get-tuple-element.120), channel_id=1, source_target_pairs={{4,0},{8,4},{12,8},{16,12},{20,16},{24,20},{28,24},{5,1},{9,5},{13... | collective-permute-start | bytes 2322440 | tf_op jit(solution)/shard_map/ppermute | solution.py:1182
  52.1 0.9 copy-start.3
  52.9 0.9 copy-start.4
  126.1 7.5 %copy-start.1 = (bf16[1,384,1152]{2,1,0:T(8,128)(2,1)S(1)}, bf16[1,384,1152]{2,1,0:T(8,128)(2,1)}, u32[]{:S(2)}) copy-start(bf16[1,384,1152]{2,1,0:T(8,128)(2,1)} %param.18) | copy-start | bytes 2654212
  126.1 7.5 %copy-start.2 = (bf16[1,384,1152]{2,1,0:T(8,128)(2,1)S(1)}, bf16[1,384,1152]{2,1,0:T(8,128)(2,1)}, u32[]{:S(2)}) copy-start(bf16[1,384,1152]{2,1,0:T(8,128)(2,1)} %param.19) | copy-start | bytes 2654212
  126.1 10.9 %copy-start.10 = (f32[8,1152]{1,0:T(8,128)S(1)}, f32[8,1152]{1,0:T(8,128)}, u32[]{:S(2)}) copy-start(f32[8,1152]{1,0:T(8,128)} %get-tuple-element.67) | copy-start | bytes 110596
  126.1 11.4 %copy-start.7 = (f32[1,4608]{1,0:T(1,128)S(1)}, f32[1,4608]{1,0:T(1,128)}, u32[]{:S(2)}) copy-start(f32[1,4608]{1,0:T(1,128)} %get-tuple-element.68) | copy-start | bytes 55300
  128.9 41.7 %copy-start = (bf16[384,1280]{1,0:T(8,128)(2,1)S(1)}, bf16[384,1280]{1,0:T(8,128)(2,1)}, u32[]{:S(2)}) copy-start(bf16[384,1280]{1,0:T(8,128)(2,1)} %get-tuple-element.52) | copy-start | bytes 2949124
  128.9 40.8 %collective-permute-start.2 = (bf16[336,1280]{1,0:T(8,128)(2,1)}, bf16[336,1280]{1,0:T(8,128)(2,1)S(1)}, u32[]{:S(2)}, u32[]{:S(2)}) collective-permute-start(bf16[336,1280]{1,0:T(8,128)(2,1)} %get-tuple-element.119), channel_id=1, source_target_pairs={{0,4},{4,8},{8,12},{12,16},{16,20},{20,24},{24,28},{1,5},{5,9},{9,... | collective-permute-start | bytes 2580488 | tf_op jit(solution)/shard_map/ppermute | solution.py:1181
  134.9 36.9 %collective-permute-start.3 = (bf16[336,1280]{1,0:T(8,128)(2,1)}, bf16[336,1280]{1,0:T(8,128)(2,1)S(1)}, u32[]{:S(2)}, u32[]{:S(2)}) collective-permute-start(bf16[336,1280]{1,0:T(8,128)(2,1)} %get-tuple-element.118), channel_id=1, source_target_pairs={{4,0},{8,4},{12,8},{16,12},{20,16},{24,20},{28,24},{5,1},{9,5},{13... | collective-permute-start | bytes 2580488 | tf_op jit(solution)/shard_map/ppermute | solution.py:1182
  425.4 10.1 %copy-start.6 = (f32[144,288]{1,0:T(8,128)S(1)}, f32[144,288]{1,0:T(8,128)}, u32[]{:S(2)}) copy-start(f32[144,288]{1,0:T(8,128)} %get-tuple-element.155) | copy-start | bytes 497668
  425.4 10.8 %copy-start.5 = (f32[144,1152]{1,0:T(8,128)S(1)}, f32[144,1152]{1,0:T(8,128)}, u32[]{:S(2)}) copy-start(f32[144,1152]{1,0:T(8,128)} %get-tuple-element.159) | copy-start | bytes 1990660

commit v2 on v1

--- a/solution.py
+++ b/solution.py
@@ -11,6 +11,7 @@
 LANES = 128
 MESH = pl.DeviceIdType.MESH
 SCALE2 = HEAD_DIM**-0.5 * 1.4426950408889634
+VMEM_MOST = 60 * 2**20
 
 
 ROOT2 = 2.0**0.5
@@ -419,7 +420,7 @@
 
     def hidden(first, keys, width):
         same = id_col[first : first + LANES] == id_row[:, keys : keys + width]
-        return jnp.where(same, 0.0, HIDE)
+        return jnp.where(same, 0.0, HIDE).astype(own_hide.dtype)
 
     for i in range(blocks):
         own_hide[i] = hidden(rows + i * LANES, i * LANES, reach)
@@ -446,7 +447,7 @@
 
     def pair(q_at, k_at, width, hide):
         q_rows, k_rows = pl.ds(q_at, LANES), pl.ds(k_at, width)
-        exponent = dot_nt(queries[q_rows], keys[k_rows]) * SCALE2 + hide
+        exponent = dot_nt(queries[q_rows], keys[k_rows]) * SCALE2 + hide.astype(jnp.float32)
         weight = jnp.exp2(exponent)
         scored = weight * dot_nt(grads[q_rows], values[k_rows])
         return weight.astype(low), scored.astype(low)
@@ -481,23 +482,16 @@
         out[h] = head_tile(value[:, : HEADS * HEAD_DIM], h, False)
 
 
-def triple_store(apart, triple, triple_a, triple_b):
+def triple_store(apart, triple):
     features = HEADS * HEAD_DIM
-    rows = apart.shape[2]
     for p in range(3):
         for h in range(HEADS):
             at = features * p + HEAD_DIM * h
             triple[:, at : at + HEAD_DIM] = apart[p, h, :, :HEAD_DIM]
-    for b in range(4):
-        x, c = b // 2, b % 2
-        value = triple[:, 864 * b : 864 * (b + 1)]
-        triple_a[c, 0, :, 512 * x : 512 * (x + 1)] = value[:, :512]
-        rest = jnp.concatenate([value[:, 512:], jnp.zeros((rows, 32), value.dtype)], axis=1)
-        triple_b[c, 0, :, 384 * x : 384 * (x + 1)] = rest
 
 
 def attend_back_kernel(
-    wins, grads_in, stats, id_col, id_row, triple, triple_a, triple_b, sums,
+    wins, grads_in, stats, id_col, id_row, triple, sums,
     window, grads, own_hide, rim_hide, probs, scored, apart, sems,
 ):
     span = window.shape[2]
@@ -521,7 +515,7 @@
         return carry
 
     lax.fori_loop(0, HEADS, body, 0)
-    triple_store(apart, triple, triple_a, triple_b)
+    triple_store(apart, triple)
     sums[...] = column_sum(triple[...].astype(jnp.float32))
 
 
@@ -534,17 +528,15 @@
         attend_back_kernel,
         out_shape=(
             jax.ShapeDtypeStruct((rows, 3 * features), low),
-            jax.ShapeDtypeStruct((2, 1, rows, 1024), low),
-            jax.ShapeDtypeStruct((2, 1, rows, 768), low),
             jax.ShapeDtypeStruct((1, 3 * features), jnp.float32),
         ),
         in_specs=[anywhere(), whole(), whole(), whole(), whole()],
-        out_specs=(whole(), whole(), whole(), whole()),
+        out_specs=(whole(), whole()),
         scratch_shapes=[
             pltpu.VMEM((3, HEADS, span, LANES), low),
             pltpu.VMEM((HEADS, span, LANES), low),
-            pltpu.VMEM((rows // LANES, LANES, span - rows + LANES), jnp.float32),
-            pltpu.VMEM((2 * rows // LANES, LANES, rows), jnp.float32),
+            pltpu.VMEM((rows // LANES, LANES, span - rows + LANES), low),
+            pltpu.VMEM((2 * rows // LANES, LANES, rows), low),
             pltpu.VMEM((span, rows), low),
             pltpu.VMEM((span, rows), low),
             pltpu.VMEM((3, HEADS, rows, LANES), low),
@@ -556,8 +548,7 @@
 
 
 def stream_back_kernel(
-    triple, weight, stream, middle_grad, gain, skip_weight, tok_grad, skip_grad, stream_grad,
-    by_core, sums, held, held_skip, grad, sems,
+    triple, weight, stream, middle_grad, gain, skip_weight, tok_grad, skip_grad, by_core, sums, held, held_skip, grad, sems,
 ):
     features = stream.shape[1]
     low = jnp.bfloat16
@@ -588,7 +579,6 @@
         unit, scale, gain[...].astype(jnp.float32), cotangent
     )
     rounded = whole_grad.astype(low)
-    stream_grad[...] = rounded
     by_core_store(by_core, rounded)
     sums[2:3] = column_sum(rounded.astype(jnp.float32))
     for p, out in enumerate((tok_grad, skip_grad)):
@@ -604,12 +594,11 @@
         out_shape=(
             jax.ShapeDtypeStruct((rows, features), low),
             jax.ShapeDtypeStruct((rows, features), low),
-            jax.ShapeDtypeStruct((rows, features), low),
             jax.ShapeDtypeStruct((2, 1, rows, 768), low),
             jax.ShapeDtypeStruct((8, features), jnp.float32),
         ),
         in_specs=[whole(), anywhere(), whole(), whole(), whole(), anywhere()],
-        out_specs=(whole(), whole(), whole(), whole(), whole()),
+        out_specs=(whole(), whole(), whole(), whole()),
         scratch_shapes=[
             pltpu.VMEM((3, features, features), low),
             pltpu.VMEM((2, features, features), low),
@@ -621,87 +610,81 @@
     )(triple, weight, stream, middle_grad, gain[None], skip_weight)
 
 
+ROWS = 144
+THIRD = ROWS // 3
+
+
 class Unit:
-    def __init__(self, left, left_at, right, right_at, tiles, rows, blocks, out, out_at):
+    def __init__(self, left, left_at, right, right_at, tiles, blocks, out, out_at):
         self.left, self.left_at = left, left_at
         self.right, self.right_at = right, right_at
         self.tiles = tiles
-        self.rows = rows
         self.blocks = blocks
-        self.places = 1 + max(block[3] for block in blocks)
         self.out, self.out_at = out, out_at
-
-    def shape(self, *lead):
-        if self.tiles:
-            return (*lead, self.rows, LANES)
-        return (*lead, self.rows * 7 // 3, LANES)
-
-    @property
-    def x_size(self):
-        return 2 * (self.tiles or 1)
-
-    @property
-    def part_shape(self):
-        return self.shape(2, self.x_size, 2, self.places)
-
-    @property
-    def first_shapes(self):
-        half = self.x_size // 2
-        if self.tiles:
-            return (self.shape(half, 2, self.places), self.shape(2 * half, self.places))
-        return (self.shape(2, self.places), self.shape(2, self.places))
-
-    @property
-    def second_shape(self):
-        if self.tiles:
-            return self.shape(self.tiles, self.places)
-        return self.shape(self.places)
-
-    @property
-    def chain_shape(self):
-        return self.shape(self.tiles) if self.tiles else self.shape()
-
-    def view(self, ref, order, x, y, place=None):
-        if x is None:
-            x_at = slice(None)
-        elif self.tiles:
-            x_at = pl.ds(x * self.tiles, self.tiles)
-        else:
-            x_at = x
-        y_at = slice(None) if y is None else y
-        if place is None:
-            return ref.at[order, x_at, y_at]
-        return ref.at[order, x_at, y_at, place]
-
-    def chains(self):
-        return sorted({(order, place, z) for _, order, _, place, z in self.blocks})
+        self.rows = ROWS * tiles if tiles else 2 * ROWS + THIRD
+        self.z_of = {(order, place): z for _, order, _, place, z in blocks}
+
+
+ORDER_OF = (0, 1, 1, 0)
+QUARTERS = tuple(
+    ((2 * z + y) * ROWS, ORDER_OF[z], y, z // 2, z) for z in range(4) for y in range(2)
+)
 
 
 def make_units():
-    order_of = (0, 1, 1, 0)
-    place_of = (0, 0, 1, 1)
-    quarter = [
-        ((2 * z + y) * 144, order_of[z], y, place_of[z], z) for z in range(4) for y in range(2)
-    ]
-    units = []
-    for z in (0, 3, 1, 2):
-        blocks = [(y * 576 + h * 288, h, y, 0, z) for y in range(2) for h in range(2)]
-        units.append(Unit("active", z * 1152, "upstream", 0, 0, 288, blocks, "shrink", z))
+    units = {}
+    for z in range(4):
+        blocks = [
+            (y * 576 + q * ROWS, q // 2, y, q % 2, z) for y in range(2) for q in range(4)
+        ]
+        units[f"shrink{z}"] = Unit("active", z * 1152, "upstream", 0, 0, blocks, "shrink", 0)
     for j in range(3):
-        units.append(Unit("second", 0, "hidden", j, 3, 144, quarter, "expand", j * 3))
-    units.append(Unit("mixed", 0, "branch", 0, 0, 144, quarter, "proj", 0))
-    units.append(Unit("normed", 0, "triple_a", 0, 4, 144, quarter, "attn", 0))
-    units.append(Unit("normed", 0, "triple_b", 0, 3, 144, quarter, "attn", 4))
-    for k in range(2):
-        blocks = [(h * 576 + y * 288, h, y, 0, 2 * k + h) for h in range(2) for y in range(2)]
-        units.append(Unit("joined", k * 1152, "stream", 0, 0, 288, blocks, "skip", k))
+        units[f"expand{j}"] = Unit("second", 0, "hidden", j, 3, QUARTERS, "expand", 3 * j)
+    units["proj"] = Unit("mixed", 0, "branch", 0, 0, QUARTERS, "proj", 0)
+    for j, (first, tiles) in enumerate(TRIPLE_TILES):
+        units[f"attn{j}"] = Unit("normed", 0, f"triple{j}", 0, tiles, QUARTERS, "attn", first)
+    for k, name in enumerate(("tok", "skp")):
+        blocks = [
+            (h * 576 + y * 288 + i * ROWS, h, y, i, 2 * k + h)
+            for h in range(2)
+            for y in range(2)
+            for i in range(2)
+        ]
+        units[f"skip{k}"] = Unit(name, 0, "stream_cols", 0, 0, blocks, "skip", 0)
     return units
 
 
-LEFTS = ("active", "second", "mixed", "normed", "joined")
-RIGHTS = ("upstream", "hidden", "branch", "triple_a", "triple_b", "stream")
-GRADS = ("shrink", "expand", "proj", "attn", "skip")
-GRAD_SHAPES = ((576, 288), (144, 1152), (144, 288), (144, 896), (288, 288))
+TRIPLE_TILES = ((0, 3), (3, 2), (5, 2))
+GRADS = (
+    ("shrink", (576, 288)),
+    ("expand", (144, 1152)),
+    ("proj", (144, 288)),
+    ("attn", (144, 896)),
+    ("skip", (288, 288)),
+)
+PART_SLOTS, FIRST_SLOTS, SECOND_SLOTS, LAST_SLOTS = 4, 4, 4, 5
+LINE_FIRST = ("expand0",)
+X_FIRST = ("shrink0", "shrink1", "shrink2", "shrink3")
+
+PLAN = (
+    "start shrink0", "start expand0", "start shrink3", "start shrink1", "start shrink2",
+    "line expand0 1 0", "line expand0 1 1", "line expand0 1 2", "second shrink0", "line expand0 2 0",
+    "second shrink3", "line expand0 2 1", "line expand0 3 0", "halo", "heads 4", "line_end expand0",
+    "second shrink1", "third shrink0", "start expand1", "third shrink3", "start expand2",
+    "hop shrink0 2", "heads 2", "hop shrink3 2", "second shrink2", "hop shrink0 3", "third shrink1",
+    "start proj", "line_x expand0", "heads 2", "hop shrink3 3", "hop shrink1 2", "hop shrink1 3",
+    "finish shrink0", "heads 2", "second expand1", "heads 2", "second expand2", "finish shrink3",
+    "finish shrink1", "third shrink2", "heads 2", "line_y expand0", "second proj", "hop shrink2 2",
+    "hop shrink2 3", "heads 2", "pack", "start attn0", "finish shrink2", "third expand1", "start attn1",
+    "hop expand1 2", "third expand2", "start attn2", "hop expand1 3", "back 0", "hop expand2 2",
+    "second attn0", "back 1", "hop expand2 3", "finish expand1", "back 2", "second attn1", "norm",
+    "vec 0", "second attn2", "vec 1", "finish expand2", "third proj", "start skip0", "hop proj 2",
+    "third attn0", "start skip1", "hop proj 3", "hop attn0 2", "out 0", "vec 2", "out 1", "hop attn0 3",
+    "out 2", "third attn1", "hop attn1 2", "finish proj", "second skip0", "third attn2", "hop attn1 3",
+    "hop attn2 2", "hop attn2 3", "finish attn0", "vec 3", "second skip1", "finish attn1", "third skip0",
+    "hop skip0 2", "finish attn2", "vec 4", "hop skip0 3", "third skip1", "hop skip1 2", "hop skip1 3",
+    "finish skip0", "vec 5", "finish skip1",
+)
 
 
 def add_into(target, other):
@@ -710,125 +693,187 @@
     )
 
 
-class Links:
-    def __init__(self):
-        self.ids = {}
-
-    def id(self, key):
-        return self.ids.setdefault(key, len(self.ids))
-
-
-def sum_kernel(units, names, *refs):
-    r = dict(zip(names, refs))
+def gradient_kernel(r):
     seq, batch = lax.axis_index("seq"), lax.axis_index("batch")
     z, y = seq // 2, seq % 2
     x, c = batch // 2, batch % 2
-    partner = (seq, 2 * x + (1 - c))
-    x_side = (seq, 2 * (1 - x) + c)
-    y_side = (2 * z + (1 - y), batch)
-    above = (2 * jnp.minimum(z + 1, 3) + y, batch)
-    below = (2 * jnp.maximum(z - 1, 0) + y, batch)
-    links = Links()
-
-    barrier = pltpu.get_barrier_semaphore()
-    for device in (partner, x_side, y_side):
-        pl.semaphore_signal(barrier, 1, device_id=device, device_id_type=MESH)
-
-    @pl.when(z < 3)
-    def _():
-        pl.semaphore_signal(barrier, 1, device_id=above, device_id_type=MESH)
-
-    @pl.when(z > 0)
-    def _():
-        pl.semaphore_signal(barrier, 1, device_id=below, device_id_type=MESH)
-
-    pl.semaphore_wait(barrier, 3 + (z < 3).astype(jnp.int32) + (z > 0).astype(jnp.int32))
-
-    def remote(key, src, dst, device):
-        i = links.id(key)
+    at = {
+        "core": (seq, 2 * x + (1 - c)),
+        "x": (seq, 2 * (1 - x) + c),
+        "y": (2 * z + (1 - y), batch),
+        "above": (2 * jnp.minimum(z + 1, 3) + y, batch),
+        "below": (2 * jnp.maximum(z - 1, 0) + y, batch),
+        "far": (2 * ((z + 2) % 4) + y, batch),
+        "next": (jnp.minimum(seq + 1, 7), batch),
+        "last": (jnp.maximum(seq - 1, 0), batch),
+    }
+    at["pair"] = (2 * (z + 1 - 2 * (z % 2)) + y, batch)
+    units = make_units()
+    low = jnp.bfloat16
+    rows, features = r["tok"].shape
+    ids = {}
+
+    def remote(key, src, dst, side):
+        i = ids.setdefault(key, len(ids))
         return pltpu.make_async_remote_copy(
             src_ref=src,
             dst_ref=dst,
             send_sem=r["sent"].at[i],
             recv_sem=r["came"].at[i],
-            device_id=device,
+            device_id=at[side],
             device_id_type=MESH,
         )
 
+    barrier = pltpu.get_barrier_semaphore()
+
+    def greet(side):
+        pl.semaphore_signal(barrier, 1, device_id=at[side], device_id_type=MESH)
+
+    for side in ("core", "x", "y", "far"):
+        greet(side)
+    for side, some in (
+        ("above", z < 3),
+        ("below", z > 0),
+        ("next", (y == 1) & (z < 3)),
+        ("last", (y == 0) & (z > 0)),
+    ):
+        pl.when(some)(lambda side=side: greet(side))
+    more = (z < 3).astype(jnp.int32) + (z > 0).astype(jnp.int32)
+    diagonal = jnp.where(y == 1, (z < 3).astype(jnp.int32), (z > 0).astype(jnp.int32))
+    pl.semaphore_wait(barrier, 4 + more + diagonal)
+
+    rim = (ITEM_MOST - 1 + 15) // 16 * 16
+    window = r["window"]
+    halo_up = remote(
+        "halo_up", r["grads"].at[pl.ds(rows - rim, rim)], window.at[pl.ds(rows - rim, rim)], "next"
+    )
+    halo_down = remote(
+        "halo_down", r["grads"].at[pl.ds(0, rim)], window.at[pl.ds(2 * rows, rim)], "last"
+    )
+    pl.when(seq < 7)(halo_up.start)
+    pl.when(seq > 0)(halo_down.start)
+
     swaps = {}
-    for unit in units:
-        key = ("left", unit.left, unit.left_at)
-        if key not in swaps:
-            at = pl.ds(unit.left_at, 1152)
-            swaps[key] = remote(
-                key, r[unit.left].at[:, at], r["far_" + unit.left].at[:, at], partner
+
+    def swap(side, name, first):
+        key = (side, name, first)
+        if key in swaps:
+            return
+        if side == "left":
+            cols = pl.ds(first, features)
+            src, dst = r[name].at[:, cols], r["far_" + name].at[:, cols]
+        else:
+            src, dst = r[name].at[1 - c, first], r["far_" + name].at[first]
+        swaps[key] = remote(key, src, dst, "core")
+        swaps[key].start()
+
+    def swap_unit(name):
+        unit = units[name]
+        swap("left", unit.left, unit.left_at)
+        swap("right", unit.right, unit.right_at)
+
+    order = [step.split()[1] for step in PLAN if step.startswith("start ")]
+    for name in order:
+        unit = units[name]
+        swap("left", unit.left, unit.left_at)
+        if not unit.right.startswith(("triple", "stream")):
+            swap("right", unit.right, unit.right_at)
+
+    slots, loads, here = {}, {}, set()
+
+    def load(side, name, first, busy=None):
+        key = (side, name, first)
+        if key in slots:
+            return
+        slot = 1 - slots.get(busy, 1)
+        for other in [k for k in slots if k[0] == side and slots[k] == slot]:
+            del slots[other]
+        slots[key] = slot
+        if key not in here:
+            swaps[key].wait_recv()
+            here.add(key)
+        if side == "left":
+            cols = pl.ds(first, features)
+            near, far = r[name].at[:, cols], r["far_" + name].at[:, cols]
+            hold = r["lefts"].at[slot]
+        else:
+            near, far = r[name].at[c, first], r["far_" + name].at[first]
+            hold = r["rights"].at[slot, :, pl.ds(0, near.shape[-1])]
+        loads[key] = []
+        for half, src in ((0, near), (1, far)):
+            copy = pltpu.make_async_copy(
+                src, hold.at[pl.ds(rows * half, rows)], r[side + "_sem"].at[slot, half]
             )
-        key = ("right", unit.right, unit.right_at)
-        if key not in swaps:
-            swaps[key] = remote(
-                key,
-                r[unit.right].at[1 - c, unit.right_at],
-                r["far_" + unit.right].at[unit.right_at],
-                partner,
+            copy.start()
+            loads[key].append(copy)
+
+    def keys_of(name):
+        unit = units[name]
+        return ("left", unit.left, unit.left_at), ("right", unit.right, unit.right_at)
+
+    started = [name for name in order if name not in LINE_FIRST]
+    both = slice(None)
+
+    def axes(u, order):
+        return ("x", "y") if order == 0 or started[u] in X_FIRST else ("y", "x")
+
+    def credit(stage, order, side):
+        return r["credit"].at[(stage * 2 + order) * 2 + ("x", "y").index(side)]
+
+    def take_credit(u, stage, order):
+        if u >= (FIRST_SLOTS, SECOND_SLOTS)[stage]:
+            pl.semaphore_wait(credit(stage, order, axes(u, order)[stage]), 1)
+
+    def give_credit(u, stage, order):
+        then = u + (FIRST_SLOTS, SECOND_SLOTS)[stage]
+        if then < len(started):
+            side = axes(then, order)[stage]
+            pl.semaphore_signal(
+                credit(stage, order, side), 1, device_id=at[side], device_id_type=MESH
             )
-    for copy in swaps.values():
-        copy.start()
-
-    slots = {}
-    turns = {"left": 0, "right": 0}
-
-    def load(unit):
-        started = []
-        for side, name, at in (
-            ("left", unit.left, unit.left_at),
-            ("right", unit.right, unit.right_at),
-        ):
-            key = (side, name, at)
-            if key in slots:
-                continue
-            slot = turns[side] % 2
-            turns[side] += 1
-            slots[key] = slot
-            swaps[key].wait_recv()
-            if side == "left":
-                cols = pl.ds(at, 1152)
-                near, far = r[name].at[:, cols], r["far_" + name].at[:, cols]
-                hold = r["lefts"].at[slot]
-            else:
-                near, far = r[name].at[c, at], r["far_" + name].at[at]
-                hold = r["rights"].at[slot, :, pl.ds(0, near.shape[-1])]
-            for half, src in ((0, near), (1, far)):
-                copy = pltpu.make_async_copy(
-                    src, hold.at[pl.ds(384 * half, 384)], r[side + "_sem"].at[slot, half]
-                )
-                copy.start()
-                started.append(copy)
-        return started
-
-    def compute(u):
-        unit = units[u]
-        part = r["part", u]
-        left = r["lefts"].at[slots["left", unit.left, unit.left_at]]
-        right = r["rights"].at[slots["right", unit.right, unit.right_at]]
+
+    def part_of(u, order, *index):
+        unit = units[started[u]]
+        place = (pl.ds(0, 2), pl.ds(0, unit.rows)) if len(index) < 3 else (pl.ds(0, unit.rows),)
+        return r["part"].at[(u % PART_SLOTS, order, *index, *place)]
+
+    def moved(u, order, stage):
+        land = r["land_one"] if stage == 0 else r["land_two"]
+        land = land.at[u % (FIRST_SLOTS, SECOND_SLOTS)[stage], order]
+        height = pl.ds(0, units[started[u]].rows)
+        if stage == 1:
+            send = (x, 1 - y) if axes(u, order)[1] == "y" else (1 - x, y)
+            return part_of(u, order, *send), part_of(u, order, x, y), land.at[:, height]
+        if axes(u, order)[0] == "x":
+            send, keep = (1 - x, both), (x, both)
+        else:
+            send, keep = (both, 1 - y), (both, y)
+        return part_of(u, order, *send), part_of(u, order, *keep), land.at[:, :, height]
+
+    def stage_copy(u, order, stage):
+        send, _, land = moved(u, order, stage)
+        return remote((u, stage, order), send, land, axes(u, order)[stage])
+
+    def compute(name, part, slot):
+        unit = units[name]
+        left_key, right_key = keys_of(name)
+        left, right = r["lefts"].at[slots[left_key]], r["rights"].at[slots[right_key]]
 
         def product(n):
             cols = pl.ds(pl.multiple_of(n * 256, 256), 256)
-            return lax.dot_general(
-                left[...],
-                right[:, cols],
-                (((0,), (0,)), ((), ())),
-                preferred_element_type=jnp.float32,
-            )
-
-        rows = unit.rows
+            return dot_tn(left[...], right[:, cols])
+
         if unit.tiles:
 
             def body(n, carry):
-                tile = product(n).astype(jnp.bfloat16)
-                for first, order, y_at, place, _ in unit.blocks:
-                    for i in range(2):
-                        part[order, 2 * n + i, y_at, place] = tile[
-                            first : first + rows, i * LANES : (i + 1) * LANES
+                tile = product(n).astype(low)
+                for i in range(2):
+                    g = 2 * n + i
+                    x_at = g // unit.tiles
+                    t = pl.multiple_of((g - x_at * unit.tiles) * ROWS, 16)
+                    for first, order, y_at, place, _ in unit.blocks:
+                        part[slot, order, x_at, y_at, place, pl.ds(t, ROWS)] = tile[
+                            first : first + ROWS, i * LANES : (i + 1) * LANES
                         ]
                 return carry
 
@@ -836,265 +881,554 @@
             return
 
         def body(n, carry):
-            tile = product(n).astype(jnp.bfloat16)
+            tile = product(n).astype(low)
             for first, order, y_at, place, _ in unit.blocks:
                 for i in range(2):
-                    part[order, n, y_at, place, pl.ds(i * rows, rows)] = tile[
-                        first : first + rows, i * LANES : (i + 1) * LANES
+                    part[slot, order, n, y_at, place, pl.ds(i * ROWS, ROWS)] = tile[
+                        first : first + ROWS, i * LANES : (i + 1) * LANES
                     ]
             return carry
 
         lax.fori_loop(0, 2, body, 0)
         tile = product(2)
-        third = rows // 3
         for first, order, y_at, place, _ in unit.blocks:
             for x_at in range(2):
                 pieces = [
-                    tile[first + s * third : first + (s + 1) * third, x_at * LANES :][:, :32]
+                    tile[first + s * THIRD : first + (s + 1) * THIRD, x_at * LANES :][:, :32]
                     for s in range(3)
                 ]
                 packed = jnp.concatenate(pieces + [jnp.zeros_like(pieces[0])], axis=1)
-                part[order, x_at, y_at, place, pl.ds(2 * rows, third)] = packed.astype(jnp.bfloat16)
-
-    def first_copies(u):
-        unit, part = units[u], r["part", u]
+                part[slot, order, x_at, y_at, place, pl.ds(2 * ROWS, THIRD)] = packed.astype(low)
+
+    def wait_sends(u):
+        for order in range(2):
+            for stage in range(2):
+                stage_copy(u, order, stage).wait_send()
+
+    def fetch(name, ahead):
+        for key in keys_of(name):
+            load(*key)
+            for copy in loads.pop(key, ()):
+                copy.wait()
+        if ahead is not None and not ahead.startswith("skip"):
+            for key, busy in zip(keys_of(ahead), keys_of(name)):
+                if key in swaps:
+                    load(*key, busy)
+
+    def first_stage(u):
+        if u >= PART_SLOTS:
+            wait_sends(u - PART_SLOTS)
+        compute(started[u], r["part"], u % PART_SLOTS)
+        for order in range(2):
+            take_credit(u, 0, order)
+            stage_copy(u, order, 0).start()
+
+    def second_stage(u):
+        for order in range(2):
+            stage_copy(u, order, 0).wait_recv()
+            _, keep, land = moved(u, order, 0)
+            add_into(keep, land)
+            give_credit(u, 0, order)
+            take_credit(u, 1, order)
+            stage_copy(u, order, 1).start()
+
+    def last_ref(u, order, place):
+        return r["ends"].at[u % LAST_SLOTS, order, place, pl.ds(0, units[started[u]].rows)]
+
+    def third_stage(u):
+        if u >= LAST_SLOTS:
+            chain_sends(u - LAST_SLOTS)
+        for order in range(2):
+            stage_copy(u, order, 1).wait_recv()
+            _, keep, land = moved(u, order, 1)
+            for place in range(2):
+                value = keep.at[place][...].astype(jnp.float32)
+                value = value + land.at[place][...].astype(jnp.float32)
+                last_ref(u, order, place)[...] = value.astype(low)
+            give_credit(u, 1, order)
+
+    def chain_copy(u, order, place, up):
+        pool, i = r["chain_at"][started[u], order, place, up]
+        dst = r[pool].at[i, pl.ds(0, units[started[u]].rows)]
+        src = last_ref(u, order, place)
+        key = (u, "chain", order, place, up)
+        return remote(key, src, dst, "above" if up else "below"), dst
+
+    def hop(u, step):
+        for up, me in ((True, step - 1), (False, 4 - step)):
+            todo = [
+                key
+                for key, z_at in sorted(
+                    units[started[u]].z_of.items(), key=lambda item: -item[1] if up else item[1]
+                )
+                if ((z_at > me) if up else (z_at < me))
+            ]
+
+            @pl.when(z == me)
+            def _():
+                for order, place in todo:
+                    copy, land = chain_copy(u, order, place, up)
+                    if step > 1:
+                        copy.wait_recv()
+                        add_into(last_ref(u, order, place), land)
+                    copy.start()
+
+    def chain_sends(u):
+        for (order, place), z_at in units[started[u]].z_of.items():
+            for up, some in ((True, z_at > 0), (False, z_at < 3)):
+                if some:
+
+                    @pl.when((z < z_at) if up else (z > z_at))
+                    def _():
+                        chain_copy(u, order, place, up)[0].wait_send()
+
+    def finish(u):
+        unit = units[started[u]]
+        for (order, place), z_at in unit.z_of.items():
+
+            @pl.when(z == z_at)
+            def _():
+                value = last_ref(u, order, place)[...].astype(jnp.float32)
+                for up, have in ((True, z_at > 0), (False, z_at < 3)):
+                    if have:
+                        copy, land = chain_copy(u, order, place, up)
+                        copy.wait_recv()
+                        value = value + land[...].astype(jnp.float32)
+                store_out(unit, order, place, value)
+
+    def store_out(unit, order, place, value):
+        out = r["out_" + unit.out]
+        if unit.tiles:
+            for t in range(unit.tiles):
+                col = (unit.out_at + t) * LANES
+                out[:, col : col + LANES] = value[t * ROWS : (t + 1) * ROWS]
+            return
+        base = {"shrink": (2 * order + place) * ROWS, "proj": 0, "skip": place * ROWS}[unit.out]
+        for i in range(2):
+            out[base : base + ROWS, i * LANES : (i + 1) * LANES] = value[i * ROWS : (i + 1) * ROWS]
+        for s in range(3):
+            out[base + s * THIRD : base + (s + 1) * THIRD, 256:288] = value[
+                2 * ROWS : 2 * ROWS + THIRD, s * 32 : (s + 1) * 32
+            ]
+
+    def line_ref(name, order, place):
+        i = LINE_FIRST.index(name)
+        return r["line"].at[i, order, both, both, place, pl.ds(0, units[name].rows)]
+
+    def line_copy(name, order, place, up):
+        i = r["line_at"][name, order, place, up]
+        dst = r["line_land"].at[i, both, both, pl.ds(0, units[name].rows)]
+        key = (name, "line", order, place, up)
+        return remote(key, line_ref(name, order, place), dst, "above" if up else "below"), dst
+
+    def line_hop(name, step, turn):
+        for up, me in ((True, step - 1), (False, 4 - step)):
+            todo = [
+                key
+                for key, z_at in sorted(
+                    units[name].z_of.items(), key=lambda item: -item[1] if up else item[1]
+                )
+                if ((z_at > me) if up else (z_at < me))
+            ][turn : turn + 1]
+
+            @pl.when(z == me)
+            def _():
+                for order, place in todo:
+                    copy, land = line_copy(name, order, place, up)
+                    if step > 1:
+                        copy.wait_recv()
+                        add_into(line_ref(name, order, place), land)
+                    copy.start()
+
+    def line_copies(name):
+        i = LINE_FIRST.index(name)
+        height = pl.ds(0, units[name].rows)
+        own = r["line_own"].at[i]
         return (
-            remote(("first", u, 0), unit.view(part, 0, 1 - x, None), r["first", u, 0], x_side),
-            remote(("first", u, 1), unit.view(part, 1, None, 1 - y), r["first", u, 1], y_side),
-        )
-
-    def second_copies(u):
-        unit, part = units[u], r["part", u]
-        return (
-            remote(("second", u, 0), unit.view(part, 0, x, 1 - y), r["second", u].at[0], y_side),
-            remote(("second", u, 1), unit.view(part, 1, 1 - x, y), r["second", u].at[1], x_side),
-        )
-
-    def first_stage(u):
-        compute(u)
-        for copy in first_copies(u):
-            copy.start()
-
-    def second_stage(u):
-        unit, part = units[u], r["part", u]
-        keeps = (unit.view(part, 0, x, None), unit.view(part, 1, None, y))
-        for order, (copy, send) in enumerate(zip(first_copies(u), second_copies(u))):
-            copy.wait_recv()
-            add_into(keeps[order], r["first", u, order])
-            send.start()
-
-    def third_stage(u):
-        unit, part = units[u], r["part", u]
-        for order, copy in enumerate(second_copies(u)):
-            copy.wait_recv()
-            add_into(unit.view(part, order, x, y), r["second", u].at[order])
-
-    def chain_copy(key, src, dsts, up):
-        return remote((key, up), src, dsts[up], above if up else below)
-
-    class Chain:
-        def __init__(self, key, src, up_ref, down_ref, z_at):
-            self.key, self.src, self.z_at = key, src, z_at
-            self.refs = {True: up_ref, False: down_ref}
-
-        def copy(self, up):
-            return remote((self.key, up), self.src, self.refs[up], above if up else below)
-
-        def hop(self, step):
-            for up, me in ((True, step - 1), (False, 4 - step)):
-                if (self.z_at > me) if up else (self.z_at < me):
-
-                    @pl.when(z == me)
+            remote((name, "line_x"), own.at[1 - x, both, height], r["line_x"].at[i, both, height], "x"),
+            remote((name, "line_y"), own.at[x, 1 - y, height], r["line_y"].at[i, height], "y"),
+        )
+
+    def line_stage(name, stage):
+        i = LINE_FIRST.index(name)
+        unit = units[name]
+        height = pl.ds(0, unit.rows)
+        if stage == "end":
+            for (order, place), z_at in unit.z_of.items():
+
+                @pl.when(z == z_at)
+                def _():
+                    lands = []
+                    for up, have in ((True, z_at > 0), (False, z_at < 3)):
+                        if have:
+                            copy, land = line_copy(name, order, place, up)
+                            copy.wait_recv()
+                            lands.append(land)
+                    for x_at in range(2):
+                        for y_at in range(2):
+                            value = line_ref(name, order, place)[x_at, y_at].astype(jnp.float32)
+                            for land in lands:
+                                value = value + land[x_at, y_at].astype(jnp.float32)
+                            r["line_own"][i, x_at, y_at, height] = value.astype(low)
+
+            line_copies(name)[0].start()
+        elif stage == "x":
+            line_copies(name)[0].wait_recv()
+            add_into(r["line_own"].at[i, x, both, height], r["line_x"].at[i, both, height])
+            line_copies(name)[1].start()
+        else:
+            line_copies(name)[1].wait_recv()
+            value = r["line_own"][i, x, y, height].astype(jnp.float32)
+            value = value + r["line_y"][i, height].astype(jnp.float32)
+            store_out(unit, 0, 0, value)
+
+    def line_drain(name):
+        for (order, place), z_at in units[name].z_of.items():
+            for up, some in ((True, z_at > 0), (False, z_at < 3)):
+                if some:
+
+                    @pl.when((z < z_at) if up else (z > z_at))
                     def _():
-                        if step > 1:
-                            self.copy(up).wait_recv()
-                            add_into(self.src, self.refs[up])
-                        self.copy(up).start()
-
-        def total(self):
-            value = self.src[...].astype(jnp.float32)
-            for up, have in ((True, self.z_at > 0), (False, self.z_at < 3)):
-                if have:
-                    self.copy(up).wait_recv()
-                    value = value + self.refs[up][...].astype(jnp.float32)
-            return value
-
-        def drain(self):
-            for up, some in ((True, self.z_at > 0), (False, self.z_at < 3)):
-                if some:
-
-                    @pl.when((z < self.z_at) if up else (z > self.z_at))
-                    def _():
-                        self.copy(up).wait_send()
-
-    def unit_chains(u):
-        unit, part = units[u], r["part", u]
-        found = []
-        for order, place, z_at in unit.chains():
-            src = unit.view(part, order, x, y, place)
-            up = r["up", u, order, place] if z_at > 0 else None
-            down = r["down", u, order, place] if z_at < 3 else None
-            found.append((order, place, Chain(("chain", u, order, place), src, up, down, z_at)))
-        return found
-
-    def hop_stage(u, step):
-        for _, _, chain in unit_chains(u):
-            chain.hop(step)
-
-    def last_stage(u):
-        unit = units[u]
-        out = r["out_" + unit.out]
-        rows = unit.rows
-        for order, place, chain in unit_chains(u):
-
-            @pl.when(z == chain.z_at)
+                        line_copy(name, order, place, up)[0].wait_send()
+
+        for copy in line_copies(name):
+            copy.wait_send()
+
+    def head_load(h):
+        return pltpu.make_async_copy(
+            r["wins"].at[:, h], r["head"].at[h % 2], r["head_sem"].at[h % 2]
+        )
+
+    done = {"heads": 0}
+
+    def halo_work():
+        head_load(0).start()
+        own = pltpu.make_async_copy(r["grads"], window.at[pl.ds(rows, rows)], r["chunk_sem"].at[0])
+        own.start()
+        pad = rows - rim
+        blank = jnp.zeros((pad, window.shape[1]), low)
+        window[0:pad] = blank
+        window[3 * rows - pad :] = blank
+
+        @pl.when(seq == 0)
+        def _():
+            window[pad:rows] = jnp.zeros((rim, window.shape[1]), low)
+
+        @pl.when(seq == 7)
+        def _():
+            window[2 * rows : 2 * rows + rim] = jnp.zeros((rim, window.shape[1]), low)
+
+        back_masks(r["id_col"], r["id_row"], r["own_hide"], r["rim_hide"], rows)
+        r["probs"][...] = jnp.zeros(r["probs"].shape, low)
+        r["scored"][...] = jnp.zeros(r["scored"].shape, low)
+        own.wait()
+        pl.when(seq > 0)(halo_up.wait_recv)
+        pl.when(seq < 7)(halo_down.wait_recv)
+        r["stats"][...] = window[:, features:].astype(jnp.float32)
+
+    def heads_work(count):
+        first = done["heads"]
+        done["heads"] += count
+
+        def body(h, carry):
+            head_load(h).wait()
+
+            @pl.when(h + 1 < HEADS)
             def _():
-                value = chain.total()
-                if unit.tiles:
-                    for t in range(unit.tiles):
-                        at = (unit.out_at + t) * LANES
-                        out[:, at : at + LANES] = value[t]
-                    return
-                base = order * rows if rows == 288 and unit.out == "shrink" else 0
-                third = rows // 3
-                for i in range(2):
-                    out[base : base + rows, i * LANES : (i + 1) * LANES] = value[
-                        i * rows : (i + 1) * rows
-                    ]
-                for s in range(3):
-                    out[base + s * third : base + (s + 1) * third, 256:288] = value[
-                        2 * rows : 2 * rows + third, s * 32 : (s + 1) * 32
-                    ]
-
-    vec = r["vec"]
-
-    def vec_copies():
-        return (
-            remote("vec_core", vec.at[1 - c], r["vec_core"], partner),
-            remote("vec_x", vec.at[c, 1 - x], r["vec_x"], x_side),
-            remote("vec_y", vec.at[c, x, 1 - y], r["vec_y"], y_side),
-        )
-
-    vec_keeps = (vec.at[c], vec.at[c, x], vec.at[c, x, y])
-    vec_lands = (r["vec_core"], r["vec_x"], r["vec_y"])
-    vec_chains = [
-        Chain(("vec", b), vec.at[c, x, y, b], r["vec_up"].at[b], r["vec_down"].at[b], b)
-        for b in range(4)
-    ]
-
-    def vec_stage(step):
-        if step < 3:
-            if step > 0:
-                vec_copies()[step - 1].wait_recv()
-                add_into(vec_keeps[step - 1], vec_lands[step - 1])
-            vec_copies()[step].start()
-        elif step < 6:
-            if step == 3:
-                vec_copies()[2].wait_recv()
-                add_into(vec_keeps[2], vec_lands[2])
-            for chain in vec_chains:
-                chain.hop(step - 2)
-        elif step == 6:
-            for chain in vec_chains:
-
-                @pl.when(z == chain.z_at)
-                def _():
-                    r["out_vec"][...] = chain.total()
-
-    count = len(units)
-    started = load(units[0])
-    for tick in range(count + 6):
-        if tick < count:
-            for copy in started:
+                head_load(h + 1).start()
+
+            tile = (h * HEAD_DIM) // LANES
+            off = h * HEAD_DIM - tile * LANES
+            cols = pl.ds(pl.multiple_of(tile * LANES, LANES), 2 * LANES)
+            pair = pltpu.roll(window[:, cols].astype(jnp.float32), (2 * LANES - off) % (2 * LANES), 1)
+            lane = lanes_of((3 * rows, LANES))
+            r["grad_head"][...] = jnp.where(lane < HEAD_DIM, pair[:, :LANES], 0.0).astype(low)
+            wide = lanes_of((rows, 2 * LANES))
+            inside = (wide >= off) & (wide < off + HEAD_DIM)
+
+            def store(part, at_row, count, value):
+                rows_at = pl.ds(at_row, count)
+                old = r["triple"][part, rows_at, cols].astype(jnp.float32)
+                spread = jnp.concatenate([value, jnp.zeros_like(value)], axis=1)
+                moved = pltpu.roll(spread, off, 1)
+                r["triple"][part, rows_at, cols] = jnp.where(inside[:count], moved, old).astype(low)
+
+            head = r["head"].at[h % 2]
+            back_head(
+                h, head.at[0], head.at[1], head.at[2], r["grad_head"], r["stats"], r["own_hide"],
+                r["rim_hide"], r["probs"], r["scored"], store,
+            )
+            return carry
+
+        lax.fori_loop(first, first + count, body, 0)
+
+    sums = r["sums"]
+
+    def pack_work():
+        for p in range(3):
+            if p != 1:
+                row = 3 + p // 2
+                sums[row : row + 1] = column_sum(r["triple"][p, :, :features].astype(jnp.float32))
+        for b in range(4):
+            pieces = []
+            for p in range(3):
+                low_at, high_at = max(864 * b, features * p), min(864 * (b + 1), features * (p + 1))
+                if low_at < high_at:
+                    pieces.append(
+                        r["triple"][p, :, low_at - features * p : high_at - features * p]
+                    )
+            pieces.append(jnp.zeros((rows, 32), low))
+            value = jnp.concatenate(pieces, axis=1)
+            for j, (first, tiles) in enumerate(TRIPLE_TILES):
+                width = tiles * LANES
+                r[f"triple{j}"][b % 2, 0, :, width * (b // 2) : width * (b // 2 + 1)] = value[
+                    :, first * LANES : first * LANES + width
+                ]
+        for j in range(len(TRIPLE_TILES)):
+            swap("right", f"triple{j}", 0)
+
+    chunks = [(p, first, count) for p in range(3) for first, count in ((0, 768), (768, 384))]
+
+    def weight_load(i):
+        slot = i % 2
+        if i < 6:
+            p, first, count = chunks[i]
+            src = r["attn_weight"].at[pl.ds(first, count), pl.ds(features * p, features)]
+        else:
+            count = 768
+            src = r["skip_weight"].at[pl.ds(768 * (i - 6), 768)]
+        return pltpu.make_async_copy(
+            src, r["lefts"].at[slot, pl.ds(0, count)], r["weight_sem"].at[slot]
+        )
+
+    def back_work(p):
+        if p == 0:
+            weight_load(0).start()
+        for i in (2 * p, 2 * p + 1):
+            _, first, count = chunks[i]
+            weight_load(i).wait()
+            if i < 5:
+                weight_load(i + 1).start()
+            part = dot_nt(r["triple"][p, :, :features], r["lefts"][i % 2, :count])
+            cols = slice(first, first + count)
+            if p == 0:
+                r["normed_grad"][:, cols] = part
+            else:
+                r["normed_grad"][:, cols] += part
+
+    def norm_work():
+        gain = r["gain"][...].astype(jnp.float32)
+        sums[0:3] = jnp.zeros((3, features), jnp.float32)
+        chunk = r["chunk"]
+        for i in range(rows // LANES):
+            here = pl.ds(i * LANES, LANES)
+            copies = [
+                pltpu.make_async_copy(r[name].at[here], chunk.at[k], r["chunk_sem"].at[k])
+                for k, name in enumerate(("stream", "middle_grad"))
+            ]
+            for copy in copies:
+                copy.start()
+            for copy in copies:
                 copy.wait()
-            if tick + 1 < count:
-                started = load(units[tick + 1])
-            first_stage(tick)
-        vec_stage(tick)
-        if 0 <= tick - 1 < count:
-            second_stage(tick - 1)
-        if 0 <= tick - 2 < count:
-            third_stage(tick - 2)
-            hop_stage(tick - 2, 1)
-        if 0 <= tick - 3 < count:
-            hop_stage(tick - 3, 2)
-        if 0 <= tick - 4 < count:
-            hop_stage(tick - 4, 3)
-        if 0 <= tick - 5 < count:
-            last_stage(tick - 5)
+            unit, scale = row_norm(chunk[0])
+            cotangent = r["normed_grad"][here]
+            rounded = (chunk[1] + norm_back(unit, scale, gain, cotangent)).astype(low)
+            window[here, :features] = rounded
+            sums[0:1] += column_sum(rounded.astype(jnp.float32))
+            sums[1:2] += column_sum(cotangent * unit)
+            sums[2:3] += column_sum(cotangent)
+        by_core_store(r["stream_cols"], window[0:rows, :features])
+        swap("right", "stream_cols", 0)
+
+    def out_copies():
+        return [
+            pltpu.make_async_copy(
+                r["triple"].at[k, :, pl.ds(0, features)], r[name], r["chunk_sem"].at[k]
+            )
+            for k, name in enumerate(("out_tok", "out_skp"))
+        ]
+
+    def out_work(k):
+        i = 6 + k
+        if k == 0:
+            weight_load(i).start()
+        weight_load(i).wait()
+        if k < 2:
+            weight_load(i + 1).start()
+        value = dot_nt(window[0:rows, :features], r["lefts"][i % 2, :768]).astype(low)
+        for half in range(2):
+            base = features * half
+            first, last = max(768 * k, base), min(768 * (k + 1), base + features)
+            if first < last:
+                r["triple"][half, :, first - base : last - base] = value[
+                    :, first - 768 * k : last - 768 * k
+                ]
+        if k == 2:
+            for copy in out_copies():
+                copy.start()
+
+    sides = ("core", "x", "y", "pair", "far")
+
+    def vec_work(step):
+        vec, land = r["vec"], r["vec_land"]
+        if step == 0:
+            vec[0] = r["vec_in"][...]
+            vec[0, 0:5] = sums[0:5]
+        else:
+            remote(("vec", step - 1), vec.at[step - 1], land.at[step - 1], sides[step - 1]).wait_recv()
+            total = vec[step - 1] + land[step - 1]
+            if step == len(sides):
+                r["out_vec"][...] = total
+            else:
+                vec[step] = total
+        if step < len(sides):
+            remote(("vec", step), vec.at[step], land.at[step], sides[step]).start()
+
+    def start(name):
+        i = order.index(name)
+        fetch(name, order[i + 1] if i + 1 < len(order) else None)
+        if name in LINE_FIRST:
+            compute(name, r["line"], LINE_FIRST.index(name))
+        else:
+            first_stage(started.index(name))
+
+    def third(name):
+        third_stage(started.index(name))
+        hop(started.index(name), 1)
+
+    steps = {
+        "start": start,
+        "second": lambda name: second_stage(started.index(name)),
+        "third": third,
+        "hop": lambda name, step: hop(started.index(name), int(step)),
+        "finish": lambda name: finish(started.index(name)),
+        "line": lambda name, step, turn: line_hop(name, int(step), int(turn)),
+        "line_end": lambda name: line_stage(name, "end"),
+        "line_x": lambda name: line_stage(name, "x"),
+        "line_y": lambda name: line_stage(name, "y"),
+        "halo": halo_work,
+        "heads": lambda count: heads_work(int(count)),
+        "pack": pack_work,
+        "back": lambda p: back_work(int(p)),
+        "norm": norm_work,
+        "out": lambda k: out_work(int(k)),
+        "vec": lambda step: vec_work(int(step)),
+    }
+    for step in PLAN:
+        kind, *rest = step.split()
+        steps[kind](*rest)
+    for copy in out_copies():
+        copy.wait()
+    for name in LINE_FIRST:
+        line_drain(name)
     for copy in swaps.values():
         copy.wait_send()
-    for u in range(count):
-        for copy in first_copies(u) + second_copies(u):
-            copy.wait_send()
-        for _, _, chain in unit_chains(u):
-            chain.drain()
-    for copy in vec_copies():
-        copy.wait_send()
-    for chain in vec_chains:
-        chain.drain()
-
-
-def weight_sums(lefts, rights, vec):
-    units = make_units()
-    low = jnp.bfloat16
-    names, in_specs, operands = [], [], []
-    for name, value in [*lefts.items(), *rights.items()]:
+    count = len(started)
+    for u in range(max(0, count - PART_SLOTS), count):
+        wait_sends(u)
+    for u in range(max(0, count - LAST_SLOTS), count):
+        chain_sends(u)
+    for step in range(len(sides)):
+        remote(("vec", step), r["vec"].at[step], r["vec_land"].at[step], sides[step]).wait_send()
+    pl.when(seq < 7)(halo_up.wait_send)
+    pl.when(seq > 0)(halo_down.wait_send)
+
+
+def gradients(values, vec):
+    low, full = jnp.bfloat16, jnp.float32
+    rows, features = values["tok"].shape
+    names, operands, in_specs, out_shape, out_specs, scratch = [], [], [], [], [], []
+    held = ("id_col", "id_row", "gain")
+    for name, value in values.items():
         names.append(name)
-        in_specs.append(pl.BlockSpec(memory_space=pl.ANY))
         operands.append(value)
+        in_specs.append(whole() if name in held else anywhere())
     names.append("vec_in")
-    in_specs.append(pl.BlockSpec(memory_space=pltpu.VMEM))
     operands.append(vec)
-    out_shape, out_specs = [], []
-    for name, shape in zip(GRADS, GRAD_SHAPES):
-        names.append("out_" + name)
-        out_shape.append(jax.ShapeDtypeStruct(shape, jnp.float32))
-        out_specs.append(pl.BlockSpec(memory_space=pltpu.VMEM))
-    names.append("out_vec")
-    out_shape.append(jax.ShapeDtypeStruct((4, LANES), jnp.float32))
-    out_specs.append(pl.BlockSpec(memory_space=pltpu.VMEM))
-    for name in LEFTS:
-        names.append("far_" + name)
-        out_shape.append(jax.ShapeDtypeStruct(lefts[name].shape, low))
-        out_specs.append(pl.BlockSpec(memory_space=pl.ANY))
-    for name in RIGHTS:
-        names.append("far_" + name)
-        out_shape.append(jax.ShapeDtypeStruct(rights[name].shape[1:], low))
-        out_specs.append(pl.BlockSpec(memory_space=pl.ANY))
-    scratch = []
+    in_specs.append(whole())
+
+    def out(name, shape, dtype, spec):
+        names.append(name)
+        out_shape.append(jax.ShapeDtypeStruct(shape, dtype))
+        out_specs.append(spec)
+
+    for name, shape in GRADS:
+        out("out_" + name, shape, full, whole())
+    out("out_vec", vec.shape, full, whole())
+    out("out_tok", (rows, features), low, anywhere())
+    out("out_skp", (rows, features), low, anywhere())
+    for name in ("active", "second", "mixed", "normed", "tok", "skp"):
+        out("far_" + name, values[name].shape, low, anywhere())
+    for name in ("upstream", "hidden", "branch"):
+        out("far_" + name, values[name].shape[1:], low, anywhere())
+    cores = {f"triple{j}": 2 * LANES * tiles for j, (_, tiles) in enumerate(TRIPLE_TILES)}
+    cores["stream_cols"] = 768
+    for name, width in cores.items():
+        out("far_" + name, (1, rows, width), low, anywhere())
 
     def add(name, kind):
         names.append(name)
         scratch.append(kind)
 
-    add("lefts", pltpu.VMEM((2, 768, 1152), low))
-    add("rights", pltpu.VMEM((2, 768, 1024), low))
+    most = 3 * ROWS
+    for name, width in cores.items():
+        add(name, pltpu.VMEM((2, 1, rows, width), low))
+    add("lefts", pltpu.VMEM((2, 2 * rows, features), low))
+    add("rights", pltpu.VMEM((2, 2 * rows, 768), low))
     add("left_sem", pltpu.SemaphoreType.DMA((2, 2)))
     add("right_sem", pltpu.SemaphoreType.DMA((2, 2)))
-    for u, unit in enumerate(units):
-        add(("part", u), pltpu.VMEM(unit.part_shape, low))
-        for order in range(2):
-            add(("first", u, order), pltpu.VMEM(unit.first_shapes[order], low))
-        add(("second", u), pltpu.VMEM((2, *unit.second_shape), low))
-        for order, place, z_at in unit.chains():
-            if z_at > 0:
-                add(("up", u, order, place), pltpu.VMEM(unit.chain_shape, low))
-            if z_at < 3:
-                add(("down", u, order, place), pltpu.VMEM(unit.chain_shape, low))
-    add("vec", pltpu.VMEM(vec.shape, jnp.float32))
-    add("vec_core", pltpu.VMEM(vec.shape[1:], jnp.float32))
-    add("vec_x", pltpu.VMEM(vec.shape[2:], jnp.float32))
-    add("vec_y", pltpu.VMEM(vec.shape[3:], jnp.float32))
-    add("vec_up", pltpu.VMEM(vec.shape[3:], jnp.float32))
-    add("vec_down", pltpu.VMEM(vec.shape[3:], jnp.float32))
+    add("part", pltpu.VMEM((PART_SLOTS, 2, 2, 2, 2, most, LANES), low))
+    add("land_one", pltpu.VMEM((FIRST_SLOTS, 2, 2, 2, most, LANES), low))
+    add("land_two", pltpu.VMEM((SECOND_SLOTS, 2, 2, most, LANES), low))
+    add("ends", pltpu.VMEM((LAST_SLOTS, 2, 2, most, LANES), low))
+    chain_at, sizes = {}, {"chain_short": 0, "chain_long": 0}
+    for name, unit in make_units().items():
+        if name in LINE_FIRST:
+            continue
+        pool = "chain_short" if unit.rows <= 2 * ROWS + THIRD else "chain_long"
+        for (order, place), z_at in unit.z_of.items():
+            for up, have in ((True, z_at > 0), (False, z_at < 3)):
+                if have:
+                    chain_at[name, order, place, up] = (pool, sizes[pool])
+                    sizes[pool] += 1
+    add("chain_short", pltpu.VMEM((sizes["chain_short"], 2 * ROWS + THIRD, LANES), low))
+    add("chain_long", pltpu.VMEM((sizes["chain_long"], most, LANES), low))
     add("sent", pltpu.SemaphoreType.DMA((256,)))
     add("came", pltpu.SemaphoreType.DMA((256,)))
+    span = 3 * rows
+    add("window", pltpu.VMEM((span, features + LANES), low))
+    add("stats", pltpu.VMEM((span, LANES), full))
+    add("head", pltpu.VMEM((2, 3, span, LANES), low))
+    add("head_sem", pltpu.SemaphoreType.DMA((2,)))
+    add("grad_head", pltpu.VMEM((span, LANES), low))
+    add("own_hide", pltpu.VMEM((rows // LANES, LANES, span - rows + LANES), low))
+    add("rim_hide", pltpu.VMEM((2 * rows // LANES, LANES, rows), low))
+    add("probs", pltpu.VMEM((span, rows), low))
+    add("scored", pltpu.VMEM((span, rows), low))
+    add("triple", pltpu.VMEM((3, rows, features + LANES), low))
+    add("weight_sem", pltpu.SemaphoreType.DMA((2,)))
+    add("normed_grad", pltpu.VMEM((rows, features), full))
+    add("chunk", pltpu.VMEM((2, LANES, features), full))
+    add("chunk_sem", pltpu.SemaphoreType.DMA((2,)))
+    add("credit", pltpu.SemaphoreType.REGULAR((8,)))
+    lines = len(LINE_FIRST)
+    line_at = {}
+    for name in LINE_FIRST:
+        for (order, place), z_at in make_units()[name].z_of.items():
+            for up, have in ((True, z_at > 0), (False, z_at < 3)):
+                if have:
+                    line_at[name, order, place, up] = len(line_at)
+    add("line", pltpu.VMEM((lines, 2, 2, 2, 2, most, LANES), low))
+    add("line_land", pltpu.VMEM((len(line_at), 2, 2, most, LANES), low))
+    add("line_own", pltpu.VMEM((lines, 2, 2, most, LANES), low))
+    add("line_x", pltpu.VMEM((lines, 2, most, LANES), low))
+    add("line_y", pltpu.VMEM((lines, most, LANES), low))
+    add("sums", pltpu.VMEM((8, features), full))
+    add("vec", pltpu.VMEM((5, *vec.shape), full))
+    add("vec_land", pltpu.VMEM((5, *vec.shape), full))
 
     def kernel(*refs):
-        r = dict(zip(names, refs))
-        r["vec"][...] = r["vec_in"][...]
-        sum_kernel(units, names, *refs)
+        gradient_kernel(dict(zip(names, refs), chain_at=chain_at, line_at=line_at))
 
     found = pl.pallas_call(
         kernel,
@@ -1103,11 +1437,11 @@
         out_specs=out_specs,
         scratch_shapes=scratch,
         compiler_params=pltpu.CompilerParams(
-            collective_id=0, has_side_effects=True, vmem_limit_bytes=60 * 2**20
+            collective_id=0, has_side_effects=True, vmem_limit_bytes=VMEM_MOST
         ),
-        name="weight_sums",
+        name="gradients",
     )(*operands)
-    return dict(zip([*GRADS, "vec"], found[:6]))
+    return dict(zip([name for name, _ in GRADS] + ["vec", "tok", "skp"], found))
 
 
 def unsplit(value):
@@ -1147,30 +1481,6 @@
         for vector in vector_list
     )
     return tuple(part.astype(jnp.float32) for part in parts), vectors
-
-
-def pack_vectors(vector_list):
-    vec = jnp.concatenate([vector.reshape(32, -1) for vector in vector_list], axis=1)
-    vec = jnp.pad(vec, ((0, 0), (0, 512 - vec.shape[1]))).reshape(4, 2, 2, 2, 4, LANES)
-    return vec.transpose(3, 2, 1, 0, 4, 5)
-
-
-def summed_by_kernel(lefts, rights, vector_list):
-    found = weight_sums(lefts, rights, pack_vectors(vector_list))
-    flat = found["vec"].reshape(-1)
-    vectors, at = [], 0
-    for vector in vector_list:
-        width = vector.shape[0] // 32
-        vectors.append(flat[at : at + width])
-        at += width
-    weight_parts = (
-        found["skip"],
-        found["attn"][:, :864],
-        found["proj"],
-        found["expand"],
-        found["shrink"],
-    )
-    return weight_parts, tuple(vectors)
 
 
 def rims(value, width):
@@ -1225,39 +1535,74 @@
             shrink_weight, shrink_bias,
         ),
     )
-    before, after = rims(mixed_grad, rim)
-    blank = jnp.zeros((rows - rim, mixed_grad.shape[1]), mixed_grad.dtype)
-    grad_window = jnp.concatenate([blank, before, mixed_grad, after, blank], axis=0)
-    stats = grad_window[:, features:].astype(jnp.float32)
-    triple, triple_a, triple_b, triple_sum = attend_back(wins, grad_window, stats, id_col, id_row)
-    tok_grad, skip_grad, stream_grad, stream_by_core, stream_sums = stream_back(
-        triple, attn_weight, stream, middle_grad, first_gain, skip_weight
-    )
-    vector_list = (
-        stream_sums[2],
-        stream_sums[0],
-        stream_sums[1],
-        jnp.concatenate([triple_sum[0, :features], triple_sum[0, 2 * features :]]),
-        sums[0],
-        sums[1],
-        sums[2],
-        hidden_sum[0],
-        sums[3],
-    )
-    joined = jnp.concatenate([tok, skp], axis=1)
-    lefts = dict(active=active, second=second, mixed=mixed, normed=normed, joined=joined)
-    rights = dict(
-        upstream=up_by_core,
-        hidden=hidden_by_core,
-        branch=branch_by_core,
-        triple_a=triple_a,
-        triple_b=triple_b,
-        stream=stream_by_core,
-    )
     if lax.axis_size("seq") == 8 and lax.axis_size("batch") == 4:
-        weight_parts, vectors = summed_by_kernel(lefts, rights, vector_list)
+        vec = jnp.concatenate(
+            [
+                jnp.zeros((5, features), jnp.float32),
+                sums[:4],
+                hidden_sum.reshape(-1, features),
+                jnp.zeros((3, features), jnp.float32),
+            ],
+            axis=0,
+        )
+        found = gradients(
+            dict(
+                active=active, second=second, mixed=mixed, normed=normed, tok=tok, skp=skp,
+                upstream=up_by_core, hidden=hidden_by_core, branch=branch_by_core, wins=wins,
+                grads=mixed_grad, id_col=id_col, id_row=id_row, stream=stream,
+                middle_grad=middle_grad, gain=first_gain[None], attn_weight=attn_weight,
+                skip_weight=skip_weight,
+            ),
+            vec,
+        )
+        tok_grad, skip_grad = found["tok"], found["skp"]
+        weight_parts = (
+            found["skip"], found["attn"][:, :864], found["proj"], found["expand"], found["shrink"]
+        )
+        total = found["vec"]
+        place = position * lax.axis_size("batch") + lax.axis_index("batch")
+
+        def mine(first, count):
+            part = total[first : first + count].reshape(-1)
+            width = part.shape[0] // 32
+            return lax.dynamic_slice_in_dim(part, place * width, width, 0)
+
+        vectors = (
+            mine(0, 1), mine(1, 1), mine(2, 1), mine(3, 2), mine(5, 1), mine(6, 1), mine(7, 1),
+            mine(9, 4), mine(8, 1),
+        )
     else:
-        weight_parts, vectors = summed(lefts, dict(rights, triple=triple), vector_list)
+        before, after = rims(mixed_grad, rim)
+        blank = jnp.zeros((rows - rim, mixed_grad.shape[1]), mixed_grad.dtype)
+        grad_window = jnp.concatenate([blank, before, mixed_grad, after, blank], axis=0)
+        stats = grad_window[:, features:].astype(jnp.float32)
+        triple, triple_sum = attend_back(wins, grad_window, stats, id_col, id_row)
+        tok_grad, skip_grad, stream_by_core, stream_sums = stream_back(
+            triple, attn_weight, stream, middle_grad, first_gain, skip_weight
+        )
+        vector_list = (
+            stream_sums[2],
+            stream_sums[0],
+            stream_sums[1],
+            jnp.concatenate([triple_sum[0, :features], triple_sum[0, 2 * features :]]),
+            sums[0],
+            sums[1],
+            sums[2],
+            hidden_sum[0],
+            sums[3],
+        )
+        joined = jnp.concatenate([tok, skp], axis=1)
+        weight_parts, vectors = summed(
+            dict(active=active, second=second, mixed=mixed, normed=normed, joined=joined),
+            dict(
+                upstream=up_by_core,
+                hidden=hidden_by_core,
+                branch=branch_by_core,
+                triple=triple,
+                stream=stream_by_core,
+            ),
+            vector_list,
+        )
     return (
         result[None],
         tok_grad[None],

time: 443 us -> 345 us (0.78)
  Pallas kernels: 337 us -> 285 us
  waiting for transfers between devices: 48 us -> 16.2 us
  local copies, waits for them, and re-layouts: 34.7 us -> 28.3 us
  starting transfers between devices: 12.7 us -> 6.38 us
    pallas_call x3 -> x1, Pallas kernels: 247 us -> 195 us  [gradients(): pl.pallas_call(kernel, out_shape=out_shape, in_specs=in_specs, out_specs=...]
    ppermute x2 -> x1, waiting for transfers between devices: 48 us -> 16.2 us  [rims(): lax.ppermute(value[-width:], 'seq', up)]
    ppermute x2 -> x1, starting transfers between devices: 9.48 us -> 4.92 us  [rims(): lax.ppermute(value[-width:], 'seq', up)]
    unnamed x41 -> x35, local copies, waits for them, and re-layouts: 13 us -> 10.4 us
  transfers between devices with their start and end apart: 4 -> 2, of which waited for: 2 -> 1; matrix products, arithmetic and copies ran while one was open for 2% -> 2% of each run, Pallas kernels for 2% -> 3%
where the time goes in v2:
time: 345 us; the launch traced here: 338 us
  Pallas kernels  285 us (83%)
  local copies, waits for them, and re-layouts  28.3 us (8%)
  waiting for transfers between devices  16.2 us (5%)
  starting transfers between devices  6.38 us (2%)
    pallas_call x1, Pallas kernels, gradients(): pl.pallas_call(kernel, out_shape=out_shape, in_specs=in_specs, out_specs=...  195 us
    pallas_call x1, Pallas kernels, layer(): pl.pallas_call(layer_kernel, grid=(4,), in_specs=[held(narrow), held(narr...  38 us
    pallas_call x1, Pallas kernels, attend(): pl.pallas_call(attend_kernel, out_shape=(jax.ShapeDtypeStruct((3, HEADS,...  34.3 us
    ppermute x1, waiting for transfers between devices, rims(): lax.ppermute(value[-width:], 'seq', up)  16.2 us
    unnamed x35, local copies, waits for them, and re-layouts  10.4 us
    pallas_call x1, Pallas kernels, own_heads(): pl.pallas_call(project_kernel, out_shape=jax.ShapeDtypeStruct((3, HEADS,...  9.96 us
    pallas_call x1, Pallas kernels, stream_norm(): pl.pallas_call(stream_kernel, out_shape=(jax.ShapeDtypeStruct((rows, feat...  7.97 us
  transfers between devices with their start and end apart: 2, of which 1 were waited for; matrix products, arithmetic and copies ran while one was open for 2% of the time, Pallas kernels for 3%

profile of v2, /device:TPU:0, one launch (start us, length us, event | category | flops | bytes accessed | tf_op | source)
XLA Modules:
  0.0 338.5 jit_solution(10753341049807787290)
XLA Ops:
  0.7 1.3 broadcast_in_dim.50.bias
  1.9 1.3 broadcast_in_dim.51.gain.refs_15_
  3.2 1.3 broadcast_in_dim.52.shift
  4.5 8.0 %stream_norm.1 = (f32[384,1152]{1,0:T(8,128)}, bf16[384,1152]{1,0:T(8,128)(2,1)}) custom-call(bf16[384,1152]{1,0:T(8,128)(2,1)} %bitcast.22, bf16[384,1152]{1,0:T(8,128)(2,1)} %bitcast.24, bf16[2304,1152]{1,0:T(8,128)(2,1)} %refs_17_.1, bf16[1,1152]{1,0:T(2,128)(2,1)} %broadcast_in_dim.50.bias, bf16[1,1152]{1,0:T(2,128)(2,1)} %broadcast_in_dim.51.gain.refs_15_, ...), custom_call_target="tpu_custom_call" | custom-call | flops 2038431744 | bytes 10000000 | tf_op jit(solution)/shard_map/stream_norm/pallas_call | solution.py:102
  12.5 0.0 copy-start.9
  12.5 0.0 copy-start.10
  12.5 0.0 copy-start.11
  12.5 0.0 copy-start.12
  12.5 0.0 copy-start.8
  12.6 1.5 fusion.7
  14.1 4.9 %collective-permute-start = (bf16[336,1152]{1,0:T(8,128)(2,1)S(1)}, bf16[336,1152]{1,0:T(8,128)(2,1)S(1)}, u32[]{:S(2)}, u32[]{:S(2)}) collective-permute-start(bf16[336,1152]{1,0:T(8,128)(2,1)S(1)} %get-tuple-element.98), channel_id=1, source_target_pairs={{0,4},{4,8},{8,12},{12,16},{16,20},{20,24},{24,28},{1,5},{5,9},{9,... | collective-permute-start | bytes 2322440 | tf_op jit(solution)/shard_map/ppermute | solution.py:1491
  19.0 1.5 collective-permute-start.1
  20.5 0.1 pad_dynamic-slice_fusion
  20.6 1.0 broadcast_in_dim.66.id_col.refs_11_
  21.6 0.6 broadcast_in_dim.55.id_row.refs_12_
  22.2 0.6 broadcast_in_dim.53.bias
  22.8 0.6 broadcast_in_dim.56.proj_bias
  23.4 0.6 broadcast_in_dim.57.gain
  24.0 0.6 broadcast_in_dim.58.shift
  24.6 0.6 broadcast_in_dim.59.expand_bias
  25.2 0.6 broadcast_in_dim.60.shrink_bias
  25.8 0.1 pad.8.clone
  25.9 10.0 %own_heads.1.own = bf16[3,16,384,128]{3,2,1,0:T(8,128)(2,1)} custom-call(bf16[384,1152]{1,0:T(8,128)(2,1)} %get-tuple-element.41.normed.refs_3_, bf16[1152,3456]{1,0:T(8,128)(2,1)} %refs_16_.1, bf16[1,2304]{1,0:T(2,128)(2,1)} %broadcast_in_dim.53.bias), custom_call_target="tpu_custom_call" | custom-call | flops 3057647616 | bytes 20000000 | tf_op jit(solution)/shard_map/own_heads/pallas_call | solution.py:170
  35.9 16.2 %collective-permute-done.before = bf16[336,1152]{1,0:T(8,128)(2,1)S(1)} collective-permute-done((bf16[336,1152]{1,0:T(8,128)(2,1)S(1)}, bf16[336,1152]{1,0:T(8,128)(2,1)S(1)}, u32[]{:S(2)}, u32[]{:S(2)}) %collective-permute-start) | collective-permute-done | bytes 774176 | tf_op jit(solution)/shard_map/ppermute | solution.py:1491
  52.1 0.9 copy-done.1
  52.9 0.9 copy-done.2
  53.8 34.3 %attend.1 = (bf16[3,16,1152,128]{3,2,1,0:T(8,128)(2,1)}, bf16[384,1152]{1,0:T(8,128)(2,1)}, f32[384,128]{1,0:T(8,128)}) custom-call(bf16[3,16,384,128]{3,2,1,0:T(8,128)(2,1)} %own_heads.1.own, bf16[336,1152]{1,0:T(8,128)(2,1)} %copy-done.1, bf16[336,1152]{1,0:T(8,128)(2,1)} %copy-done.2, bf16[1152,3456]{1,0:T(8,128)(2,1)} %refs_16_.1, ...), custom_call_target="tpu_custom_call" | custom-call | tf_op jit(solution)/shard_map/attend/pallas_call | solution.py:258
  88.2 38.0 %layer.1 = (bf16[384,1152]{1,0:T(8,128)(2,1)}, bf16[384,4608]{1,0:T(8,128)(2,1)}, bf16[2,3,384,768]{3,2,1,0:T(8,128)(2,1)}, bf16[384,1152]{1,0:T(8,128)(2,1)}, b...) custom-call(f32[384,1152]{1,0:T(8,128)} %get-tuple-element.40.stream, ...), custom_call_target="tpu_custom_call" | custom-call | tf_op jit(solution)/shard_map/layer/pallas_call | solution.py:375
  126.1 0.8 reduce
  126.9 0.8 slice.41
  127.7 0.7 maximum_maximum_fusion.refs_18_
  128.4 194.9 %gradients.1 = (f32[576,288]{1,0:T(8,128)}, f32[144,1152]{1,0:T(8,128)}, f32[144,288]{1,0:T(8,128)}, f32[144,896]{1,0:T(8,128)}, f32[288,288]{1,0:T(8,128)}, /*i...) custom-call(bf16[384,4608]{1,0:T(8,128)(2,1)} %get-tuple-element.45., ...), custom_call_target="tpu_custom_call" | custom-call | tf_op jit(solution)/shard_map/gradients/pallas_call | solution.py:1433
  323.3 1.2 fusion.8
  324.6 0.8 slice.46
  325.3 0.8 slice.50
  326.2 2.4 copy.38
  328.6 0.6 fusion.6
  329.2 0.6 fusion
  329.7 0.6 fusion.2
  330.3 0.6 dynamic_slice.51
  330.9 0.6 fusion.4
  331.5 0.6 dynamic_slice.58
  332.1 2.1 copy.45
  334.3 0.9 copy.46
  335.2 0.8 copy.47
  336.0 0.8 copy.48
  336.8 0.7 copy.49
  337.4 0.8 copy.50
  (28 shorter events, 0.1 us)
Async XLA Ops:
  4.5 16.0 %copy-start.7 = (s32[1,3072]{1,0:T(1,128)S(1)}, s32[1,3072]{1,0:T(1,128)}, u32[]{:S(2)}) copy-start(s32[1,3072]{1,0:T(1,128)} %param.20) | copy-start | bytes 36868
  12.5 9.7 %copy-start.9 = (bf16[2304]{0:T(1024)(128)(2,1)S(1)}, bf16[2304]{0:T(1024)(128)(2,1)}, u32[]{:S(2)}) copy-start(bf16[2304]{0:T(1024)(128)(2,1)} %param.27) | copy-start | bytes 13828
  12.5 10.3 %copy-start.10 = (bf16[1152]{0:T(1024)(128)(2,1)S(1)}, bf16[1152]{0:T(1024)(128)(2,1)}, u32[]{:S(2)}) copy-start(bf16[1152]{0:T(1024)(128)(2,1)} %param.29) | copy-start | bytes 6916
  12.5 10.9 %copy-start.11 = (bf16[1152]{0:T(1024)(128)(2,1)S(1)}, bf16[1152]{0:T(1024)(128)(2,1)}, u32[]{:S(2)}) copy-start(bf16[1152]{0:T(1024)(128)(2,1)} %param.30) | copy-start | bytes 6916
  12.5 11.5 %copy-start.12 = (bf16[1152]{0:T(1024)(128)(2,1)S(1)}, bf16[1152]{0:T(1024)(128)(2,1)}, u32[]{:S(2)}) copy-start(bf16[1152]{0:T(1024)(128)(2,1)} %param.31) | copy-start | bytes 6916
  12.5 12.1 %copy-start.8 = (bf16[4608]{0:T(1024)(128)(2,1)S(1)}, bf16[4608]{0:T(1024)(128)(2,1)}, u32[]{:S(2)}) copy-start(bf16[4608]{0:T(1024)(128)(2,1)} %param.33) | copy-start | bytes 27652
  12.5 12.7 %copy-start.13 = (bf16[1152]{0:T(1024)(128)(2,1)S(1)}, bf16[1152]{0:T(1024)(128)(2,1)}, u32[]{:S(2)}) copy-start(bf16[1152]{0:T(1024)(128)(2,1)} %param.35) | copy-start | bytes 6916
  14.1 38.0 %collective-permute-start = (bf16[336,1152]{1,0:T(8,128)(2,1)S(1)}, bf16[336,1152]{1,0:T(8,128)(2,1)S(1)}, u32[]{:S(2)}, u32[]{:S(2)}) collective-permute-start(bf16[336,1152]{1,0:T(8,128)(2,1)S(1)} %get-tuple-element.98), channel_id=1, source_target_pairs={{0,4},{4,8},{8,12},{12,16},{16,20},{20,24},{24,28},{1,5},{5,9},{9,... | collective-permute-start | bytes 2322440 | tf_op jit(solution)/shard_map/ppermute | solution.py:1491
  19.0 33.1 %collective-permute-start.1 = (bf16[336,1152]{1,0:T(8,128)(2,1)S(1)}, bf16[336,1152]{1,0:T(8,128)(2,1)S(1)}, u32[]{:S(2)}, u32[]{:S(2)}) collective-permute-start(bf16[336,1152]{1,0:T(8,128)(2,1)S(1)} %get-tuple-element.97), channel_id=1, source_target_pairs={{4,0},{8,4},{12,8},{16,12},{20,16},{24,20},{28,24},{5,1},{9,5},{13... | collective-permute-start | bytes 2322440 | tf_op jit(solution)/shard_map/ppermute | solution.py:1492
  52.0 0.9 copy-start.1
  52.9 0.9 copy-start.2
  323.3 11.0 %copy-start = (bf16[384,1152]{1,0:T(8,128)(2,1)S(1)}, bf16[384,1152]{1,0:T(8,128)(2,1)}, u32[]{:S(2)}) copy-start(bf16[384,1152]{1,0:T(8,128)(2,1)} %get-tuple-element.56) | copy-start | bytes 2654212
  323.3 11.9 %copy-start.5 = (f32[288,288]{1,0:T(8,128)S(1)}, f32[288,288]{1,0:T(8,128)}, u32[]{:S(2)}) copy-start(f32[288,288]{1,0:T(8,128)} %get-tuple-element.132) | copy-start | bytes 995332
  323.3 12.6 %copy-start.4 = (f32[144,896]{1,0:T(8,128)S(1)}, f32[144,896]{1,0:T(8,128)}, u32[]{:S(2)}) copy-start(f32[144,896]{1,0:T(8,128)} %get-tuple-element.59) | copy-start | bytes 1548292
  326.1 10.6 %copy-start.6 = (f32[144,288]{1,0:T(8,128)S(1)}, f32[144,288]{1,0:T(8,128)}, u32[]{:S(2)}) copy-start(f32[144,288]{1,0:T(8,128)} %get-tuple-element.138) | copy-start | bytes 497668
  326.2 11.3 %copy-start.3 = (f32[144,1152]{1,0:T(8,128)S(1)}, f32[144,1152]{1,0:T(8,128)}, u32[]{:S(2)}) copy-start(f32[144,1152]{1,0:T(8,128)} %get-tuple-element.142) | copy-start | bytes 1990660

commit v3 on v2

--- a/solution.py
+++ b/solution.py
@@ -31,6 +31,11 @@
     return lax.dot_general(
         left, right, (((0,), (0,)), ((), ())), preferred_element_type=jnp.float32
     )
+
+
+def vector(ref, first=0, count=None):
+    count = ref.shape[0] if count is None else count
+    return ref[pl.ds(first, count)].astype(jnp.float32).reshape(1, count)
 
 
 def whole():
@@ -89,12 +94,10 @@
         stream[:, at] = (
             dot(tok[...], held[n, :features])
             + dot(skp[...], held[n, features:])
-            + bias[:, at].astype(jnp.float32)
+            + vector(bias, 384 * n, 384)
         )
     unit, _ = row_norm(stream[...])
-    normed[...] = (unit * gain[...].astype(jnp.float32) + shift[...].astype(jnp.float32)).astype(
-        jnp.bfloat16
-    )
+    normed[...] = (unit * vector(gain) + vector(shift)).astype(jnp.bfloat16)
 
 
 def stream_norm(tok, skp, weight, bias, gain, shift):
@@ -116,7 +119,7 @@
             flops=4 * rows * features * features, bytes_accessed=10**7, transcendentals=0
         ),
         name="stream_norm",
-    )(tok, skp, weight, bias[None], gain[None], shift[None])
+    )(tok, skp, weight, bias, gain, shift)
 
 
 MARKS = (HEAD_DIM, HEAD_DIM + 16, HEAD_DIM + 32)
@@ -142,7 +145,7 @@
     value = dot(rows_ref[...], weight_ref[...])
     if part != 1:
         at = 0 if part == 0 else features
-        value = value + bias[:, at : at + features].astype(jnp.float32)
+        value = value + vector(bias, at, features)
     value = value.astype(jnp.bfloat16)
     for h in range(HEADS):
         store(part, h, head_tile(value, h, part > 0))
@@ -181,7 +184,7 @@
             flops=6 * rows * features * features, bytes_accessed=2 * 10**7, transcendentals=0
         ),
         name="own_heads",
-    )(normed, weight, bias[None])
+    )(normed, weight, bias)
 
 
 HIDE = -1e30
@@ -227,24 +230,33 @@
         hide[i] = jnp.where(same, 0.0, HIDE)
     lse[...] = jnp.zeros_like(lse)
 
-    def body(h, carry):
-        for i in range(blocks):
-            keys = pl.ds(i * LANES, reach)
-            scores = dot_nt(
-                window[0, h, rows + i * LANES : rows + (i + 1) * LANES], window[1, h, keys]
+    def body(pair, carry):
+        jobs = [(2 * pair + k, i) for k in range(2) for i in range(blocks)]
+        scores = [
+            dot_nt(
+                window[0, h, rows + i * LANES : rows + (i + 1) * LANES],
+                window[1, h, pl.ds(i * LANES, reach)],
             )
-            scores = scores * SCALE2 + hide[i]
-            highest = jnp.max(scores, axis=-1, keepdims=True)
-            raised = jnp.exp2(scores - highest).astype(jnp.bfloat16)
-            total = dot(raised, window[2, h, keys])
+            * SCALE2
+            + hide[i]
+            for h, i in jobs
+        ]
+        highest = [jnp.max(value, axis=-1, keepdims=True) for value in scores]
+        raised = [
+            jnp.exp2(value - most).astype(jnp.bfloat16) for value, most in zip(scores, highest)
+        ]
+        totals = [
+            dot(value, window[2, h, pl.ds(i * LANES, reach)]) for value, (h, i) in zip(raised, jobs)
+        ]
+        for total, most, (h, i) in zip(totals, highest, jobs):
+            at = slice(i * LANES, (i + 1) * LANES)
             denominator = total[:, HEAD_DIM : HEAD_DIM + 1]
-            gathered[h, i * LANES : (i + 1) * LANES] = total / denominator
-            value = highest + jnp.log2(denominator)
-            at = slice(i * LANES, (i + 1) * LANES)
+            gathered[h, at] = total / denominator
+            value = most + jnp.log2(denominator)
             lse[at] = jnp.where(lanes_of((LANES, LANES)) == h, value, lse[at])
         return carry
 
-    lax.fori_loop(0, HEADS, body, 0)
+    lax.fori_loop(0, HEADS // 2, body, 0)
     for h in range(HEADS):
         mixed[:, HEAD_DIM * h : HEAD_DIM * (h + 1)] = gathered[h, :, :HEAD_DIM].astype(jnp.bfloat16)
     for copy in out_copies:
@@ -275,17 +287,17 @@
         ],
         compiler_params=params(),
         name="attend",
-    )(own, before, after, weight, bias[None], id_col, id_row)
+    )(own, before, after, weight, bias, id_col, id_row)
 
 
 def by_core_store(ref, value):
-    rows = value.shape[0]
-    blank = jnp.zeros((rows, LANES - 32), value.dtype)
+    blank = jnp.zeros((value.shape[0], 32), value.dtype)
     for b in range(4):
         x, c = b // 2, b % 2
         ref[c, 0, :, 256 * x : 256 * x + 256] = value[:, 288 * b : 288 * b + 256]
+        rest = value[:, 288 * b + 256 : 288 * b + 288]
         ref[c, 0, :, 512 + LANES * x : 640 + LANES * x] = jnp.concatenate(
-            [value[:, 288 * b + 256 : 288 * b + 288], blank], axis=1
+            [rest, rest, rest, blank], axis=1
         )
 
 
@@ -299,25 +311,27 @@
 def layer_kernel(
     stream, mixed, lse, upstream, proj, proj_bias, gain, shift, expand, expand_bias, shrink,
     shrink_bias, result, active, hidden_by_core, second, branch, branch_by_core, up_by_core,
-    middle_grad, mixed_grad, hidden_sum, sums, middle, total, second_grad,
+    middle_grad, mixed_grad, sums, middle, total, second_grad,
+    bias_rows,
 ):
     step, steps = pl.program_id(0), pl.num_programs(0)
     low = jnp.bfloat16
+    wide = expand.shape[1]
 
     @pl.when(step == 0)
     def _():
         middle[...] = (
-            stream[...] + dot(mixed[...], proj[...]) + proj_bias[...].astype(jnp.float32)
+            stream[...] + dot(mixed[...], proj[...]) + vector(proj_bias)
         )
         unit, _ = row_norm(middle[...])
-        second[...] = (
-            unit * gain[...].astype(jnp.float32) + shift[...].astype(jnp.float32)
-        ).astype(low)
-        total[...] = middle[...] + shrink_bias[...].astype(jnp.float32)
+        second[...] = (unit * vector(gain) + vector(shift)).astype(low)
+        total[...] = middle[...] + vector(shrink_bias)
         second_grad[...] = jnp.zeros_like(second_grad)
+        for t in range(4):
+            bias_rows[t : t + 1] = vector(expand_bias, wide * t, wide)
         by_core_store(up_by_core, upstream[...])
 
-    hidden = dot(second[...], expand[...]) + expand_bias[...].astype(jnp.float32)
+    hidden = dot(second[...], expand[...]) + bias_rows[pl.ds(step, 1)]
     active_grad = dot_nt(upstream[...], shrink[...])
     cdf = 0.5 + 0.5 * erf(hidden * (1.0 / ROOT2))
     density = jnp.exp(-0.5 * hidden * hidden) * 0.3989422804014327
@@ -326,7 +340,12 @@
     hidden_grad = (active_grad * (cdf + hidden * density)).astype(low)
     for j in range(3):
         hidden_by_core[0, j] = hidden_grad[:, 384 * j : 384 * (j + 1)]
-    hidden_sum[...] = column_sum(hidden_grad.astype(jnp.float32))
+    for t in range(4):
+
+        @pl.when(step == t)
+        def _():
+            sums[9 + t : 10 + t] = column_sum(hidden_grad.astype(jnp.float32))
+
     total[...] += dot(raised, shrink[...])
     second_grad[...] += dot_nt(hidden_grad, expand[...])
 
@@ -336,15 +355,17 @@
         unit, scale = row_norm(middle[...])
         cotangent = second_grad[...]
         above = upstream[...].astype(jnp.float32)
-        grad = above + norm_back(unit, scale, gain[...].astype(jnp.float32), cotangent)
+        grad = above + norm_back(unit, scale, vector(gain), cotangent)
         middle_grad[...] = grad
         branched = grad.astype(low)
         branch[...] = branched
         by_core_store(branch_by_core, branched)
-        sums[0:1] = column_sum(branched.astype(jnp.float32))
-        sums[1:2] = column_sum(cotangent * unit)
-        sums[2:3] = column_sum(cotangent)
-        sums[3:4] = column_sum(above)
+        sums[0:5] = jnp.zeros((5, sums.shape[1]), jnp.float32)
+        sums[5:6] = column_sum(branched.astype(jnp.float32))
+        sums[6:7] = column_sum(cotangent * unit)
+        sums[7:8] = column_sum(cotangent)
+        sums[8:9] = column_sum(above)
+        sums[13:16] = jnp.zeros((3, sums.shape[1]), jnp.float32)
         back = dot_nt(branched, proj[...]).astype(low)
         features = back.shape[1]
         mixed_grad[:, :features] = back
@@ -370,18 +391,17 @@
         return pl.BlockSpec(shape, lambda t: (0,) * len(shape))
 
     narrow = (rows, features)
-    vector = (1, features)
     split = (2, 1, rows, 768)
     return pl.pallas_call(
         layer_kernel,
         grid=(4,),
         in_specs=[
             held(narrow), held(narrow), held((rows, LANES)), held(narrow),
-            held((features, features)), held(vector), held(vector), held(vector),
+            held((features, features)), whole(), whole(), whole(),
             pl.BlockSpec((features, wide), lambda t: (0, t)),
-            pl.BlockSpec((1, wide), lambda t: (0, t)),
+            whole(),
             pl.BlockSpec((wide, features), lambda t: (t, 0)),
-            held(vector),
+            whole(),
         ],
         out_specs=(
             held(narrow),
@@ -389,8 +409,7 @@
             pl.BlockSpec((1, 3, rows, 384), lambda t: (t % 2, 0, 0, t // 2)),
             held(narrow), held(narrow), held(split), held(split), held(narrow),
             held((rows, features + LANES)),
-            pl.BlockSpec((1, wide), lambda t: (0, t)),
-            held((8, features)),
+            held((16, features)),
         ),
         out_shape=(
             jax.ShapeDtypeStruct(narrow, low),
@@ -402,15 +421,15 @@
             jax.ShapeDtypeStruct(split, low),
             jax.ShapeDtypeStruct(narrow, jnp.float32),
             jax.ShapeDtypeStruct((rows, features + LANES), low),
-            jax.ShapeDtypeStruct((1, hidden), jnp.float32),
-            jax.ShapeDtypeStruct((8, features), jnp.float32),
+            jax.ShapeDtypeStruct((16, features), jnp.float32),
         ),
-        scratch_shapes=[pltpu.VMEM(narrow, jnp.float32)] * 3,
+        scratch_shapes=[pltpu.VMEM(narrow, jnp.float32)] * 3
+        + [pltpu.VMEM((4, wide), jnp.float32)],
         compiler_params=params(),
         name="layer",
     )(
-        stream, mixed, lse, upstream, proj, proj_bias[None], gain[None], shift[None], expand,
-        expand_bias[None], shrink, shrink_bias[None],
+        stream, mixed, lse, upstream, proj, proj_bias, gain, shift, expand, expand_bias, shrink,
+        shrink_bias,
     )
 
 
@@ -430,50 +449,46 @@
 
 
 def with_stats(value, stats, shift):
-    lane = lanes_of(value.shape)
-    moved = pltpu.roll(stats, shift, 1)
-    return jnp.where(marked(lane), moved, value.astype(jnp.float32)).astype(value.dtype)
-
-
-def back_head(h, queries, keys, values, grads, stats, own_hide, rim_hide, probs, scored, store):
+    return jnp.where(marked(lanes_of(value.shape)), pltpu.roll(stats, shift, 1), value)
+
+
+def back_head(h, queries, keys, values, grads, stats, own_hide, rim_hide, probs, scored):
     span = queries.shape[0]
     rows = span // 3
     blocks = rows // LANES
     reach = span - rows + LANES
-    low = jnp.bfloat16
-    queries[...] = with_stats(queries[...], stats[...], MARKS[0] - h)
+    low, full = jnp.bfloat16, jnp.float32
+    queries[...] = with_stats(queries[...], stats, MARKS[0] - h)
     turn = MARKS[0] - 3 * HEADS - h
-    grads[...] = with_stats(grads[...], stats[...], jnp.where(turn < 0, turn + LANES, turn))
-
-    def pair(q_at, k_at, width, hide):
-        q_rows, k_rows = pl.ds(q_at, LANES), pl.ds(k_at, width)
-        exponent = dot_nt(queries[q_rows], keys[k_rows]) * SCALE2 + hide.astype(jnp.float32)
-        weight = jnp.exp2(exponent)
-        scored = weight * dot_nt(grads[q_rows], values[k_rows])
-        return weight.astype(low), scored.astype(low)
-
-    query_grad = []
+    grads[...] = with_stats(grads[...], stats, jnp.where(turn < 0, turn + LANES, turn))
+    jobs = []
     for i in range(blocks):
-        at = rows + i * LANES
-        weight, score = pair(at, i * LANES, reach, own_hide[i])
-        query_grad.append(dot(score, keys[i * LANES : i * LANES + reach]))
-        mine = slice(rows - i * LANES, 2 * rows - i * LANES)
-        probs[at : at + LANES] = weight[:, mine]
-        scored[at : at + LANES] = score[:, mine]
+        jobs.append(
+            (rows + i * LANES, i * LANES, reach, own_hide[i], rows - i * LANES, rows, 0)
+        )
     for w in range(blocks):
-        for at, first, width in (
-            (w * LANES, 0, (w + 1) * LANES),
-            (2 * rows + w * LANES, w * LANES, rows - w * LANES),
-        ):
-            hide = rim_hide[w if at < rows else blocks + w]
-            weight, score = pair(at, rows + first, width, hide[:, first : first + width])
-            probs[at : at + LANES, first : first + width] = weight
-            scored[at : at + LANES, first : first + width] = score
+        width = (w + 1) * LANES
+        jobs.append((w * LANES, rows, width, rim_hide[w][:, :width], 0, width, 0))
+        first, width = w * LANES, rows - w * LANES
+        hide = rim_hide[blocks + w][:, first:]
+        jobs.append((2 * rows + first, rows + first, width, hide, 0, width, first))
+    scores = [dot_nt(queries[q : q + LANES], keys[k : k + n]) for q, k, n, *_ in jobs]
+    inner = [dot_nt(grads[q : q + LANES], values[k : k + n]) for q, k, n, *_ in jobs]
+    weights = [
+        jnp.exp2(value * SCALE2 + job[3].astype(full)) for value, job in zip(scores, jobs)
+    ]
+    scores = [(weight * value).astype(low) for weight, value in zip(weights, inner)]
+    weights = [weight.astype(low) for weight in weights]
+    for weight, score, (q, _, _, _, first, count, place) in zip(weights, scores, jobs):
+        probs[q : q + LANES, place : place + count] = weight[:, first : first + count]
+        scored[q : q + LANES, place : place + count] = score[:, first : first + count]
     factor = HEAD_DIM**-0.5
-    for i in range(blocks):
-        store(0, i * LANES, LANES, query_grad[i] * factor)
-    store(1, 0, rows, dot_tn(scored[...], queries[...]) * factor)
-    store(2, 0, rows, dot_tn(probs[...], grads[...]))
+    query_grad = jnp.concatenate(
+        [dot(scores[i], keys[i * LANES : i * LANES + reach]) * factor for i in range(blocks)], axis=0
+    )
+    key_grad = dot_tn(scored[...], queries[...]) * factor
+    value_grad = dot_tn(probs[...], grads[...])
+    return query_grad.astype(low), key_grad.astype(low), value_grad.astype(low)
 
 
 def heads_apart(row_ref, out):
@@ -505,13 +520,12 @@
     copy.wait()
 
     def body(h, carry):
-        def store(part, first, count, value):
-            apart[part, h, pl.ds(first, count)] = value.astype(jnp.bfloat16)
-
-        back_head(
-            h, window.at[0, h], window.at[1, h], window.at[2, h], grads.at[h], stats, own_hide,
-            rim_hide, probs, scored, store,
+        found = back_head(
+            h, window.at[0, h], window.at[1, h], window.at[2, h], grads.at[h], stats[...],
+            own_hide, rim_hide, probs, scored,
         )
+        for part, value in enumerate(found):
+            apart[part, h] = value
         return carry
 
     lax.fori_loop(0, HEADS, body, 0)
@@ -575,9 +589,7 @@
     cotangent = grad[...]
     sums[0:1] = column_sum(cotangent * unit)
     sums[1:2] = column_sum(cotangent)
-    whole_grad = middle_grad[...] + norm_back(
-        unit, scale, gain[...].astype(jnp.float32), cotangent
-    )
+    whole_grad = middle_grad[...] + norm_back(unit, scale, vector(gain), cotangent)
     rounded = whole_grad.astype(low)
     by_core_store(by_core, rounded)
     sums[2:3] = column_sum(rounded.astype(jnp.float32))
@@ -607,7 +619,7 @@
         ],
         compiler_params=params(),
         name="stream_back",
-    )(triple, weight, stream, middle_grad, gain[None], skip_weight)
+    )(triple, weight, stream, middle_grad, gain, skip_weight)
 
 
 ROWS = 144
@@ -631,18 +643,23 @@
 )
 
 
+SHRINK, EXPAND, PROJ, ATTN, SKIP = (0, 1, 2, 3), (4, 5, 6), 7, (8, 9, 10), (11, 12)
+START, TURN, SETTLE, HOP, FINISH, LINE, LINE_END, LINE_X, LINE_Y = range(9)
+HALO, HEAD, PACK, BACK, NORM, OUT, VECTOR = range(9, 16)
+
+
 def make_units():
     units = {}
     for z in range(4):
         blocks = [
             (y * 576 + q * ROWS, q // 2, y, q % 2, z) for y in range(2) for q in range(4)
         ]
-        units[f"shrink{z}"] = Unit("active", z * 1152, "upstream", 0, 0, blocks, "shrink", 0)
+        units[SHRINK[z]] = Unit("active", z * 1152, "upstream", 0, 0, blocks, "shrink", 0)
     for j in range(3):
-        units[f"expand{j}"] = Unit("second", 0, "hidden", j, 3, QUARTERS, "expand", 3 * j)
-    units["proj"] = Unit("mixed", 0, "branch", 0, 0, QUARTERS, "proj", 0)
+        units[EXPAND[j]] = Unit("second", 0, "hidden", j, 3, QUARTERS, "expand", 3 * j)
+    units[PROJ] = Unit("mixed", 0, "branch", 0, 0, QUARTERS, "proj", 0)
     for j, (first, tiles) in enumerate(TRIPLE_TILES):
-        units[f"attn{j}"] = Unit("normed", 0, f"triple{j}", 0, tiles, QUARTERS, "attn", first)
+        units[ATTN[j]] = Unit("normed", 0, f"triple{j}", 0, tiles, QUARTERS, "attn", first)
     for k, name in enumerate(("tok", "skp")):
         blocks = [
             (h * 576 + y * 288 + i * ROWS, h, y, i, 2 * k + h)
@@ -650,7 +667,7 @@
             for y in range(2)
             for i in range(2)
         ]
-        units[f"skip{k}"] = Unit(name, 0, "stream_cols", 0, 0, blocks, "skip", 0)
+        units[SKIP[k]] = Unit(name, 0, "stream_cols", 0, 0, blocks, "skip", 0)
     return units
 
 
@@ -659,31 +676,35 @@
     ("shrink", (576, 288)),
     ("expand", (144, 1152)),
     ("proj", (144, 288)),
-    ("attn", (144, 896)),
+    ("attn", (144, 864)),
     ("skip", (288, 288)),
 )
 PART_SLOTS, FIRST_SLOTS, SECOND_SLOTS, LAST_SLOTS = 4, 4, 4, 5
-LINE_FIRST = ("expand0",)
-X_FIRST = ("shrink0", "shrink1", "shrink2", "shrink3")
-
+LINE_FIRST = (EXPAND[0], ATTN[0])
+X_FIRST = (SHRINK[0], SHRINK[1], SHRINK[2], SHRINK[3])
 PLAN = (
-    "start shrink0", "start expand0", "start shrink3", "start shrink1", "start shrink2",
-    "line expand0 1 0", "line expand0 1 1", "line expand0 1 2", "second shrink0", "line expand0 2 0",
-    "second shrink3", "line expand0 2 1", "line expand0 3 0", "halo", "heads 4", "line_end expand0",
-    "second shrink1", "third shrink0", "start expand1", "third shrink3", "start expand2",
-    "hop shrink0 2", "heads 2", "hop shrink3 2", "second shrink2", "hop shrink0 3", "third shrink1",
-    "start proj", "line_x expand0", "heads 2", "hop shrink3 3", "hop shrink1 2", "hop shrink1 3",
-    "finish shrink0", "heads 2", "second expand1", "heads 2", "second expand2", "finish shrink3",
-    "finish shrink1", "third shrink2", "heads 2", "line_y expand0", "second proj", "hop shrink2 2",
-    "hop shrink2 3", "heads 2", "pack", "start attn0", "finish shrink2", "third expand1", "start attn1",
-    "hop expand1 2", "third expand2", "start attn2", "hop expand1 3", "back 0", "hop expand2 2",
-    "second attn0", "back 1", "hop expand2 3", "finish expand1", "back 2", "second attn1", "norm",
-    "vec 0", "second attn2", "vec 1", "finish expand2", "third proj", "start skip0", "hop proj 2",
-    "third attn0", "start skip1", "hop proj 3", "hop attn0 2", "out 0", "vec 2", "out 1", "hop attn0 3",
-    "out 2", "third attn1", "hop attn1 2", "finish proj", "second skip0", "third attn2", "hop attn1 3",
-    "hop attn2 2", "hop attn2 3", "finish attn0", "vec 3", "second skip1", "finish attn1", "third skip0",
-    "hop skip0 2", "finish attn2", "vec 4", "hop skip0 3", "third skip1", "hop skip1 2", "hop skip1 3",
-    "finish skip0", "vec 5", "finish skip1",
+    (START, SHRINK[0]), (START, EXPAND[0]), (LINE, EXPAND[0], 1, 0), (LINE, EXPAND[0], 1, 1),
+    (LINE, EXPAND[0], 1, 2), (START, SHRINK[3]), (START, SHRINK[1]), (START, SHRINK[2]),
+    (LINE, EXPAND[0], 2, 0), (TURN, SHRINK[0]), (TURN, SHRINK[3]), (LINE, EXPAND[0], 2, 1),
+    (LINE, EXPAND[0], 3, 0), (HALO,), (HEAD, 4), (SETTLE, SHRINK[0]), (START, EXPAND[1]),
+    (TURN, SHRINK[1]), (LINE_END, EXPAND[0]), (HEAD, 2), (SETTLE, SHRINK[3]), (HOP, SHRINK[0], 2),
+    (START, EXPAND[2]), (HEAD, 2), (TURN, SHRINK[2]), (HOP, SHRINK[0], 3), (HOP, SHRINK[3], 2),
+    (HEAD, 4), (TURN, EXPAND[1]), (SETTLE, SHRINK[1]), (HOP, SHRINK[3], 3), (START, PROJ),
+    (FINISH, SHRINK[0]), (LINE_X, EXPAND[0]), (HEAD, 2), (HOP, SHRINK[1], 2), (HOP, SHRINK[1], 3),
+    (HEAD, 2), (TURN, EXPAND[2]), (SETTLE, SHRINK[2]), (FINISH, SHRINK[3]), (PACK,), (START, ATTN[0]),
+    (SETTLE, EXPAND[1]), (START, ATTN[1]), (HOP, SHRINK[2], 2), (START, ATTN[2]), (TURN, PROJ),
+    (LINE_Y, EXPAND[0]), (HOP, EXPAND[1], 2), (HOP, SHRINK[2], 3), (LINE, ATTN[0], 1, 0),
+    (LINE, ATTN[0], 1, 1), (LINE, ATTN[0], 1, 2), (FINISH, SHRINK[1]), (BACK, 0), (SETTLE, EXPAND[2]),
+    (FINISH, SHRINK[2]), (BACK, 1), (HOP, EXPAND[1], 3), (BACK, 2), (TURN, ATTN[1]),
+    (LINE, ATTN[0], 2, 0), (FINISH, EXPAND[1]), (NORM,), (TURN, ATTN[2]), (START, SKIP[0]),
+    (SETTLE, PROJ), (START, SKIP[1]), (LINE, ATTN[0], 2, 1), (LINE, ATTN[0], 3, 0), (SETTLE, ATTN[1]),
+    (VECTOR, 0), (OUT, 0), (SETTLE, ATTN[2]), (VECTOR, 1), (OUT, 1), (OUT, 2), (TURN, SKIP[0]),
+    (HOP, EXPAND[2], 2), (LINE_END, ATTN[0]), (HOP, EXPAND[2], 3), (TURN, SKIP[1]), (HOP, PROJ, 2),
+    (VECTOR, 2), (FINISH, EXPAND[2]), (HOP, ATTN[1], 2), (HOP, PROJ, 3), (HOP, ATTN[1], 3),
+    (HOP, ATTN[2], 2), (HOP, ATTN[2], 3), (SETTLE, SKIP[0]), (HOP, SKIP[0], 2), (SETTLE, SKIP[1]),
+    (VECTOR, 3), (FINISH, PROJ), (LINE_X, ATTN[0]), (FINISH, ATTN[1]), (FINISH, ATTN[2]),
+    (HOP, SKIP[0], 3), (HOP, SKIP[1], 2), (HOP, SKIP[1], 3), (LINE_Y, ATTN[0]), (FINISH, SKIP[0]),
+    (VECTOR, 4), (FINISH, SKIP[1]), (VECTOR, 5),
 )
 
 
@@ -772,7 +793,7 @@
         swap("left", unit.left, unit.left_at)
         swap("right", unit.right, unit.right_at)
 
-    order = [step.split()[1] for step in PLAN if step.startswith("start ")]
+    order = [rest[0] for kind, *rest in PLAN if kind == START]
     for name in order:
         unit = units[name]
         swap("left", unit.left, unit.left_at)
@@ -890,15 +911,18 @@
             return carry
 
         lax.fori_loop(0, 2, body, 0)
-        tile = product(2)
+        tile = product(2).astype(low)
+        lane = lanes_of((THIRD, LANES))
         for first, order, y_at, place, _ in unit.blocks:
             for x_at in range(2):
                 pieces = [
-                    tile[first + s * THIRD : first + (s + 1) * THIRD, x_at * LANES :][:, :32]
+                    tile[first + s * THIRD : first + (s + 1) * THIRD, x_at * LANES :][:, :LANES]
                     for s in range(3)
                 ]
-                packed = jnp.concatenate(pieces + [jnp.zeros_like(pieces[0])], axis=1)
-                part[slot, order, x_at, y_at, place, pl.ds(2 * ROWS, THIRD)] = packed.astype(low)
+                packed = jnp.where(
+                    lane < 32, pieces[0], jnp.where(lane < 64, pieces[1], pieces[2])
+                )
+                part[slot, order, x_at, y_at, place, pl.ds(2 * ROWS, THIRD)] = packed
 
     def wait_sends(u):
         for order in range(2):
@@ -910,7 +934,7 @@
             load(*key)
             for copy in loads.pop(key, ()):
                 copy.wait()
-        if ahead is not None and not ahead.startswith("skip"):
+        if ahead is not None and ahead not in SKIP:
             for key, busy in zip(keys_of(ahead), keys_of(name)):
                 if key in swaps:
                     load(*key, busy)
@@ -1001,7 +1025,8 @@
         if unit.tiles:
             for t in range(unit.tiles):
                 col = (unit.out_at + t) * LANES
-                out[:, col : col + LANES] = value[t * ROWS : (t + 1) * ROWS]
+                width = min(LANES, out.shape[1] - col)
+                out[:, col : col + width] = value[t * ROWS : (t + 1) * ROWS, :width]
             return
         base = {"shrink": (2 * order + place) * ROWS, "proj": 0, "skip": place * ROWS}[unit.out]
         for i in range(2):
@@ -1012,8 +1037,7 @@
             ]
 
     def line_ref(name, order, place):
-        i = LINE_FIRST.index(name)
-        return r["line"].at[i, order, both, both, place, pl.ds(0, units[name].rows)]
+        return r["line"].at[0, order, both, both, place, pl.ds(0, units[name].rows)]
 
     def line_copy(name, order, place, up):
         i = r["line_at"][name, order, place, up]
@@ -1039,6 +1063,18 @@
                         copy.wait_recv()
                         add_into(line_ref(name, order, place), land)
                     copy.start()
+
+    def line_credit(act):
+        for some, side, here, there in ((z < 3, "above", 8, 9), (z > 0, "below", 9, 8)):
+
+            @pl.when(some)
+            def _():
+                if act is pl.semaphore_wait:
+                    pl.semaphore_wait(r["credit"].at[here], 1)
+                else:
+                    pl.semaphore_signal(
+                        r["credit"].at[there], 1, device_id=at[side], device_id_type=MESH
+                    )
 
     def line_copies(name):
         i = LINE_FIRST.index(name)
@@ -1072,6 +1108,8 @@
                             r["line_own"][i, x_at, y_at, height] = value.astype(low)
 
             line_copies(name)[0].start()
+            if i + 1 < len(LINE_FIRST):
+                line_credit(pl.semaphore_signal)
         elif stage == "x":
             line_copies(name)[0].wait_recv()
             add_into(r["line_own"].at[i, x, both, height], r["line_x"].at[i, both, height])
@@ -1091,9 +1129,6 @@
                     def _():
                         line_copy(name, order, place, up)[0].wait_send()
 
-        for copy in line_copies(name):
-            copy.wait_send()
-
     def head_load(h):
         return pltpu.make_async_copy(
             r["wins"].at[:, h], r["head"].at[h % 2], r["head_sem"].at[h % 2]
@@ -1124,7 +1159,7 @@
         own.wait()
         pl.when(seq > 0)(halo_up.wait_recv)
         pl.when(seq < 7)(halo_down.wait_recv)
-        r["stats"][...] = window[:, features:].astype(jnp.float32)
+        r["stats"][...] = window[:, features:]
 
     def heads_work(count):
         first = done["heads"]
@@ -1140,24 +1175,20 @@
             tile = (h * HEAD_DIM) // LANES
             off = h * HEAD_DIM - tile * LANES
             cols = pl.ds(pl.multiple_of(tile * LANES, LANES), 2 * LANES)
-            pair = pltpu.roll(window[:, cols].astype(jnp.float32), (2 * LANES - off) % (2 * LANES), 1)
-            lane = lanes_of((3 * rows, LANES))
-            r["grad_head"][...] = jnp.where(lane < HEAD_DIM, pair[:, :LANES], 0.0).astype(low)
+            pair = pltpu.roll(window[:, cols], (2 * LANES - off) % (2 * LANES), 1)[:, :LANES]
+            r["grad_head"][...] = jnp.where(
+                lanes_of((3 * rows, LANES)) < HEAD_DIM, pair, jnp.zeros_like(pair)
+            )
+            head = r["head"].at[h % 2]
+            found = back_head(
+                h, head.at[0], head.at[1], head.at[2], r["grad_head"], r["stats"][...],
+                r["own_hide"], r["rim_hide"], r["probs"], r["scored"],
+            )
             wide = lanes_of((rows, 2 * LANES))
             inside = (wide >= off) & (wide < off + HEAD_DIM)
-
-            def store(part, at_row, count, value):
-                rows_at = pl.ds(at_row, count)
-                old = r["triple"][part, rows_at, cols].astype(jnp.float32)
-                spread = jnp.concatenate([value, jnp.zeros_like(value)], axis=1)
-                moved = pltpu.roll(spread, off, 1)
-                r["triple"][part, rows_at, cols] = jnp.where(inside[:count], moved, old).astype(low)
-
-            head = r["head"].at[h % 2]
-            back_head(
-                h, head.at[0], head.at[1], head.at[2], r["grad_head"], r["stats"], r["own_hide"],
-                r["rim_hide"], r["probs"], r["scored"], store,
-            )
+            for part, value in enumerate(found):
+                moved = pltpu.roll(jnp.concatenate([value, jnp.zeros_like(value)], axis=1), off, 1)
+                r["triple"][part, :, cols] = jnp.where(inside, moved, r["triple"][part, :, cols])
             return carry
 
         lax.fori_loop(first, first + count, body, 0)
@@ -1217,7 +1248,7 @@
                 r["normed_grad"][:, cols] += part
 
     def norm_work():
-        gain = r["gain"][...].astype(jnp.float32)
+        gain = vector(r["gain"])
         sums[0:3] = jnp.zeros((3, features), jnp.float32)
         chunk = r["chunk"]
         for i in range(rows // LANES):
@@ -1288,7 +1319,11 @@
         i = order.index(name)
         fetch(name, order[i + 1] if i + 1 < len(order) else None)
         if name in LINE_FIRST:
-            compute(name, r["line"], LINE_FIRST.index(name))
+            i = LINE_FIRST.index(name)
+            if i > 0:
+                line_drain(LINE_FIRST[i - 1])
+                line_credit(pl.semaphore_wait)
+            compute(name, r["line"], 0)
         else:
             first_stage(started.index(name))
 
@@ -1297,30 +1332,32 @@
         hop(started.index(name), 1)
 
     steps = {
-        "start": start,
-        "second": lambda name: second_stage(started.index(name)),
-        "third": third,
-        "hop": lambda name, step: hop(started.index(name), int(step)),
-        "finish": lambda name: finish(started.index(name)),
-        "line": lambda name, step, turn: line_hop(name, int(step), int(turn)),
-        "line_end": lambda name: line_stage(name, "end"),
-        "line_x": lambda name: line_stage(name, "x"),
-        "line_y": lambda name: line_stage(name, "y"),
-        "halo": halo_work,
-        "heads": lambda count: heads_work(int(count)),
-        "pack": pack_work,
-        "back": lambda p: back_work(int(p)),
-        "norm": norm_work,
-        "out": lambda k: out_work(int(k)),
-        "vec": lambda step: vec_work(int(step)),
+        START: start,
+        TURN: lambda name: second_stage(started.index(name)),
+        SETTLE: third,
+        HOP: lambda name, step: hop(started.index(name), step),
+        FINISH: lambda name: finish(started.index(name)),
+        LINE: line_hop,
+        LINE_END: lambda name: line_stage(name, "end"),
+        LINE_X: lambda name: line_stage(name, "x"),
+        LINE_Y: lambda name: line_stage(name, "y"),
+        HALO: halo_work,
+        HEAD: heads_work,
+        PACK: pack_work,
+        BACK: back_work,
+        NORM: norm_work,
+        OUT: out_work,
+        VECTOR: vec_work,
     }
-    for step in PLAN:
-        kind, *rest = step.split()
+    for kind, *rest in PLAN:
         steps[kind](*rest)
     for copy in out_copies():
         copy.wait()
+    for name in LINE_FIRST[-1:]:
+        line_drain(name)
     for name in LINE_FIRST:
-        line_drain(name)
+        for copy in line_copies(name):
+            copy.wait_send()
     for copy in swaps.values():
         copy.wait_send()
     count = len(started)
@@ -1397,7 +1434,7 @@
     add("came", pltpu.SemaphoreType.DMA((256,)))
     span = 3 * rows
     add("window", pltpu.VMEM((span, features + LANES), low))
-    add("stats", pltpu.VMEM((span, LANES), full))
+    add("stats", pltpu.VMEM((span, LANES), low))
     add("head", pltpu.VMEM((2, 3, span, LANES), low))
     add("head_sem", pltpu.SemaphoreType.DMA((2,)))
     add("grad_head", pltpu.VMEM((span, LANES), low))
@@ -1410,16 +1447,18 @@
     add("normed_grad", pltpu.VMEM((rows, features), full))
     add("chunk", pltpu.VMEM((2, LANES, features), full))
     add("chunk_sem", pltpu.SemaphoreType.DMA((2,)))
-    add("credit", pltpu.SemaphoreType.REGULAR((8,)))
+    add("credit", pltpu.SemaphoreType.REGULAR((10,)))
     lines = len(LINE_FIRST)
     line_at = {}
     for name in LINE_FIRST:
         for (order, place), z_at in make_units()[name].z_of.items():
             for up, have in ((True, z_at > 0), (False, z_at < 3)):
                 if have:
-                    line_at[name, order, place, up] = len(line_at)
-    add("line", pltpu.VMEM((lines, 2, 2, 2, 2, most, LANES), low))
-    add("line_land", pltpu.VMEM((len(line_at), 2, 2, most, LANES), low))
+                    line_at[name, order, place, up] = len(
+                        [key for key in line_at if key[0] == name]
+                    )
+    add("line", pltpu.VMEM((1, 2, 2, 2, 2, most, LANES), low))
+    add("line_land", pltpu.VMEM((6, 2, 2, most, LANES), low))
     add("line_own", pltpu.VMEM((lines, 2, 2, most, LANES), low))
     add("line_x", pltpu.VMEM((lines, 2, most, LANES), low))
     add("line_y", pltpu.VMEM((lines, most, LANES), low))
@@ -1442,6 +1481,44 @@
         name="gradients",
     )(*operands)
     return dict(zip([name for name, _ in GRADS] + ["vec", "tok", "skp"], found))
+
+
+VECTORS = ((0, 1), (1, 1), (2, 1), (3, 2), (5, 1), (6, 1), (7, 1), (9, 4), (8, 1))
+
+
+def results_kernel(*refs):
+    count = len(GRADS) + 2
+    total, sources, targets = refs[0], refs[1 : 1 + count], refs[1 + count :]
+    for source, target in zip(sources, targets):
+        target[...] = source[...].T if source.shape != target.shape else source[...]
+    features = total.shape[1]
+    place = lax.axis_index("seq") * lax.axis_size("batch") + lax.axis_index("batch")
+    for (first, rows), target in zip(VECTORS, targets[count:]):
+        width = target.shape[0]
+        row = place * width // features
+        off = place * width - row * features
+        line = jnp.broadcast_to(total[pl.ds(first + row, 1)], (8, features))
+        target[...] = pltpu.roll(line, (features - off) % features, 1)[0, :width]
+
+
+def results(found):
+    values = [found[name] for name in [*(name for name, _ in GRADS), "tok", "skp"]]
+    devices = lax.axis_size("seq") * lax.axis_size("batch")
+    features = found["vec"].shape[1]
+    shapes = [values[0].shape[::-1], *(value.shape for value in values[1:])]
+    out = [jax.ShapeDtypeStruct(shape, value.dtype) for shape, value in zip(shapes, values)]
+    out += [
+        jax.ShapeDtypeStruct((rows * features // devices,), jnp.float32) for _, rows in VECTORS
+    ]
+    got = pl.pallas_call(
+        results_kernel,
+        out_shape=out,
+        in_specs=[whole()] * (1 + len(values)),
+        out_specs=[whole()] * len(out),
+        compiler_params=params(),
+        name="results",
+    )(found["vec"], *values)
+    return (got[0].T, *got[1 : len(values)]), got[len(values) :]
 
 
 def unsplit(value):
@@ -1527,7 +1604,7 @@
     wins, mixed, lse = attend(own, before, after, attn_weight, attn_bias, id_col, id_row)
     (
         result, active, hidden_by_core, second, branch, branch_by_core, up_by_core, middle_grad,
-        mixed_grad, hidden_sum, sums,
+        mixed_grad, sums,
     ) = layer(
         stream, mixed, lse, above,
         (
@@ -1536,46 +1613,23 @@
         ),
     )
     if lax.axis_size("seq") == 8 and lax.axis_size("batch") == 4:
-        vec = jnp.concatenate(
-            [
-                jnp.zeros((5, features), jnp.float32),
-                sums[:4],
-                hidden_sum.reshape(-1, features),
-                jnp.zeros((3, features), jnp.float32),
-            ],
-            axis=0,
-        )
         found = gradients(
             dict(
                 active=active, second=second, mixed=mixed, normed=normed, tok=tok, skp=skp,
                 upstream=up_by_core, hidden=hidden_by_core, branch=branch_by_core, wins=wins,
                 grads=mixed_grad, id_col=id_col, id_row=id_row, stream=stream,
-                middle_grad=middle_grad, gain=first_gain[None], attn_weight=attn_weight,
+                middle_grad=middle_grad, gain=first_gain, attn_weight=attn_weight,
                 skip_weight=skip_weight,
             ),
-            vec,
+            sums,
         )
-        tok_grad, skip_grad = found["tok"], found["skp"]
-        weight_parts = (
-            found["skip"], found["attn"][:, :864], found["proj"], found["expand"], found["shrink"]
-        )
-        total = found["vec"]
-        place = position * lax.axis_size("batch") + lax.axis_index("batch")
-
-        def mine(first, count):
-            part = total[first : first + count].reshape(-1)
-            width = part.shape[0] // 32
-            return lax.dynamic_slice_in_dim(part, place * width, width, 0)
-
-        vectors = (
-            mine(0, 1), mine(1, 1), mine(2, 1), mine(3, 2), mine(5, 1), mine(6, 1), mine(7, 1),
-            mine(9, 4), mine(8, 1),
-        )
+        (shrink, expand, proj, attn, skip, tok_grad, skip_grad), vectors = results(found)
+        weight_parts = (skip, attn, proj, expand, shrink)
     else:
         before, after = rims(mixed_grad, rim)
         blank = jnp.zeros((rows - rim, mixed_grad.shape[1]), mixed_grad.dtype)
         grad_window = jnp.concatenate([blank, before, mixed_grad, after, blank], axis=0)
-        stats = grad_window[:, features:].astype(jnp.float32)
+        stats = grad_window[:, features:]
         triple, triple_sum = attend_back(wins, grad_window, stats, id_col, id_row)
         tok_grad, skip_grad, stream_by_core, stream_sums = stream_back(
             triple, attn_weight, stream, middle_grad, first_gain, skip_weight
@@ -1585,11 +1639,11 @@
             stream_sums[0],
             stream_sums[1],
             jnp.concatenate([triple_sum[0, :features], triple_sum[0, 2 * features :]]),
-            sums[0],
-            sums[1],
-            sums[2],
-            hidden_sum[0],
-            sums[3],
+            sums[5],
+            sums[6],
+            sums[7],
+            sums[9:13].reshape(-1),
+            sums[8],
         )
         joined = jnp.concatenate([tok, skp], axis=1)
         weight_parts, vectors = summed(

time: 345 us -> 313 us (0.907)
  local copies, waits for them, and re-layouts: 28.3 us -> 4.08 us
  Pallas kernels: 285 us -> 277 us
  waiting for transfers between devices: 16.2 us -> 20.2 us
    pallas_call x1, Pallas kernels: 34.3 us -> 23.6 us  [attend(): pl.pallas_call(attend_kernel, out_shape=(jax.ShapeDtypeStruct((3, HEADS,...]
    unnamed x35 -> x6, local copies, waits for them, and re-layouts: 10.4 us -> 0.88 us
    broadcast_in_dim x11 -> x0, local copies, waits for them, and re-layouts: 7.45 us -> none  [the longest x1 1.28 us: stream_norm(): bias[None]]
    pallas_call x0 -> x1, Pallas kernels: none -> 4.71 us  [results(): pl.pallas_call(results_kernel, out_shape=out, in_specs=[whole()] * (1 + l...]
    dynamic_slice x6 -> x0, local copies, waits for them, and re-layouts: 3.56 us -> none  [mine(): return lax.dynamic_slice_in_dim(part, place * width, width, 0)]
    slice x4 -> x0, local copies, waits for them, and re-layouts: 3.55 us -> none  [the longest x3 2.77 us: mine(): part = total[first:first + count].reshape(-1)]
  transfers between devices with their start and end apart: 2 -> 2, of which waited for: 1 -> 2; matrix products, arithmetic and copies ran while one was open for 2% -> 1% of each run, Pallas kernels for 3% -> 3%
where the time goes in v3:
time: 313 us; the launch traced here: 309 us
  Pallas kernels  277 us (88%)
  waiting for transfers between devices  20.2 us (6%)
  starting transfers between devices  7.01 us (2%)
  local copies, waits for them, and re-layouts  4.08 us (1%)
    pallas_call x1, Pallas kernels, gradients(): pl.pallas_call(kernel, out_shape=out_shape, in_specs=in_specs, out_specs=...  192 us
    pallas_call x1, Pallas kernels, layer(): pl.pallas_call(layer_kernel, grid=(4,), in_specs=[held(narrow), held(narr...  39 us
    pallas_call x1, Pallas kernels, attend(): pl.pallas_call(attend_kernel, out_shape=(jax.ShapeDtypeStruct((3, HEADS,...  23.6 us
    ppermute x1, waiting for transfers between devices, rims(): lax.ppermute(value[-width:], 'seq', up)  16.7 us
    pallas_call x1, Pallas kernels, own_heads(): pl.pallas_call(project_kernel, out_shape=jax.ShapeDtypeStruct((3, HEADS,...  9.97 us
    pallas_call x1, Pallas kernels, stream_norm(): pl.pallas_call(stream_kernel, out_shape=(jax.ShapeDtypeStruct((rows, feat...  7.96 us
  transfers between devices with their start and end apart: 2, of which 2 were waited for; matrix products, arithmetic and copies ran while one was open for 1% of the time, Pallas kernels for 3%

profile of v3, /device:TPU:0, one launch (start us, length us, event | category | flops | bytes accessed | tf_op | source)
XLA Modules:
  0.0 309.4 jit_solution(15907775905898379637)
XLA Ops:
  0.7 0.0 copy-start.2
  0.7 8.0 %stream_norm.1 = (f32[384,1152]{1,0:T(8,128)}, bf16[384,1152]{1,0:T(8,128)(2,1)}) custom-call(bf16[384,1152]{1,0:T(8,128)(2,1)} %bitcast.9, bf16[384,1152]{1,0:T(8,128)(2,1)} %bitcast.11, bf16[2304,1152]{1,0:T(8,128)(2,1)} %refs_17_.1, bf16[1152]{0:T(1024)(128)(2,1)} %bias.3, bf16[1152]{0:T(1024)(128)(2,1)} %refs_15_.1, bf16[1152]{0:T(1024)(128)(2,1)} %shift.2), custom_call_target="tpu_custom_call" | custom-call | flops 2038431744 | bytes 10000000 | tf_op jit(solution)/shard_map/stream_norm/pallas_call | solution.py:105
  8.6 1.5 fusion
  10.1 1.3 collective-permute-start.1
  11.4 5.7 %collective-permute-start = (bf16[336,1152]{1,0:T(8,128)(2,1)S(1)}, bf16[336,1152]{1,0:T(8,128)(2,1)S(1)}, u32[]{:S(2)}, u32[]{:S(2)}) collective-permute-start(bf16[336,1152]{1,0:T(8,128)(2,1)S(1)} %get-tuple-element.94), channel_id=1, source_target_pairs={{0,4},{4,8},{8,12},{12,16},{16,20},{20,24},{24,28},{1,5},{5,9},{9,... | collective-permute-start | bytes 2322440 | tf_op jit(solution)/shard_map/ppermute | solution.py:1568
  17.2 0.0 copy-done.2
  17.2 0.1 pad_dynamic-slice_fusion
  17.2 0.6 broadcast_in_dim.16.id_row.refs_12_
  17.8 1.0 broadcast_in_dim.20.id_col.refs_11_
  18.9 10.0 %own_heads.1.own = bf16[3,16,384,128]{3,2,1,0:T(8,128)(2,1)} custom-call(bf16[384,1152]{1,0:T(8,128)(2,1)} %get-tuple-element.56.normed.refs_3_, bf16[1152,3456]{1,0:T(8,128)(2,1)} %refs_16_.1, bf16[2304]{0:T(1024)(128)(2,1)} %bias.5), custom_call_target="tpu_custom_call" | custom-call | flops 3057647616 | bytes 20000000 | tf_op jit(solution)/shard_map/own_heads/pallas_call | solution.py:173
  28.9 3.4 %collective-permute-done.1.after = bf16[336,1152]{1,0:T(8,128)(2,1)S(1)} collective-permute-done((bf16[336,1152]{1,0:T(8,128)(2,1)S(1)}, bf16[336,1152]{1,0:T(8,128)(2,1)S(1)}, u32[]{:S(2)}, u32[]{:S(2)}) %collective-permute-start.1) | collective-permute-done | bytes 774176 | tf_op jit(solution)/shard_map/ppermute | solution.py:1569
  32.3 0.0 copy-start
  32.3 16.7 %collective-permute-done.before = bf16[336,1152]{1,0:T(8,128)(2,1)S(1)} collective-permute-done((bf16[336,1152]{1,0:T(8,128)(2,1)S(1)}, bf16[336,1152]{1,0:T(8,128)(2,1)S(1)}, u32[]{:S(2)}, u32[]{:S(2)}) %collective-permute-start) | collective-permute-done | bytes 774176 | tf_op jit(solution)/shard_map/ppermute | solution.py:1568
  49.0 0.0 copy-done
  49.0 0.0 copy-start.1
  49.0 0.9 copy-done.1
  49.9 23.6 %attend.1 = (bf16[3,16,1152,128]{3,2,1,0:T(8,128)(2,1)}, bf16[384,1152]{1,0:T(8,128)(2,1)}, f32[384,128]{1,0:T(8,128)}) custom-call(bf16[3,16,384,128]{3,2,1,0:T(8,128)(2,1)} %own_heads.1.own, bf16[336,1152]{1,0:T(8,128)(2,1)} %copy-done.1, bf16[336,1152]{1,0:T(8,128)(2,1)} %copy-done, bf16[1152,3456]{1,0:T(8,128)(2,1)} %refs_16_.1, bf16[2304]{0:T(1024)(128)(2,1)} %bias.5, ...), custom_call_target="tpu_custom_call" | custom-call | tf_op jit(solution)/shard_map/attend/pallas_call | solution.py:270
  73.4 39.0 %layer.1 = (bf16[384,1152]{1,0:T(8,128)(2,1)}, bf16[384,4608]{1,0:T(8,128)(2,1)}, bf16[2,3,384,768]{3,2,1,0:T(8,128)(2,1)}, bf16[384,1152]{1,0:T(8,128)(2,1)}, b...) custom-call(f32[384,1152]{1,0:T(8,128)} %get-tuple-element.55.stream, ...), custom_call_target="tpu_custom_call" | custom-call | tf_op jit(solution)/shard_map/layer/pallas_call | solution.py:395
  112.5 191.7 %gradients.1 = (f32[576,288]{1,0:T(8,128)}, f32[144,1152]{1,0:T(8,128)}, f32[144,288]{1,0:T(8,128)}, f32[144,864]{1,0:T(8,128)}, f32[288,288]{1,0:T(8,128)}, /*i...) custom-call(bf16[384,4608]{1,0:T(8,128)(2,1)} %get-tuple-element.60., ...), custom_call_target="tpu_custom_call" | custom-call | tf_op jit(solution)/shard_map/gradients/pallas_call | solution.py:1472
  304.2 4.7 %results.1 = (f32[288,576]{1,0:T(8,128)}, f32[144,1152]{1,0:T(8,128)}, f32[144,288]{1,0:T(8,128)}, f32[144,864]{1,0:T(8,128)}, f32[288,288]{1,0:T(8,128)}, /*ind...) custom-call(f32[16,1152]{1,0:T(8,128)} %get-tuple-element.69.refs_0_, ...), custom_call_target="tpu_custom_call" | custom-call | tf_op jit(solution)/shard_map/results/pallas_call | solution.py:1513
Async XLA Ops:
  0.7 16.5 %copy-start.2 = (s32[1,3072]{1,0:T(1,128)S(1)}, s32[1,3072]{1,0:T(1,128)}, u32[]{:S(2)}) copy-start(s32[1,3072]{1,0:T(1,128)} %param.20) | copy-start | bytes 36868
  10.1 22.1 %collective-permute-start.1 = (bf16[336,1152]{1,0:T(8,128)(2,1)S(1)}, bf16[336,1152]{1,0:T(8,128)(2,1)S(1)}, u32[]{:S(2)}, u32[]{:S(2)}) collective-permute-start(bf16[336,1152]{1,0:T(8,128)(2,1)S(1)} %get-tuple-element.93), channel_id=1, source_target_pairs={{4,0},{8,4},{12,8},{16,12},{20,16},{24,20},{28,24},{5,1},{9,5},{13... | collective-permute-start | bytes 2322440 | tf_op jit(solution)/shard_map/ppermute | solution.py:1569
  11.4 37.6 %collective-permute-start = (bf16[336,1152]{1,0:T(8,128)(2,1)S(1)}, bf16[336,1152]{1,0:T(8,128)(2,1)S(1)}, u32[]{:S(2)}, u32[]{:S(2)}) collective-permute-start(bf16[336,1152]{1,0:T(8,128)(2,1)S(1)} %get-tuple-element.94), channel_id=1, source_target_pairs={{0,4},{4,8},{8,12},{12,16},{16,20},{20,24},{24,28},{1,5},{5,9},{9,... | collective-permute-start | bytes 2322440 | tf_op jit(solution)/shard_map/ppermute | solution.py:1568
  32.3 16.7 %copy-start = (bf16[336,1152]{1,0:T(8,128)(2,1)}, bf16[336,1152]{1,0:T(8,128)(2,1)S(1)}, u32[]{:S(2)}) copy-start(bf16[336,1152]{1,0:T(8,128)(2,1)S(1)} %collective-permute-done.1.after) | copy-start | bytes 2322436
  49.0 0.9 copy-start.1
